TPU v7x, 32 devices: a whole 2x2x4 slice. The times are simulated.
32 devices in a mesh: rep: 16 (over z, y, core), fsdp: 2 (over x).
Axes of the slice: x: 2, y: 2, z: 4, core: 2. Of those that a mesh axis runs over, the one named last changes fastest.
Arguments:
- frames: float32 [32, 1024, 1280], P('rep', 'fsdp'), may hold values from -6 to 6
- cotangent: float32 [32, 1024, 1280], P('rep', 'fsdp'), may hold values from -6 to 6
- clip_lengths: int32 [32], replicated, may hold values from 256 to 1024, as said below
- clip_slots: int32 [32], P('rep'), may hold values from 0 to 31, as said below
- gain_attn: bfloat16 [1280], P('fsdp'), may hold values from 0.25 to 1.75
- shift_attn: bfloat16 [1280], P('fsdp'), may hold values from -1.75 to 1.75
- w_qkv: bfloat16 [1280, 3840], P('fsdp'), may hold values from -0.25 to 0.25
- bias_query: bfloat16 [1280], P('fsdp'), may hold values from -3 to 3
- bias_value: bfloat16 [1280], P('fsdp'), may hold values from -3 to 3
- w_out: bfloat16 [1280, 1280], P('fsdp'), may hold values from -1 to 1
- bias_out: bfloat16 [1280], P('fsdp'), may hold values from -1.75 to 1.75
- gain_ffn: bfloat16 [1280], P('fsdp'), may hold values from 0.25 to 1.75
- shift_ffn: bfloat16 [1280], P('fsdp'), may hold values from -1.75 to 1.75
- w_up: bfloat16 [1280, 5120], P('fsdp'), may hold values from -0.15625 to 0.15625
- bias_up: bfloat16 [5120], P('fsdp'), may hold values from -3 to 3
- w_down: bfloat16 [5120, 1280], P('fsdp'), may hold values from -0.078125 to 0.078125
- bias_down: bfloat16 [1280], P('fsdp'), may hold values from -1.75 to 1.75
Outputs:
- output: float32 [32, 1024, 1280], P('rep', 'fsdp')
- frames_grad: float32 [32, 1024, 1280], P('rep', 'fsdp')
- gain_attn_grad: float32 [1280], P('fsdp')
- shift_attn_grad: float32 [1280], P('fsdp')
- w_qkv_grad: float32 [1280, 3840], P('fsdp')
- bias_query_grad: float32 [1280], P('fsdp')
- bias_value_grad: float32 [1280], P('fsdp')
- w_out_grad: float32 [1280, 1280], P('fsdp')
- bias_out_grad: float32 [1280], P('fsdp')
- gain_ffn_grad: float32 [1280], P('fsdp')
- shift_ffn_grad: float32 [1280], P('fsdp')
- w_up_grad: float32 [1280, 5120], P('fsdp')
- bias_up_grad: float32 [5120], P('fsdp')
- w_down_grad: float32 [5120, 1280], P('fsdp')
- bias_down_grad: float32 [1280], P('fsdp')
Inputs may be any that keep to these rules, and one draw needn't show every extreme that they name: `clip_lengths`: every clip numbered below 16 is longer than 512 frames; clip 0 has 1024 frames and clip 16 has 256. `clip_slots`: A permutation of the clip numbers; the 2 slots of each group hold exactly one clip numbered below 16.
All inputs are finite; a program needn't handle non-finite values.
Results may differ from a plain program's by a relative error of at most 0.012.
The roundings to bfloat16 on the way count: a program that leaves them out, or rounds other values in their place, can miss the bound.
Values may be sent and summed in bfloat16 or wider, within the bound.
No kernel may reach another device: no remote copies, remote signals or barrier semaphores. Data moves between devices by JAX's collectives and lax.ppermute only.
A program may use at most 512 MiB of HBM per device.

v0:
```python
import jax
import jax.numpy as jnp
from jax import lax
from jax.sharding import PartitionSpec as P

HEADS = 16


def layer_norm(rows, gain, shift):
    mean = jnp.mean(rows, axis=-1, keepdims=True)
    centred = rows - mean
    spread = jnp.mean(centred * centred, axis=-1, keepdims=True)
    return centred * lax.rsqrt(spread + 1e-05) * gain + shift


def exact_gelu(values):
    return jax.nn.gelu(values, approximate=False)


def product(left, right):
    return jnp.dot(left, right, preferred_element_type=jnp.float32)


def product_left(left, right):
    return lax.dot_general(
        left, right, (((0,), (0,)), ((), ())), preferred_element_type=jnp.float32
    )


def product_right(left, right):
    return lax.dot_general(
        left, right, (((1,), (1,)), ((), ())), preferred_element_type=jnp.float32
    )


def head_blocks(query, keys, values, block):
    rows, width = query.shape
    half = width // 2
    per = HEADS // 2
    size = width // HEADS
    lower = block * half
    query_part = query[:, lower : lower + half].reshape(rows, per, size)
    key_part = keys[:, lower : lower + half].reshape(keys.shape[0], per, size)
    value_part = values[:, lower : lower + half].reshape(values.shape[0], per, size)
    return (query_part, key_part, value_part)


def masked_scores(query_part, key_part, valid, scale):
    scores = (
        jnp.einsum("qhd,khd->hqk", query_part, key_part, preferred_element_type=jnp.float32) * scale
    )
    return jnp.where(valid[None, None, :], scores, -1e30)


def attend(query, keys, values, valid):
    rows, width = query.shape
    scale = (width // HEADS) ** (-0.5)
    pieces = []
    totals = []
    for block in range(2):
        query_part, key_part, value_part = head_blocks(query, keys, values, block)
        scores = masked_scores(query_part, key_part, valid, scale)
        peak = jnp.max(scores, axis=-1, keepdims=True)
        raised = jnp.exp(scores - peak)
        summed = jnp.sum(raised, axis=-1, keepdims=True)
        probs = (raised / summed).astype(jnp.bfloat16)
        mixed = jnp.einsum("hqk,khd->qhd", probs, value_part, preferred_element_type=jnp.float32)
        pieces.append(mixed.reshape(rows, width // 2))
        totals.append(peak + jnp.log(summed))
    return (jnp.concatenate(pieces, axis=1), totals)


def attend_back(query, keys, values, valid, totals, d_mixed):
    rows, width = query.shape
    scale = (width // HEADS) ** (-0.5)
    query_grads = []
    key_grads = []
    value_grads = []
    for block in range(2):
        query_part, key_part, value_part = head_blocks(query, keys, values, block)
        upper = d_mixed[:, block * (width // 2) : (block + 1) * (width // 2)].reshape(
            query_part.shape
        )
        scores = masked_scores(query_part, key_part, valid, scale)
        probs = jnp.exp(scores - totals[block])
        d_probs = jnp.einsum("qhd,khd->hqk", upper, value_part, preferred_element_type=jnp.float32)
        centre = jnp.sum(probs * d_probs, axis=-1, keepdims=True)
        d_scores = (probs * (d_probs - centre)).astype(jnp.bfloat16)
        d_query = (
            jnp.einsum("hqk,khd->qhd", d_scores, key_part, preferred_element_type=jnp.float32)
            * scale
        )
        d_key = (
            jnp.einsum("hqk,qhd->khd", d_scores, query_part, preferred_element_type=jnp.float32)
            * scale
        )
        d_value = jnp.einsum(
            "hqk,qhd->khd", probs.astype(jnp.bfloat16), upper, preferred_element_type=jnp.float32
        )
        query_grads.append(d_query.reshape(rows, width // 2))
        key_grads.append(d_key.reshape(keys.shape[0], width // 2))
        value_grads.append(d_value.reshape(keys.shape[0], width // 2))
    return (
        jnp.concatenate(query_grads, axis=1),
        jnp.concatenate(key_grads, axis=1),
        jnp.concatenate(value_grads, axis=1),
    )


def add_tuples(first, second):
    if first is None:
        return second
    return tuple((left + right for left, right in zip(first, second)))


def weight_grads(pieces, smalls):
    norm_a, d_qkv, attn_in, d_attn, norm_f, d_up, hidden, d_out = pieces
    gain_one, shift_one, gain_two, shift_two = smalls
    width = norm_a.shape[1]
    grad_qkv = product_left(norm_a, d_qkv)
    columns = jnp.sum(d_qkv.astype(jnp.float32), axis=0)
    grad_query_bias = columns[:width]
    grad_value_bias = columns[2 * width :]
    grad_out = product_left(attn_in, d_attn)
    grad_out_bias = jnp.sum(d_attn.astype(jnp.float32), axis=0)
    grad_up = product_left(norm_f, d_up)
    grad_up_bias = jnp.sum(d_up.astype(jnp.float32), axis=0)
    grad_down = product_left(hidden, d_out)
    grad_down_bias = jnp.sum(d_out.astype(jnp.float32), axis=0)
    return (
        gain_one,
        shift_one,
        grad_qkv,
        grad_query_bias,
        grad_value_bias,
        grad_out,
        grad_out_bias,
        gain_two,
        shift_two,
        grad_up,
        grad_up_bias,
        grad_down,
        grad_down_bias,
    )


def on_device(
    frames,
    cotangent,
    clip_lengths,
    clip_slots,
    gain_attn,
    shift_attn,
    w_qkv,
    bias_query,
    bias_value,
    w_out,
    bias_out,
    gain_ffn,
    shift_ffn,
    w_up,
    bias_up,
    w_down,
    bias_down,
):
    shards = (
        gain_attn,
        shift_attn,
        w_qkv,
        bias_query,
        bias_value,
        w_out,
        bias_out,
        gain_ffn,
        shift_ffn,
        w_up,
        bias_up,
        w_down,
        bias_down,
    )
    micro, rows, width = frames.shape
    group_size = lax.axis_size("fsdp")
    length_all = rows * group_size
    positions = jnp.arange(length_all, dtype=jnp.int32)
    numbers = jnp.arange(clip_lengths.shape[0], dtype=jnp.int32)
    outputs = []
    input_grads = []
    summed = None
    kept_pieces = []
    small_sum = None
    for slot in range(micro):
        span = jnp.sum(jnp.where(numbers == clip_slots[slot], clip_lengths, 0))
        valid = positions < span
        whole = (
            lax.all_gather(shards[0], "fsdp", axis=0, tiled=True),
            lax.all_gather(shards[1], "fsdp", axis=0, tiled=True),
            lax.all_gather(shards[2], "fsdp", axis=0, tiled=True),
            lax.all_gather(shards[3], "fsdp", axis=0, tiled=True),
            lax.all_gather(shards[4], "fsdp", axis=0, tiled=True),
            lax.all_gather(shards[5], "fsdp", axis=0, tiled=True),
            lax.all_gather(shards[6], "fsdp", axis=0, tiled=True),
            lax.all_gather(shards[7], "fsdp", axis=0, tiled=True),
            lax.all_gather(shards[8], "fsdp", axis=0, tiled=True),
            lax.all_gather(shards[9], "fsdp", axis=0, tiled=True),
            lax.all_gather(shards[10], "fsdp", axis=0, tiled=True),
            lax.all_gather(shards[11], "fsdp", axis=0, tiled=True),
            lax.all_gather(shards[12], "fsdp", axis=0, tiled=True),
        )
        frame_rows = frames[slot]
        gain_one = whole[0].astype(jnp.float32)
        shift_one = whole[1].astype(jnp.float32)
        norm_a = layer_norm(frame_rows, gain_one, shift_one).astype(jnp.bfloat16)
        qkv = product(norm_a, whole[2])
        query = (qkv[:, :width] + whole[3].astype(jnp.float32)).astype(jnp.bfloat16)
        key = qkv[:, width : 2 * width].astype(jnp.bfloat16)
        value = (qkv[:, 2 * width :] + whole[4].astype(jnp.float32)).astype(jnp.bfloat16)
        keys_all, values_all = (
            lax.all_gather(key, "fsdp", axis=0, tiled=True),
            lax.all_gather(value, "fsdp", axis=0, tiled=True),
        )
        mixed, totals = attend(query, keys_all, values_all, valid)
        attn_in = mixed.astype(jnp.bfloat16)
        resid = frame_rows + product(attn_in, whole[5]) + whole[6].astype(jnp.float32)
        gain_two = whole[7].astype(jnp.float32)
        shift_two = whole[8].astype(jnp.float32)
        norm_f = layer_norm(resid, gain_two, shift_two).astype(jnp.bfloat16)
        upward = product(norm_f, whole[9]) + whole[10].astype(jnp.float32)
        hidden = exact_gelu(upward).astype(jnp.bfloat16)
        outputs.append(resid + product(hidden, whole[11]) + whole[12].astype(jnp.float32))
        whole = (
            lax.all_gather(shards[0], "fsdp", axis=0, tiled=True),
            lax.all_gather(shards[1], "fsdp", axis=0, tiled=True),
            lax.all_gather(shards[2], "fsdp", axis=0, tiled=True),
            lax.all_gather(shards[3], "fsdp", axis=0, tiled=True),
            lax.all_gather(shards[4], "fsdp", axis=0, tiled=True),
            lax.all_gather(shards[5], "fsdp", axis=0, tiled=True),
            lax.all_gather(shards[6], "fsdp", axis=0, tiled=True),
            lax.all_gather(shards[7], "fsdp", axis=0, tiled=True),
            lax.all_gather(shards[8], "fsdp", axis=0, tiled=True),
            lax.all_gather(shards[9], "fsdp", axis=0, tiled=True),
            lax.all_gather(shards[10], "fsdp", axis=0, tiled=True),
            lax.all_gather(shards[11], "fsdp", axis=0, tiled=True),
            lax.all_gather(shards[12], "fsdp", axis=0, tiled=True),
        )
        d_out = cotangent[slot].astype(jnp.bfloat16)
        d_hidden = product_right(d_out, whole[11])
        unused, gelu_back = jax.vjp(exact_gelu, upward)
        d_up = gelu_back(d_hidden)[0].astype(jnp.bfloat16)
        unused, norm_two_back = jax.vjp(layer_norm, resid, gain_two, shift_two)
        d_resid_norm, grad_gain_two, grad_shift_two = norm_two_back(product_right(d_up, whole[9]))
        d_resid = cotangent[slot] + d_resid_norm
        d_attn = d_resid.astype(jnp.bfloat16)
        d_mixed = product_right(d_attn, whole[5]).astype(jnp.bfloat16)
        d_query, key_terms, value_terms = attend_back(
            query, keys_all, values_all, valid, totals, d_mixed
        )
        d_key, d_value = (
            lax.psum_scatter(key_terms, "fsdp", scatter_dimension=0, tiled=True),
            lax.psum_scatter(value_terms, "fsdp", scatter_dimension=0, tiled=True),
        )
        d_query = d_query.astype(jnp.bfloat16)
        d_key = d_key.astype(jnp.bfloat16)
        d_value = d_value.astype(jnp.bfloat16)
        d_qkv = jnp.concatenate([d_query, d_key, d_value], axis=1)
        unused, norm_one_back = jax.vjp(layer_norm, frame_rows, gain_one, shift_one)
        d_frames_norm, grad_gain_one, grad_shift_one = norm_one_back(product_right(d_qkv, whole[2]))
        input_grads.append(d_resid + d_frames_norm)
        pieces = (norm_a, d_qkv, attn_in, d_attn, norm_f, d_up, hidden, d_out)
        smalls = (grad_gain_one, grad_shift_one, grad_gain_two, grad_shift_two)
        kept_pieces.append(pieces)
        small_sum = add_tuples(small_sum, smalls)
    joined = tuple(
        (jnp.concatenate([group[index] for group in kept_pieces], axis=0) for index in range(8))
    )
    owned = lax.psum_scatter(
        weight_grads(joined, small_sum), "fsdp", scatter_dimension=0, tiled=True
    )
    summed = lax.psum(
        (
            owned[0],
            owned[1],
            owned[2],
            owned[3],
            owned[4],
            owned[5],
            owned[6],
            owned[7],
            owned[8],
            owned[9],
            owned[10],
            owned[11],
            owned[12],
        ),
        "rep",
    )
    return (jnp.stack(outputs), jnp.stack(input_grads)) + tuple(summed)


def solution(mesh):
    return jax.shard_map(
        on_device,
        mesh=mesh,
        in_specs=(
            P("rep", "fsdp", None),
            P("rep", "fsdp", None),
            P(),
            P("rep"),
            P("fsdp"),
            P("fsdp"),
            P("fsdp", None),
            P("fsdp"),
            P("fsdp"),
            P("fsdp", None),
            P("fsdp"),
            P("fsdp"),
            P("fsdp"),
            P("fsdp", None),
            P("fsdp"),
            P("fsdp", None),
            P("fsdp"),
        ),
        out_specs=(
            P("rep", "fsdp", None),
            P("rep", "fsdp", None),
            P("fsdp"),
            P("fsdp"),
            P("fsdp", None),
            P("fsdp"),
            P("fsdp"),
            P("fsdp", None),
            P("fsdp"),
            P("fsdp"),
            P("fsdp"),
            P("fsdp", None),
            P("fsdp"),
            P("fsdp", None),
            P("fsdp"),
        ),
        check_vma=False,
    )
```

profile of v0, /device:TPU:0, one launch (start us, length us, event | category | flops | bytes accessed | tf_op | source)
XLA Modules:
  0.0 2675.9 jit_solution(11532650856768018959)
XLA Ops:
  28.1 106.5 %all-gather.18.cloned.1.call-done = bf16[1280,3840]{1,0:T(8,128)(2,1)} async-done(((bf16[640,3840]{1,0:T(8,128)(2,1)}), bf16[1280,3840]{1,0:T(8,128)(2,1)}) %all-gather.18.cloned.1.call-update) | async-done | bytes 9830416 | tf_op jit(solution)/shard_map/all_gather | solution.py:197
  212.9 14.3 all-gather.20.cloned.1.call-done
  233.1 35.1 %all-gather.32.cloned.1.call-done = bf16[1024,1280]{1,0:T(8,128)(2,1)} async-done(((bf16[512,1280]{1,0:T(8,128)(2,1)}), bf16[1024,1280]{1,0:T(8,128)(2,1)}) %all-gather.32.cloned.1.call-update) | async-done | bytes 2621456 | tf_op jit(solution)/shard_map/all_gather | solution.py:218
  339.5 17.6 all-gather.30.cloned.1.call-done
  401.3 115.7 %all-gather.26.cloned.1.call-done = bf16[1280,5120]{1,0:T(8,128)(2,1)} async-done(((bf16[640,5120]{1,0:T(8,128)(2,1)}), bf16[1280,5120]{1,0:T(8,128)(2,1)}) %all-gather.26.cloned.1.call-update) | async-done | bytes 13107216 | tf_op jit(solution)/shard_map/all_gather | solution.py:204
  517.0 15.3 fusion.135
  541.9 135.0 %all-gather.28.cloned.1.call-done = bf16[5120,1280]{1,0:T(8,128)(2,1)} async-done(((bf16[2560,1280]{1,0:T(8,128)(2,1)}), bf16[5120,1280]{1,0:T(8,128)(2,1)}) %all-gather.28.cloned.1.call-update) | async-done | bytes 13107216 | tf_op jit(solution)/shard_map/all_gather | solution.py:206
  676.9 34.9 %add_convert_fusion.1 = (bf16[512,5120]{1,0:T(8,128)(2,1)S(1)}, f32[512,5120]{1,0:T(8,128)}) fusion(f32[512,5120]{1,0:T(8,128)} %fusion.135, f32[5120]{0:T(1024)S(1)} %bitcast.260, bf16[512,1280]{1,0:T(8,128)(2,1)S(1)} %copy-done.55, bf16[5120,1280]{1,0:T(8,128)(2,1)} %all-gather.28.cloned.1.call-done), kind=kOutput, calls=%fused_computation.44 | convolution fusion | flops 6902251520 | bytes 40652800 | tf_op jit(solution)/shard_map/dot_general | solution.py:31
  711.8 13.5 fusion.138
  725.3 36.5 %add_convert_fusion = (bf16[512,5120]{1,0:T(8,128)(2,1)}, f32[512,5120]{1,0:T(8,128)}, bf16[512,5120]{1,0:T(8,128)(2,1)}) fusion(f32[512,5120]{1,0:T(8,128)S(1)} %copy-done.31, f32[5120]{0:T(1024)S(1)} %bitcast.261, f32[512,5120]{1,0:T(8,128)} %get-tuple-element.64, f32[512,5120]{1,0:T(8,128)} %fusion.135, bf16[512,1280]{1,0:T(8,128)(2,1)S(1)} %copy-done.57, ...), kind=kOutput, calls=%fused_computation.43 | convolution fusion | flops 6912737280 | bytes 66867200 | tf_op jit(solution)/shard_map/dot_general | solution.py:31
  761.9 17.0 multiply_reduce_fusion.4
  838.2 11.0 multiply_reduce_fusion.1
  849.2 12.7 multiply_convert_fusion.1
  894.8 11.9 multiply_reduce_fusion.3
  906.8 12.5 multiply_convert_fusion.3
  986.2 28.7 %reduce-scatter.13.cloned.1.call-done = f32[512,1280]{0,1:T(8,128)} async-done(((f32[1024,1280]{0,1:T(8,128)}), f32[512,1280]{0,1:T(8,128)}) %reduce-scatter.13.cloned.1.call-update) | async-done | bytes 2621456 | tf_op jit(solution)/shard_map/reduce_scatter | solution.py:258
  1017.9 65.0 %reduce-scatter.9.cloned.1.call-done = f32[512,1280]{0,1:T(8,128)} async-done(((f32[1024,1280]{0,1:T(8,128)}), f32[512,1280]{0,1:T(8,128)}) %reduce-scatter.9.cloned.1.call-update) | async-done | bytes 2621456 | tf_op jit(solution)/shard_map/reduce_scatter | solution.py:258
  1085.9 31.7 %fusion.67 = f32[1280,3840]{1,0:T(8,128)} fusion(bf16[512,1280]{1,0:T(8,128)(2,1)} %copy-done.70, bf16[512,1280]{1,0:T(8,128)(2,1)} %copy-done.69, bf16[512,1280]{0,1:T(8,128)(2,1)S(1)} %convert_element_type.198, bf16[512,1280]{0,1:T(8,128)(2,1)} %convert_element_type.195, bf16[512,640]{0,1:T(8,128)(2,1)} %bitcast.246, bf16[512,640]{0,1:T(8,128)(2,1)} %bitcast.243, ...), kind=kOutput, calls=%fused_computation.137 | convolution fusion | flops 10134487040 | bytes 30146560 | tf_op jit(solution)/shard_map/dot_general | solution.py:25
  1118.3 10.8 multiply_convert_fusion.4
  1129.1 21.6 fusion.10
  1152.5 21.7 fusion.40
  1174.3 213.3 %reduce-scatter.17.cloned.1.call-done = f32[640,3840]{1,0:T(8,128)} async-done(((f32[1280,3840]{1,0:T(8,128)}), f32[640,3840]{1,0:T(8,128)}) %reduce-scatter.17.cloned.1.call-update) | async-done | bytes 9830416 | tf_op jit(solution)/shard_map/reduce_scatter | solution.py:275
  1387.6 292.8 %reduce-scatter.23.cloned.1.call-done = f32[2560,1280]{1,0:T(8,128)} async-done(((f32[5120,1280]{1,0:T(8,128)}), f32[2560,1280]{1,0:T(8,128)}) %reduce-scatter.23.cloned.1.call-update) | async-done | bytes 13107216 | tf_op jit(solution)/shard_map/reduce_scatter | solution.py:275
  1680.4 292.8 %reduce-scatter.21.cloned.1.call-done = f32[640,5120]{1,0:T(8,128)} async-done(((f32[1280,5120]{1,0:T(8,128)}), f32[640,5120]{1,0:T(8,128)}) %reduce-scatter.21.cloned.1.call-update) | async-done | bytes 13107216 | tf_op jit(solution)/shard_map/reduce_scatter | solution.py:275
  1985.4 12.1 fusion.61
  2016.2 11.1 fusion.49
  2027.3 13.3 multiply_reduce_fusion.7
  2040.6 23.6 convert_reduce_fusion.1
  2072.8 64.3 %all-reduce.9 = (f32[640]{0:T(1024)}, f32[640]{0:T(1024)}, f32[640]{0:T(1024)}, f32[640]{0:T(1024)}, f32[640]{0:T(1024)}, /*index=5*/f32[640]{0:T(1024)}, f32[640]{0:T(1024)}, f32[2560]{0:T(1024)}, f32[640]{0:T(1024)}) all-reduce(f32[640]{0:T(1024)S(1)} %dynamic-slice.1, ...), channel_id=1, replica_groups=mesh['rep'=16,'fsdp'=2] {'rep'}, use_global_device_ids=true, to_apply=%region_37.38 | all-reduce | flops 7680 | bytes 61440 | tf_op jit(solution)/shard_map/psum | solution.py:278
  2148.1 489.1 %all-reduce.14.cloned.1.call-done = (f32[640,3840]{1,0:T(8,128)}, f32[640,1280]{1,0:T(8,128)}, f32[640,5120]{1,0:T(8,128)}, f32[2560,1280]{1,0:T(8,128)}) async-done(((f32[640,3840]{1,0:T(8,128)}, f32[640,1280]{1,0:T(8,128)}, f32[640,5120]{1,0:T(8,128)}, f32[2560,1280]{1,0:T(8,128)}), (f32[640,3840]{1,0:T(8,128)}, f32[640,1280]{1,0:T(8,128)}, f32[640,5120]{1,0:T(8,128)}, ...) | async-done | bytes 39321616 | tf_op jit(solution)/shard_map/psum | solution.py:278
  2647.4 11.3 copy.102
  2658.6 10.5 copy.103
  (517 shorter events, 455.1 us)
Async XLA Ops:
  7.2 127.4 %all-gather.18.cloned.1.call-start = ((), (), s32[]{:S(2)}) async-start(), calls=%async_computation.8 | async-start | bytes 14745600 | tf_op jit(solution)/shard_map/all_gather | solution.py:197
  7.9 198.6 %all-gather.22.cloned.1.call-start = ((), (), s32[]{:S(2)}) async-start(), calls=%async_computation.10 | async-start | bytes 3932160 | tf_op jit(solution)/shard_map/all_gather | solution.py:218
  28.1 114.2 %copy-start.69 = (bf16[512,1280]{1,0:T(8,128)(2,1)}, bf16[512,1280]{1,0:T(8,128)(2,1)S(1)}, u32[]{:S(2)}) copy-start(bf16[512,1280]{1,0:T(8,128)(2,1)S(1)} %get-tuple-element.73) | copy-start | bytes 3932164
  28.1 127.5 %copy-start.70 = (bf16[512,1280]{1,0:T(8,128)(2,1)}, bf16[512,1280]{1,0:T(8,128)(2,1)S(1)}, u32[]{:S(2)}) copy-start(bf16[512,1280]{1,0:T(8,128)(2,1)S(1)} %get-tuple-element.74) | copy-start | bytes 3932164
  146.7 80.5 %all-gather.20.cloned.1.call-start = ((), (), s32[]{:S(2)}) async-start(), calls=%async_computation.9 | async-start | bytes 3932160 | tf_op jit(solution)/shard_map/all_gather | solution.py:219
  168.0 100.2 %all-gather.32.cloned.1.call-start = ((), (), s32[]{:S(2)}) async-start(), calls=%async_computation.15 | async-start | bytes 3932160 | tf_op jit(solution)/shard_map/all_gather | solution.py:218
  171.0 145.1 %all-gather.24.cloned.1.call-start = ((), (), s32[]{:S(2)}) async-start(), calls=%async_computation.11 | async-start | bytes 4915200 | tf_op jit(solution)/shard_map/all_gather | solution.py:200
  171.6 185.5 %all-gather.30.cloned.1.call-start = ((), (), s32[]{:S(2)}) async-start(), calls=%async_computation.14 | async-start | bytes 3932160 | tf_op jit(solution)/shard_map/all_gather | solution.py:219
  172.3 344.7 %all-gather.26.cloned.1.call-start = ((), (), s32[]{:S(2)}) async-start(), calls=%async_computation.12 | async-start | bytes 19660800 | tf_op jit(solution)/shard_map/all_gather | solution.py:204
  173.0 503.8 %all-gather.28.cloned.1.call-start = ((), (), s32[]{:S(2)}) async-start(), calls=%async_computation.13 | async-start | bytes 19660800 | tf_op jit(solution)/shard_map/all_gather | solution.py:206
  173.8 808.1 %reduce-scatter.15.cloned.1.call-start = ((), (), s32[]{:S(2)}) async-start(), calls=%async_computation.19 | async-start | bytes 7864320 | tf_op jit(solution)/shard_map/reduce_scatter | solution.py:259
  187.6 211.2 %copy-start.87 = (f32[1280]{0:T(1024)}, f32[1280]{0:T(1024)S(1)}, u32[]{:S(2)}) copy-start(f32[1280]{0:T(1024)S(1)} %reshape.382) | copy-start | bytes 15364
  210.8 81.9 %copy-start.25 = (bf16[1024,640]{0,1:T(8,128)(2,1)}, bf16[1024,640]{0,1:T(8,128)(2,1)S(1)}, u32[]{:S(2)}) copy-start(bf16[1024,640]{0,1:T(8,128)(2,1)S(1)} %copy.82) | copy-start | bytes 3932164
  321.4 77.5 %copy-start.9 = (f32[512,1280]{1,0:T(8,128)}, f32[512,1280]{1,0:T(8,128)S(1)}, u32[]{:S(2)}) copy-start(f32[512,1280]{1,0:T(8,128)S(1)} %get-tuple-element.122) | copy-start | bytes 7864324
  321.4 77.5 %copy-start.97 = (f32[512]{0:T(512)}, f32[512]{0:T(512)S(1)}, u32[]{:S(2)}) copy-start(f32[512]{0:T(512)S(1)} %broadcast_multiply_fusion.2) | copy-start | bytes 6148
  397.2 135.1 %copy-start.119 = (f32[512]{0:T(512)}, f32[512]{0:T(512)S(1)}, u32[]{:S(2)}) copy-start(f32[512]{0:T(512)S(1)} %multiply_reduce_fusion.12) | copy-start | bytes 6148
  397.2 135.1 %copy-start.115 = (f32[512]{0:T(512)}, f32[512]{0:T(512)S(1)}, u32[]{:S(2)}) copy-start(f32[512]{0:T(512)S(1)} %fusion.101) | copy-start | bytes 6148
  532.3 144.6 %copy-start.55 = (bf16[512,1280]{1,0:T(8,128)(2,1)S(1)}, bf16[512,1280]{1,0:T(8,128)(2,1)}, u32[]{:S(2)}) copy-start(bf16[512,1280]{1,0:T(8,128)(2,1)} %get-tuple-element.81) | copy-start | bytes 3932164
  532.3 144.6 %copy-start.83 = (f32[2,1,2560]{2,1,0:T(1,128)S(1)}, f32[2,1,2560]{2,1,0:T(1,128)}, u32[]{:S(2)}) copy-start(f32[2,1,2560]{2,1,0:T(1,128)} %convert_element_type.210) | copy-start | bytes 61444
  813.1 170.7 %reduce-scatter.11.cloned.1.call-start = ((), (), s32[]{:S(2)}) async-start(), calls=%async_computation.17 | async-start | bytes 7864320 | tf_op jit(solution)/shard_map/reduce_scatter | solution.py:259
  836.5 178.4 %reduce-scatter.13.cloned.1.call-start = ((), (), s32[]{:S(2)}) async-start(), calls=%async_computation.18 | async-start | bytes 7864320 | tf_op jit(solution)/shard_map/reduce_scatter | solution.py:258
  893.3 189.6 %reduce-scatter.9.cloned.1.call-start = ((), (), s32[]{:S(2)}) async-start(), calls=%async_computation.16 | async-start | bytes 7864320 | tf_op jit(solution)/shard_map/reduce_scatter | solution.py:258
  950.6 223.6 %reduce-scatter.19.cloned.1.call-start = ((), (), s32[]{:S(2)}) async-start(), calls=%async_computation.21 | async-start | bytes 9830400 | tf_op jit(solution)/shard_map/reduce_scatter | solution.py:275
  960.2 427.4 %reduce-scatter.17.cloned.1.call-start = ((), (), s32[]{:S(2)}) async-start(), calls=%async_computation.20 | async-start | bytes 29491200 | tf_op jit(solution)/shard_map/reduce_scatter | solution.py:275
  983.8 102.1 %copy-start.63 = (bf16[512,1280]{0,1:T(8,128)(2,1)}, bf16[512,1280]{0,1:T(8,128)(2,1)S(1)}, u32[]{:S(2)}) copy-start(bf16[512,1280]{0,1:T(8,128)(2,1)S(1)} %convert_element_type.198) | copy-start | bytes 3932164
  986.2 131.4 %copy-start.65 = (bf16[512,1280]{0,1:T(8,128)(2,1)}, bf16[512,1280]{0,1:T(8,128)(2,1)S(1)}, u32[]{:S(2)}) copy-start(bf16[512,1280]{0,1:T(8,128)(2,1)S(1)} %convert_element_type.188) | copy-start | bytes 3932164
  1117.6 562.7 %reduce-scatter.23.cloned.1.call-start = ((), (), s32[]{:S(2)}) async-start(), calls=%async_computation.23 | async-start | bytes 39321600 | tf_op jit(solution)/shard_map/reduce_scatter | solution.py:275
  1150.8 822.3 %reduce-scatter.21.cloned.1.call-start = ((), (), s32[]{:S(2)}) async-start(), calls=%async_computation.22 | async-start | bytes 39321600 | tf_op jit(solution)/shard_map/reduce_scatter | solution.py:275
  1174.2 1463.0 %all-reduce.14.cloned.1.call-start = ((), (), s32[]{:S(2)}) async-start(), calls=%async_computation.24 | async-start | bytes 78643200 | tf_op jit(solution)/shard_map/psum | solution.py:278
  2040.6 96.5 %copy-start.104 = (f32[512]{0:T(512)S(1)}, f32[512]{0:T(512)}, u32[]{:S(2)}) copy-start(f32[512]{0:T(512)} %copy-done.103) | copy-start | bytes 6148
  2040.6 96.5 %copy-start.102 = (f32[512]{0:T(512)S(1)}, f32[512]{0:T(512)}, u32[]{:S(2)}) copy-start(f32[512]{0:T(512)} %copy-done.101) | copy-start | bytes 6148
  2040.6 101.7 %slice-start.14 = ((s8[5242880]{0:T(1024)(128)(4,1)}), s8[1048576]{0:T(1024)(128)(4,1)S(1)}, s32[]{:S(2)}) async-start(s8[5242880]{0:T(1024)(128)(4,1)} %bitcast.196), calls=%async_computation.39 | async-start | bytes 2097152
  (139 other events, 1381.2 us)
Sparse Core Ops, SparseCore 0:
  9.6 125.0 all-gather.17
  146.8 39.1 all-gather.21
  188.2 39.0 all-gather.19
  229.2 39.0 all-gather.31
  269.7 46.3 all-gather.23
  318.1 39.0 all-gather.29
  358.7 158.2 all-gather.25
  518.6 158.2 all-gather.27
  813.3 65.6 reduce-scatter.14
  881.2 65.6 reduce-scatter.10
  949.3 65.6 reduce-scatter.12
  1017.2 65.6 reduce-scatter.8
  1085.2 79.8 reduce-scatter.18
  1167.5 220.0 reduce-scatter.16
  1389.7 290.5 reduce-scatter.22
  1682.5 290.5 reduce-scatter.20
  1977.8 659.3 all-reduce.13
where the time goes:
time: 2680 us
  waiting for transfers between devices  1820 us (68%)
  matrix products  426 us (16%)
  other arithmetic  164 us (6%)
  local copies, waits for them, and re-layouts  136 us (5%)
  blocking collectives  112 us (4%)
    reduce_scatter x4, waiting for transfers between devices, on_device(): lax.psum_scatter(weight_grads(joined, small_sum), 'fsdp', scatter_dimensi...  799 us
    psum x1, waiting for transfers between devices, on_device(): lax.psum((owned[0], owned[1], owned[2], owned[3], owned[4], owned[5], own...  489 us
    all_gather x1, waiting for transfers between devices, on_device(): lax.all_gather(shards[11], 'fsdp', axis=0, tiled=True)  135 us
    dot_general x8, matrix products, product_right(): lax.dot_general(left, right, (((1,), (1,)), ((), ())), preferred_element_...  131 us
    all_gather x1, waiting for transfers between devices, on_device(): lax.all_gather(shards[9], 'fsdp', axis=0, tiled=True)  116 us
    all_gather x1, waiting for transfers between devices, on_device(): lax.all_gather(shards[2], 'fsdp', axis=0, tiled=True)  107 us
    reduce_scatter x2, waiting for transfers between devices, on_device(): lax.psum_scatter(key_terms, 'fsdp', scatter_dimension=0, tiled=True)  93.8 us
    unnamed x331, local copies, waits for them, and re-layouts  82.9 us
  transfers between devices with their start and end apart: 17, of which 13 were waited for; matrix products, arithmetic and copies ran while one was open for 19% of the time, Pallas kernels for 0%

commit v1 on v0

--- a/solution.py
+++ b/solution.py
@@ -1,6 +1,10 @@
+import functools
+
 import jax
 import jax.numpy as jnp
 from jax import lax
+from jax.experimental import pallas as pl
+from jax.experimental.pallas import tpu as pltpu
 from jax.sharding import PartitionSpec as P
 
 HEADS = 16
@@ -144,7 +148,7 @@
     )
 
 
-def on_device(
+def general_device(
     frames,
     cotangent,
     clip_lengths,
@@ -296,9 +300,792 @@
     return (jnp.stack(outputs), jnp.stack(input_grads)) + tuple(summed)
 
 
+LOW = jnp.bfloat16
+FULL = jnp.float32
+VMEM = 60 * 2**20
+
+
+def contract(left, right, left_dim, right_dim):
+    return lax.dot_general(
+        left, right, (((left_dim,), (right_dim,)), ((), ())), preferred_element_type=FULL
+    )
+
+
+def const_spec(shape):
+    return pl.BlockSpec(shape, lambda *at: (0,) * len(shape), pipeline_mode=pl.Buffered(1))
+
+
+def call(kernel, grid, in_specs, out_specs, out_shape, scratch=(), flops=0, moved=0, exps=0, aliases=None):
+    return pl.pallas_call(
+        kernel,
+        grid_spec=pltpu.PrefetchScalarGridSpec(
+            num_scalar_prefetch=1,
+            grid=grid,
+            in_specs=in_specs,
+            out_specs=out_specs,
+            scratch_shapes=list(scratch),
+        ),
+        out_shape=out_shape,
+        input_output_aliases=aliases or {},
+        compiler_params=pltpu.CompilerParams(vmem_limit_bytes=VMEM),
+        cost_estimate=pl.CostEstimate(flops=flops, bytes_accessed=moved, transcendentals=exps),
+    )
+
+
+def spread(rows):
+    mean = jnp.mean(rows, axis=-1, keepdims=True)
+    centred = rows - mean
+    scale = lax.rsqrt(jnp.mean(centred * centred, axis=-1, keepdims=True) + 1e-05)
+    return centred * scale, scale
+
+
+def norm_pull(unit, scale, gain, grad):
+    inner = grad * gain
+    along = jnp.mean(inner * unit, axis=-1, keepdims=True)
+    return scale * (inner - jnp.mean(inner, axis=-1, keepdims=True) - unit * along)
+
+
+def vector(params_ref, at, half):
+    return jnp.concatenate(
+        [params_ref[0:1, at : at + half], params_ref[1:2, at : at + half]], axis=1
+    )
+
+
+def struct(shape, dtype):
+    return jax.ShapeDtypeStruct(shape, dtype)
+
+
+def first_norm_kernel(ids, frames_ref, params_ref, norm_ref, low_ref):
+    rows = frames_ref[0]
+    half = rows.shape[1] // 2
+    unit, unused = spread(rows)
+    norm_ref[...] = (unit * vector(params_ref, 0, half) + vector(params_ref, half, half)).astype(LOW)
+    low_ref[...] = rows.astype(LOW)
+
+
+def first_norm(ids, frames, params, other):
+    unused, rows, width = frames.shape
+    block = rows // 2
+    return call(
+        first_norm_kernel,
+        (2,),
+        [
+            pl.BlockSpec((1, block, width), lambda i, ids: (ids[0] ^ other, i, 0)),
+            const_spec(params.shape),
+        ],
+        [pl.BlockSpec((block, width), lambda i, ids: (i, 0))] * 2,
+        [struct((rows, width), LOW)] * 2,
+        moved=rows * width * 8,
+    )(ids, frames, params)
+
+
+def place_weights(ids, target, own_ref, piece_refs):
+    half = own_ref.shape[0]
+    quarter = piece_refs[0].shape[0]
+    side, mine = ids[0], ids[1] // 4
+    target[pl.ds(pl.multiple_of(side * half, half), half), :] = own_ref[...]
+    base = (1 - side) * half
+    for turn in range(4):
+        at = pl.multiple_of(base + (mine ^ turn) * quarter, quarter)
+        target[pl.ds(at, quarter), :] = piece_refs[turn][...]
+
+
+def project_kernel(ids, own_rows, got_rows, own_ref, p0, p1, p2, p3, bias_ref, out_ref, whole_ref, rows_scr):
+    half = own_rows.shape[0]
+
+    @pl.when(pl.program_id(0) == 0)
+    def _():
+        rows_scr[0:half] = own_rows[...]
+        rows_scr[half:] = got_rows[...]
+
+    place_weights(ids, whole_ref, own_ref, (p0, p1, p2, p3))
+    out = contract(rows_scr[...], whole_ref[...], 1, 0) + bias_ref[...]
+    out_ref[...] = out.astype(LOW)
+
+
+def project(ids, own_rows, got_rows, own, pieces, bias):
+    half, width = own_rows.shape
+    columns = own.shape[1]
+    tile = 768
+    return call(
+        project_kernel,
+        (columns // tile,),
+        [const_spec((half, width))] * 2
+        + [pl.BlockSpec((width // 2, tile), lambda j, ids: (0, j))]
+        + [pl.BlockSpec((width // 8, tile), lambda j, ids: (0, j))] * 4
+        + [pl.BlockSpec((1, tile), lambda j, ids: (0, j))],
+        [
+            pl.BlockSpec((2 * half, tile), lambda j, ids: (0, j)),
+            pl.BlockSpec((width, tile), lambda j, ids: (0, j)),
+        ],
+        [struct((2 * half, columns), LOW), struct((width, columns), LOW)],
+        [pltpu.VMEM((2 * half, width), LOW)],
+        flops=4 * half * width * columns,
+        moved=2 * (2 * half * width + 2 * half * columns + 2 * width * columns),
+    )(ids, own_rows, got_rows, own, *pieces, bias)
+
+
+def window(head, size):
+    first = head * size // 128
+    last = -(-(head + 1) * size // 128)
+    return first * 128, last * 128, head * size - first * 128
+
+
+def head_lanes(lanes, offset, size):
+    lane = lax.broadcasted_iota(jnp.int32, (1, lanes), 1)
+    return (lane >= offset) & (lane < offset + size)
+
+
+def attend_kernel(size, per, ids, query_ref, key_ref, value_ref, bias_ref, out_ref, total_ref, acc):
+    scale = size ** (-0.5)
+    bias = bias_ref[...]
+    lane = lax.broadcasted_iota(jnp.int32, (1, 128), 1)
+    acc[...] = jnp.zeros_like(acc)
+    stats = jnp.zeros((query_ref.shape[0], 128), FULL)
+    for head in range(per):
+        low, high, offset = window(head, size)
+        inside = head_lanes(high - low, offset, size)
+        query = query_ref[:, low:high]
+        query = jnp.where(inside, query, jnp.zeros_like(query))
+        scores = contract(query, key_ref[:, low:high], 1, 1) * scale + bias
+        peak = jnp.max(scores, axis=-1, keepdims=True)
+        raised = jnp.exp(scores - peak)
+        summed = jnp.sum(raised, axis=-1, keepdims=True)
+        probs = (raised * (1.0 / summed)).astype(LOW)
+        mixed = contract(probs, value_ref[:, low:high], 1, 0)
+        acc[:, low:high] += jnp.where(inside, mixed, 0.0)
+        stats = jnp.where(lane == head, peak + jnp.log(summed), stats)
+    out_ref[...] = acc[...].astype(LOW)
+    total_ref[...] = stats.T[:per]
+
+
+def attend_rows(ids, qkv, bias, tile=512, groups=2):
+    rows, width = qkv.shape[0], qkv.shape[1] // 3
+    size, per, part = width // HEADS, HEADS // groups, width // groups
+    return call(
+        functools.partial(attend_kernel, size, per),
+        (groups, rows // tile),
+        [
+            pl.BlockSpec((tile, part), lambda g, i, ids: (i, g)),
+            pl.BlockSpec((rows, part), lambda g, i, ids: (0, groups + g)),
+            pl.BlockSpec((rows, part), lambda g, i, ids: (0, 2 * groups + g)),
+            const_spec((1, rows)),
+        ],
+        [
+            pl.BlockSpec((tile, part), lambda g, i, ids: (i, g)),
+            pl.BlockSpec((per, tile), lambda g, i, ids: (g, i)),
+        ],
+        [struct((rows, width), LOW), struct((HEADS, rows), FULL)],
+        [pltpu.VMEM((tile, part), FULL)],
+        flops=12 * rows * rows * width,
+        moved=8 * rows * width,
+        exps=HEADS * rows * rows,
+    )(ids, qkv, qkv, qkv, bias)
+
+
+def attend_back_kernel(
+    size, per, ids, query_ref, key_ref, value_ref, upper_ref, bias_ref, total_ref, grad_ref, acc, key_sum, value_sum
+):
+    step = pl.program_id(1)
+    scale = size ** (-0.5)
+    bias = bias_ref[...]
+    tile = query_ref.shape[0]
+
+    @pl.when(step == 0)
+    def _():
+        key_sum[...] = jnp.zeros_like(key_sum)
+        value_sum[...] = jnp.zeros_like(value_sum)
+
+    acc[...] = jnp.zeros_like(acc)
+    for head in range(per):
+        low, high, offset = window(head, size)
+        inside = head_lanes(high - low, offset, size)
+        query = query_ref[:, low:high]
+        query = jnp.where(inside, query, jnp.zeros_like(query))
+        upper = upper_ref[:, low:high]
+        upper = jnp.where(inside, upper, jnp.zeros_like(upper))
+        keys = key_ref[:, low:high]
+        scores = contract(keys, query, 1, 1) * scale + bias
+        probs = jnp.exp(scores - total_ref[head : head + 1, :])
+        d_probs = contract(value_ref[:, low:high], upper, 1, 1)
+        terms = probs * d_probs
+        d_scores = (terms - probs * jnp.sum(terms, axis=0, keepdims=True)).astype(LOW)
+        value_sum[:, low:high] += contract(probs.astype(LOW), upper, 1, 0)
+        key_sum[:, low:high] += contract(d_scores, query, 1, 0)
+        acc[:, low:high] += jnp.where(inside, contract(d_scores, keys, 0, 0), 0.0)
+    grad_ref[0, pl.ds(pl.multiple_of(step * tile, tile), tile), :] = (acc[...] * scale).astype(LOW)
+
+    @pl.when(step == pl.num_programs(1) - 1)
+    def _():
+        grad_ref[1] = (key_sum[...] * scale).astype(LOW)
+        grad_ref[2] = value_sum[...].astype(LOW)
+
+
+def attend_back_rows(ids, qkv, upper, bias, totals, tile=512, groups=2):
+    rows, width = upper.shape
+    size, per, part = width // HEADS, HEADS // groups, width // groups
+    return call(
+        functools.partial(attend_back_kernel, size, per),
+        (groups, rows // tile),
+        [
+            pl.BlockSpec((tile, part), lambda g, i, ids: (i, g)),
+            pl.BlockSpec((rows, part), lambda g, i, ids: (0, groups + g)),
+            pl.BlockSpec((rows, part), lambda g, i, ids: (0, 2 * groups + g)),
+            pl.BlockSpec((tile, part), lambda g, i, ids: (i, g)),
+            const_spec((rows, 1)),
+            pl.BlockSpec((per, tile), lambda g, i, ids: (g, i)),
+        ],
+        pl.BlockSpec((3, rows, part), lambda g, i, ids: (0, 0, g)),
+        struct((3, rows, width), LOW),
+        [pltpu.VMEM((tile, part), FULL), pltpu.VMEM((rows, part), FULL), pltpu.VMEM((rows, part), FULL)],
+        flops=24 * rows * rows * width,
+        moved=14 * rows * width,
+        exps=HEADS * rows * rows,
+    )(ids, qkv, qkv, qkv, upper, bias, totals)
+
+
+def out_kernel(ids, mixed_ref, own_ref, p0, p1, p2, p3, frames_ref, got_ref, params_ref, resid_ref, norm_ref, whole_ref):
+    step = pl.program_id(0)
+    half = own_ref.shape[0]
+
+    @pl.when(step == 0)
+    def _():
+        place_weights(ids, whole_ref, own_ref, (p0, p1, p2, p3))
+
+    near = (step < pl.num_programs(0) // 2).astype(FULL)
+    start = frames_ref[0] * near + got_ref[...].astype(FULL) * (1.0 - near)
+    resid = start + contract(mixed_ref[...], whole_ref[...], 1, 0) + vector(params_ref, 4 * half, half)
+    resid_ref[...] = resid
+    unit, unused = spread(resid)
+    norm_ref[...] = (unit * vector(params_ref, 5 * half, half) + vector(params_ref, 6 * half, half)).astype(LOW)
+
+
+def near_spec(tile, width, count):
+    return pl.BlockSpec((1, tile, width), lambda i, ids: (ids[0], jnp.minimum(i, count // 2 - 1), 0))
+
+
+def far_spec(tile, width, count):
+    return pl.BlockSpec((tile, width), lambda i, ids: (jnp.maximum(i - count // 2, 0), 0))
+
+
+def row_spec(tile, width):
+    return pl.BlockSpec((tile, width), lambda i, ids: (i, 0))
+
+
+def out_rows(ids, mixed, own, pieces, frames, got, params, tile=256):
+    rows, width = mixed.shape
+    count = rows // tile
+    piece = pl.BlockSpec((width // 8, width), lambda i, ids: (0, 4), pipeline_mode=pl.Buffered(1))
+    return call(
+        out_kernel,
+        (count,),
+        [row_spec(tile, width), const_spec((width // 2, width))]
+        + [piece] * 4
+        + [near_spec(tile, width, count), far_spec(tile, width, count), const_spec(params.shape)],
+        [row_spec(tile, width), row_spec(tile, width), const_spec((width, width))],
+        [struct((rows, width), FULL), struct((rows, width), LOW), struct((width, width), LOW)],
+        flops=2 * rows * width * width,
+        moved=rows * width * 12 + width * width * 4,
+    )(ids, mixed, own, *pieces, frames, got, params)
+
+
+def bell_parts(values):
+    bell = jnp.exp(values * values * -0.5)
+    return 0.5 + 0.5 * lax.erf(values * (0.5**0.5)), bell
+
+
+def put_pieces(ids, keep_ref, send_ref, source, block):
+    count = keep_ref.shape[1]
+    for far in range(2):
+        for turn in range(2 * count):
+            piece = (ids[0] ^ far) * 2 * count + (ids[1] ^ turn)
+            rows = source[pl.ds(pl.multiple_of(piece * block, block), block), :].astype(LOW)
+            if turn < count:
+                keep_ref[far, turn] = rows
+            else:
+                send_ref[far, turn - count] = rows
+
+
+def feed_kernel(
+    far, tiles, ids, norm_ref, cot_ref, got_ref, resid_ref, own_ref, p0, p1, p2, p3, *refs
+):
+    if far:
+        d0, d1, d2, d3, params_ref = refs[:5]
+        refs = refs[5:]
+    else:
+        down_ref, params_ref = refs[:2]
+        refs = refs[2:]
+    y_ref, dn_ref, keep_ref, send_ref, down_keep, down_send, bias_ref, up_w, down_w, norm_t, grad, grad_low, dout = refs
+    step = pl.program_id(0)
+    half = own_ref.shape[0]
+    tile = own_ref.shape[1]
+    rows = norm_ref.shape[0]
+
+    @pl.when(step == 0)
+    def _():
+        if far:
+            y_ref[...] = jnp.zeros_like(y_ref)
+        else:
+            y_ref[...] = resid_ref[...] + vector(params_ref, 7 * half, half)
+        dn_ref[...] = jnp.zeros_like(dn_ref)
+        norm_t[...] = norm_ref[...].T
+        dout[: rows // 2] = cot_ref[0].astype(LOW)
+        dout[rows // 2 :] = got_ref[...]
+
+    place_weights(ids, up_w, own_ref, (p0, p1, p2, p3))
+    if far:
+        part = tile // 4
+        mine = ids[1] // 4
+        for turn, ref in enumerate((d0, d1, d2, d3)):
+            down_w[pl.ds(pl.multiple_of((mine ^ turn) * part, part), part), :] = ref[0]
+        down = down_w[...]
+    else:
+        down = down_ref[...]
+    up = up_w[...]
+    upper = dout[...]
+    at = pl.multiple_of(8 * half + step * tile, tile)
+    side = (ids[0] ^ far) == 0
+    bias = jnp.where(side, params_ref[0:1, pl.ds(at, tile)], params_ref[1:2, pl.ds(at, tile)])
+    raised = contract(norm_ref[...], up, 1, 0) + bias
+    d_hidden = contract(upper, down, 1, 1)
+    lower, bell = bell_parts(raised)
+    hidden = (raised * lower).astype(LOW)
+    d_up = (d_hidden * (lower + raised * bell * (0.5 / jnp.pi) ** 0.5)).astype(LOW)
+    bias_ref[...] = jnp.sum(d_up.astype(FULL), axis=0, keepdims=True)
+    y_ref[...] += contract(hidden, down, 1, 0)
+    dn_ref[...] += contract(d_up, up, 1, 1)
+    grad[...] = contract(norm_t[...], d_up, 1, 0)
+    put_pieces(ids, keep_ref, send_ref, grad, keep_ref.shape[2])
+    grad_low[...] = contract(hidden, upper, 0, 0)
+    count, block = down_keep.shape[0], down_keep.shape[1]
+    for turn in range(2 * count):
+        low = grad_low[pl.ds(pl.multiple_of((ids[1] ^ turn) * block, block), block), :].astype(LOW)
+        if turn < count:
+            down_keep[turn] = low
+        else:
+            down_send[turn - count] = low
+
+
+def feed_rows(far, ids, norm, cotangent, got, resid, own, pieces, down, params, tile=512):
+    rows, width = norm.shape
+    half = own.shape[1] // 2
+    tiles = half // tile
+    side = lambda ids: ids[0] ^ far
+    own_spec = pl.BlockSpec((width // 2, tile), lambda j, ids: (0, side(ids) * tiles + j))
+    piece_spec = pl.BlockSpec((width // 8, tile), lambda j, ids: (0, side(ids) * tiles + j))
+    if far:
+        down_specs = [pl.BlockSpec((1, tile // 4, width), lambda j, ids: (j, 0, 0))] * 4
+    else:
+        down_specs = [pl.BlockSpec((tile, width), lambda j, ids: (j, 0))]
+        down = (down,)
+    block, fine = width // 32, tile // 16
+    return call(
+        functools.partial(feed_kernel, far, tiles),
+        (tiles,),
+        [
+            const_spec((rows, width)),
+            pl.BlockSpec((1, rows // 2, width), lambda j, ids: (ids[0], 0, 0), pipeline_mode=pl.Buffered(1)),
+            const_spec((rows // 2, width)),
+            const_spec((rows, width)) if not far else const_spec((8, width)),
+            own_spec,
+        ]
+        + [piece_spec] * 4
+        + down_specs
+        + [const_spec(params.shape)],
+        [
+            const_spec((rows, width)),
+            const_spec((rows, width)),
+            pl.BlockSpec((2, 8, block, tile), lambda j, ids: (0, 0, 0, j)),
+            pl.BlockSpec((2, 8, block, tile), lambda j, ids: (0, 0, 0, j)),
+            pl.BlockSpec((8, fine, width), lambda j, ids: (0, j, 0)),
+            pl.BlockSpec((8, fine, width), lambda j, ids: (0, j, 0)),
+            pl.BlockSpec((1, tile), lambda j, ids: (0, j)),
+        ],
+        [struct((rows, width), FULL)] * 2
+        + [struct((2, 8, block, half), LOW)] * 2
+        + [struct((8, half // 16, width), LOW)] * 2
+        + [struct((1, half), FULL)],
+        [
+            pltpu.VMEM((width, tile), LOW),
+            pltpu.VMEM((tile, width), LOW),
+            pltpu.VMEM((width, rows), LOW),
+            pltpu.VMEM((width, tile), FULL),
+            pltpu.VMEM((tile, width), FULL),
+            pltpu.VMEM((rows, width), LOW),
+        ],
+        flops=12 * rows * width * half,
+        moved=rows * width * 14 + width * half * 8,
+        exps=2 * rows * half,
+    )(ids, norm, cotangent, got, resid, own, *pieces, *down, params)
+
+
+def middle_kernel(
+    ids, y0_ref, y1_ref, dn0_ref, dn1_ref, resid_ref, cot_ref, got_ref, mixed_ref, whole_ref, params_ref,
+    near_ref, far_ref, d_resid_ref, d_mixed_ref, keep_ref, send_ref, small_ref, grad, sums,
+):
+    step = pl.program_id(0)
+    count = pl.num_programs(0)
+    half = params_ref.shape[1] // 12
+
+    @pl.when(step == 0)
+    def _():
+        grad[...] = jnp.zeros_like(grad)
+        sums[...] = jnp.zeros_like(sums)
+
+    out = y0_ref[...] + y1_ref[...]
+    is_near = step < count // 2
+
+    @pl.when(is_near)
+    def _():
+        near_ref[0] = out
+
+    @pl.when(jnp.logical_not(is_near))
+    def _():
+        far_ref[...] = out.astype(LOW)
+
+    pick = is_near.astype(FULL)
+    cot = cot_ref[0] * pick + got_ref[...].astype(FULL) * (1.0 - pick)
+    d_norm = dn0_ref[...] + dn1_ref[...]
+    unit, scale = spread(resid_ref[...])
+    d_resid = cot + norm_pull(unit, scale, vector(params_ref, 5 * half, half), d_norm)
+    d_attn = d_resid.astype(LOW)
+    d_resid_ref[...] = d_resid
+    d_mixed_ref[...] = contract(d_attn, whole_ref[...], 1, 1).astype(LOW)
+    grad[...] += contract(mixed_ref[...], d_attn, 0, 0)
+    sums[0:1] += jnp.sum(d_attn.astype(FULL), axis=0, keepdims=True)
+    sums[1:2] += jnp.sum(d_norm * unit, axis=0, keepdims=True)
+    sums[2:3] += jnp.sum(d_norm, axis=0, keepdims=True)
+    sums[3:4] += jnp.sum(cot.astype(LOW).astype(FULL), axis=0, keepdims=True)
+
+    @pl.when(step == count - 1)
+    def _():
+        put_pieces(ids, keep_ref, send_ref, grad, keep_ref.shape[2])
+        small_ref[...] = sums[...]
+
+
+def middle_rows(ids, y0, y1, dn0, dn1, resid, cotangent, got, mixed, whole, params, tile=256):
+    rows, width = mixed.shape
+    count = rows // tile
+    wide = row_spec(tile, width)
+    piece = const_spec((2, 8, width // 32, width))
+    return call(
+        middle_kernel,
+        (count,),
+        [wide] * 5
+        + [near_spec(tile, width, count), far_spec(tile, width, count), wide, const_spec((width, width)), const_spec(params.shape)],
+        [near_spec(tile, width, count), far_spec(tile, width, count), wide, wide, piece, piece, const_spec((8, width))],
+        [
+            struct(cotangent.shape, FULL),
+            struct((rows // 2, width), LOW),
+            struct((rows, width), FULL),
+            struct((rows, width), LOW),
+            struct((2, 8, width // 32, width), LOW),
+            struct((2, 8, width // 32, width), LOW),
+            struct((8, width), FULL),
+        ],
+        [pltpu.VMEM((width, width), FULL), pltpu.VMEM((8, width), FULL)],
+        flops=4 * rows * width * width,
+        moved=rows * width * 36 + width * width * 4,
+    )(ids, y0, y1, dn0, dn1, resid, cotangent, got, mixed, whole, params)
+
+
+def project_grad_kernel(ids, own_rows, got_rows, grad_ref, keep_ref, send_ref, bias_ref, norm_t, grad):
+    half = own_rows.shape[0]
+
+    @pl.when(pl.program_id(0) == 0)
+    def _():
+        norm_t[:, :half] = own_rows[...].T
+        norm_t[:, half:] = got_rows[...].T
+
+    d_part = grad_ref[0]
+    grad[...] = contract(norm_t[...], d_part, 1, 0)
+    put_pieces(ids, keep_ref, send_ref, grad, keep_ref.shape[2])
+    bias_ref[0] = jnp.sum(d_part.astype(FULL), axis=0, keepdims=True)
+
+
+def project_grad(ids, own_rows, got_rows, d_qkv):
+    half, width = own_rows.shape
+    piece = pl.BlockSpec((2, 8, width // 32, width), lambda j, ids: (0, 0, 0, j))
+    return call(
+        project_grad_kernel,
+        (3,),
+        [const_spec((half, width))] * 2 + [pl.BlockSpec((1, 2 * half, width), lambda j, ids: (j, 0, 0))],
+        [piece, piece, pl.BlockSpec((1, 1, width), lambda j, ids: (j, 0, 0))],
+        [struct((2, 8, width // 32, 3 * width), LOW)] * 2 + [struct((3, 1, width), FULL)],
+        [pltpu.VMEM((width, 2 * half), LOW), pltpu.VMEM((width, width), FULL)],
+        flops=12 * half * width * width,
+        moved=16 * half * width + 6 * width * width,
+    )(ids, own_rows, got_rows, d_qkv)
+
+
+def last_kernel(ids, d_qkv_ref, whole_ref, frames_ref, low_ref, d_resid_ref, params_ref, near_ref, far_ref, small_ref, sums):
+    step = pl.program_id(0)
+    count = pl.num_programs(0)
+    half = params_ref.shape[1] // 12
+    width = 2 * half
+
+    @pl.when(step == 0)
+    def _():
+        sums[...] = jnp.zeros_like(sums)
+
+    d_norm = contract(d_qkv_ref[0], whole_ref[:, :width], 1, 1)
+    d_norm += contract(d_qkv_ref[1], whole_ref[:, width : 2 * width], 1, 1)
+    d_norm += contract(d_qkv_ref[2], whole_ref[:, 2 * width :], 1, 1)
+    is_near = step < count // 2
+    pick = is_near.astype(FULL)
+    rows = frames_ref[0] * pick + low_ref[...].astype(FULL) * (1.0 - pick)
+    unit, scale = spread(rows)
+    grad = d_resid_ref[...] + norm_pull(unit, scale, vector(params_ref, 0, half), d_norm)
+    sums[0:1] += jnp.sum(d_norm * unit, axis=0, keepdims=True)
+    sums[1:2] += jnp.sum(d_norm, axis=0, keepdims=True)
+
+    @pl.when(is_near)
+    def _():
+        near_ref[0] = grad
+
+    @pl.when(jnp.logical_not(is_near))
+    def _():
+        far_ref[...] = grad.astype(LOW)
+
+    @pl.when(step == count - 1)
+    def _():
+        small_ref[...] = sums[...]
+
+
+def last_rows(ids, d_qkv, whole, frames, low, d_resid, params, tile=256):
+    rows, width = d_resid.shape
+    count = rows // tile
+    return call(
+        last_kernel,
+        (count,),
+        [
+            pl.BlockSpec((3, tile, width), lambda i, ids: (0, i, 0)),
+            const_spec((width, 3 * width)),
+            near_spec(tile, width, count),
+            far_spec(tile, width, count),
+            row_spec(tile, width),
+            const_spec(params.shape),
+        ],
+        [near_spec(tile, width, count), far_spec(tile, width, count), const_spec((8, width))],
+        [struct(frames.shape, FULL), struct((rows // 2, width), LOW), struct((8, width), FULL)],
+        [pltpu.VMEM((8, width), FULL)],
+        flops=6 * rows * width * width,
+        moved=rows * width * 18 + width * width * 6,
+    )(ids, d_qkv, whole, frames, low, d_resid, params)
+
+
+def fill_kernel(ids, whole_ref, part_ref, out_ref):
+    out_ref[0] = part_ref[...].astype(FULL)
+
+
+def fill_rows(ids, whole, part):
+    rows, width = part.shape
+    tile = rows // 2
+    return call(
+        fill_kernel,
+        (2,),
+        [pl.BlockSpec(memory_space=pl.ANY), pl.BlockSpec((tile, width), lambda i, ids: (i, 0))],
+        pl.BlockSpec((1, tile, width), lambda i, ids: (1 - ids[0], i, 0)),
+        struct(whole.shape, FULL),
+        moved=rows * width * 6,
+        aliases={1: 0},
+    )(ids, whole, part)
+
+
+def settle_kernel(ids, *refs):
+    out_ref = refs[-1]
+    step = pl.program_id(0)
+    for at in range(len(refs) // 2):
+        keep_ref, got_ref = refs[2 * at], refs[2 * at + 1]
+
+        @pl.when((step >= 16 * at) & (step < 16 * at + 8))
+        def _():
+            out_ref[...] = keep_ref[...].reshape(out_ref.shape).astype(FULL)
+
+        @pl.when((step >= 16 * at + 8) & (step < 16 * at + 16))
+        def _():
+            out_ref[...] = got_ref[...].reshape(out_ref.shape).astype(FULL)
+
+
+def settle(ids, pairs, shape, block, place):
+    count, rows, columns = pairs[0][0].shape
+    specs = []
+    for at in range(len(pairs)):
+        for side in range(2):
+            first = 16 * at + 8 * side
+            specs.append(
+                pl.BlockSpec((1, rows, columns), lambda s, ids, first=first: (jnp.clip(s - first, 0, 7), 0, 0))
+            )
+    return call(
+        settle_kernel,
+        (16 * len(pairs),),
+        specs,
+        pl.BlockSpec(block, lambda s, ids: place(ids, s // 16, (s % 16) ^ ids[1])),
+        struct(shape, FULL),
+        moved=len(pairs) * 16 * rows * columns * 6,
+    )(ids, *[array for pair in pairs for array in pair])
+
+
+CORE, Y, NEAR_Z, FAR_Z = 1, 2, 4, 8
+
+
+def swap(array, bit):
+    return lax.ppermute(array, "rep", [(at, at ^ bit) for at in range(16)])
+
+
+def cross(array):
+    return lax.ppermute(array, "fsdp", [(0, 1), (1, 0)])
+
+
+def plus(first, second):
+    return first.astype(FULL) + second.astype(FULL)
+
+
+def reduce_pieces(keep_near, keep_far, send_near, send_far):
+    got_far = swap(send_far, CORE)
+    got_near = swap(send_near, CORE)
+    over = cross(plus(keep_far, got_far).astype(LOW))
+    total = plus(keep_near, got_near) + over.astype(FULL)
+    return reduce_rest(total)
+
+
+def reduce_rest(total):
+    for bit in (Y, NEAR_Z, FAR_Z):
+        half = total.shape[0] // 2
+        got = swap(total[half:].astype(LOW), bit)
+        total = plus(total[:half], got)
+    return total.astype(LOW)
+
+
+def gather_pieces(piece):
+    for bit in (FAR_Z, NEAR_Z, Y):
+        piece = jnp.concatenate([piece, swap(piece, bit)], axis=0)
+    return piece, swap(piece, CORE)
+
+
+def fetch(piece):
+    first = cross(piece)
+    second = swap(first, Y)
+    return first, second, swap(first, CORE), swap(second, CORE)
+
+
+def paired_device(
+    frames, cotangent, clip_lengths, clip_slots, gain_attn, shift_attn, w_qkv, bias_query, bias_value,
+    w_out, bias_out, gain_ffn, shift_ffn, w_up, bias_up, w_down, bias_down,
+):
+    unused, rows, width = frames.shape
+    half = width // 2
+    quarter = half // 4
+    side = lax.axis_index("fsdp")
+    at = lax.axis_index("rep")
+    mine = ((at & 1) << 3) | ((at & 2) << 1) | ((at & 4) >> 1) | ((at & 8) >> 3)
+    ids = jnp.stack([side, mine]).astype(jnp.int32)
+    fourth = mine // 4
+
+    own_small = jnp.concatenate(
+        [gain_attn, shift_attn, bias_query, bias_value, bias_out, gain_ffn, shift_ffn, bias_down, bias_up]
+    )[None]
+    got_small = cross(own_small)
+    params = jnp.concatenate(
+        [jnp.where(side == 0, own_small, got_small), jnp.where(side == 0, got_small, own_small)], axis=0
+    ).astype(FULL)
+
+    def piece_of(weight):
+        return lax.dynamic_slice_in_dim(weight, fourth * quarter, quarter, axis=0)
+
+    pieces_qkv = fetch(piece_of(w_qkv))
+    send_norm, send_low = first_norm(ids, frames, params, 1)
+    own_norm, unused = first_norm(ids, frames, params, 0)
+    got_norm = cross(send_norm)
+    got_low = cross(send_low)
+    got_cot = cross(lax.dynamic_index_in_dim(cotangent, 1 - side, 0, keepdims=False).astype(LOW))
+    pieces_up = fetch(jnp.concatenate([piece_of(w_up), piece_of(w_out)], axis=1))
+    tile = 512
+    tiles = w_down.shape[0] // tile
+    pieces_down = fetch(
+        lax.dynamic_index_in_dim(w_down.reshape(tiles, 4, tile // 4, width), fourth, 1, keepdims=False)
+    )
+
+    bias_qkv = jnp.concatenate(
+        [params[:, 2 * half : 3 * half].reshape(1, width), jnp.zeros((1, width), FULL), params[:, 3 * half : 4 * half].reshape(1, width)],
+        axis=1,
+    )
+    slot = lax.dynamic_index_in_dim(clip_slots, side, 0, keepdims=False)
+    numbers = jnp.arange(clip_lengths.shape[0], dtype=jnp.int32)
+    span = jnp.sum(jnp.where(numbers == slot, clip_lengths, 0))
+    place = jnp.arange(2 * rows, dtype=jnp.int32)
+    place = jnp.where(place < rows, place + side * rows, place - rows + (1 - side) * rows)
+    mask = jnp.where(place < span, 0.0, -1e30).astype(FULL)
+
+    qkv, whole_qkv = project(ids, own_norm, got_norm, w_qkv, pieces_qkv, bias_qkv)
+    mixed, totals = attend_rows(ids, qkv, mask[None])
+    resid, norm_f, whole_out = out_rows(ids, mixed, w_out, pieces_up, frames, got_low, params)
+    y0, dn0, up_keep0, up_send0, down_keep0, down_send0, bias0 = feed_rows(
+        0, ids, norm_f, cotangent, got_cot, resid, w_up, pieces_up, w_down, params
+    )
+    y1, dn1, up_keep1, up_send1, down_keep1, down_send1, bias1 = feed_rows(
+        1, ids, norm_f, cotangent, got_cot, resid, w_up, pieces_up, pieces_down, params
+    )
+    up0 = gather_pieces(reduce_pieces(up_keep0[0], up_keep1[1], up_send0[0], up_send1[1]))
+    up1 = gather_pieces(reduce_pieces(up_keep1[0], up_keep0[1], up_send1[0], up_send0[1]))
+    down = gather_pieces(reduce_pieces(down_keep0, down_keep1, down_send0, down_send1))
+    output, far_out, d_resid, d_mixed, out_keep, out_send, small_mid = middle_rows(
+        ids, y0, y1, dn0, dn1, resid, cotangent, got_cot, mixed, whole_out, params
+    )
+    out = gather_pieces(reduce_pieces(out_keep[0], out_keep[1], out_send[0], out_send[1]))
+    output = fill_rows(ids, output, cross(far_out))
+    d_qkv = attend_back_rows(ids, qkv, d_mixed, mask[:, None], totals)
+    qkv_keep, qkv_send, small_qkv = project_grad(ids, own_norm, got_norm, d_qkv)
+    qkv_grad = gather_pieces(reduce_pieces(qkv_keep[0], qkv_keep[1], qkv_send[0], qkv_send[1]))
+    frames_grad, far_grad, small_last = last_rows(ids, d_qkv, whole_qkv, frames, got_low, d_resid, params)
+    frames_grad = fill_rows(ids, frames_grad, cross(far_grad))
+
+    bias_up_sum = jnp.where(side == 0, jnp.concatenate([bias0, bias1]), jnp.concatenate([bias1, bias0]))
+    vectors = [small_last[0], small_last[1], small_qkv[0, 0], small_qkv[2, 0], small_mid[0], small_mid[1], small_mid[2], small_mid[3]]
+    small = jnp.concatenate([v.reshape(2, half) for v in vectors] + [bias_up_sum], axis=1)
+    got = cross(lax.dynamic_slice_in_dim(small, 1 - side, 1, axis=0))
+    small = lax.dynamic_slice_in_dim(small, side, 1, axis=0) + got
+    for bit in (CORE, Y, NEAR_Z, FAR_Z):
+        small = small + swap(small, bit)
+    small = small[0]
+    parts = [small[k * half : (k + 1) * half] for k in range(8)] + [small[8 * half :]]
+
+    def row_place(ids, part, piece):
+        return (piece, 0, 0)
+
+    block = half // 16
+    qkv_out = settle(ids, [qkv_grad], (16, block, 3 * width), (1, block, 3 * width), row_place)
+    out_out = settle(ids, [out], (16, block, width), (1, block, width), row_place)
+    ff = w_up.shape[1]
+    up_out = settle(
+        ids, [up0, up1], (16, block, ff), (1, block, ff // 2), lambda ids, part, piece: (piece, 0, part ^ ids[0])
+    )
+    down_out = settle(
+        ids, [down], (tiles, 16, tile // 16, width), (tiles, 1, tile // 16, width), lambda ids, part, piece: (0, piece, 0, 0)
+    )
+    return (
+        output,
+        frames_grad,
+        parts[0],
+        parts[1],
+        qkv_out.reshape(half, 3 * width),
+        parts[2],
+        parts[3],
+        out_out.reshape(half, width),
+        parts[4],
+        parts[5],
+        parts[6],
+        up_out.reshape(half, ff),
+        parts[8],
+        down_out.reshape(ff // 2, width),
+        parts[7],
+    )
+
+
 def solution(mesh):
+    fast = mesh.shape["fsdp"] == 2 and mesh.shape["rep"] == 16
     return jax.shard_map(
-        on_device,
+        paired_device if fast else general_device,
         mesh=mesh,
         in_specs=(
             P("rep", "fsdp", None),

time: 2680 us -> 1070 us (0.40)
  waiting for transfers between devices: 1820 us -> 570 us
  matrix products: 426 us -> 0 us
  Pallas kernels: 0 us -> 365 us
  other arithmetic: 164 us -> 31.6 us
  blocking collectives: 112 us -> 0 us
  local copies, waits for them, and re-layouts: 136 us -> 35.2 us
  starting transfers between devices: 0.86 us -> 59.8 us
    reduce_scatter x8 -> x0, waiting for transfers between devices: 893 us -> none  [the longest x4 799 us: on_device(): lax.psum_scatter(weight_grads(joined, small_sum), 'fsdp', scatter_dimensi...]
    ppermute x0 -> x73, waiting for transfers between devices: none -> 570 us  [the longest x58 292 us: swap(): return lax.ppermute(array, 'rep', [(at, at ^ bit) for at in range(16)])]
    psum x1 -> x0, waiting for transfers between devices: 489 us -> none  [on_device(): lax.psum((owned[0], owned[1], owned[2], owned[3], owned[4], owned[5], own...]
    all_gather x8 -> x0, waiting for transfers between devices: 434 us -> none  [the longest x1 135 us: on_device(): lax.all_gather(shards[11], 'fsdp', axis=0, tiled=True)]
    dot_general x44 -> x0, matrix products: 426 us -> none  [the longest x8 131 us: product_right(): lax.dot_general(left, right, (((1,), (1,)), ((), ())), preferred_element_...]
    pallas_call x0 -> x17, Pallas kernels: none -> 365 us  [the longest x2 111 us: feed_rows(): call(functools.partial(feed_kernel, far, tiles), (tiles,), [const_spec((r...]
    unnamed x331 -> x81, local copies, waits for them, and re-layouts: 82.9 us -> 10.8 us
    reduce_sum x15 -> x1, other arithmetic: 72.7 us -> 1.28 us  [paired_device(): span = jnp.sum(jnp.where(numbers == slot, clip_lengths, 0))]
  transfers between devices with their start and end apart: 17 -> 73, of which waited for: 13 -> 35; matrix products, arithmetic and copies ran while one was open for 19% -> 5% of each run, Pallas kernels for 0% -> 28%
where the time goes in v1:
time: 1070 us; the launch traced here: 1060 us
  waiting for transfers between devices  570 us (53%)
  Pallas kernels  365 us (34%)
  starting transfers between devices  59.8 us (6%)
  local copies, waits for them, and re-layouts  35.2 us (3%)
  other arithmetic  31.6 us (3%)
    ppermute x58, waiting for transfers between devices, swap(): return lax.ppermute(array, 'rep', [(at, at ^ bit) for at in range(16)])  292 us
    ppermute x15, waiting for transfers between devices, cross(): return lax.ppermute(array, 'fsdp', [(0, 1), (1, 0)])  278 us
    pallas_call x2, Pallas kernels, feed_rows(): call(functools.partial(feed_kernel, far, tiles), (tiles,), [const_spec((r...  111 us
    pallas_call x1, Pallas kernels, attend_back_rows(): call(functools.partial(attend_back_kernel, size, per), (groups, rows // t...  57.3 us
    pallas_call x4, Pallas kernels, settle(): call(settle_kernel, (16 * len(pairs),), specs, pl.BlockSpec(block, lambda...  56.9 us
    ppermute x58, starting transfers between devices, swap(): return lax.ppermute(array, 'rep', [(at, at ^ bit) for at in range(16)])  45.7 us
    pallas_call x1, Pallas kernels, attend_rows(): call(functools.partial(attend_kernel, size, per), (groups, rows // tile),...  33.9 us
    pallas_call x1, Pallas kernels, middle_rows(): call(middle_kernel, (count,), [wide] * 5 + [near_spec(tile, width, count)...  24.1 us
  transfers between devices with their start and end apart: 73, of which 35 were waited for; matrix products, arithmetic and copies ran while one was open for 5% of the time, Pallas kernels for 28%

profile of v1, /device:TPU:0, one launch (start us, length us, event | category | flops | bytes accessed | tf_op | source)
XLA Modules:
  0.0 1063.2 jit_solution(14214417374178115285)
XLA Ops:
  22.1 20.6 %collective-permute-done.2.p0 = bf16[160,3840]{1,0:T(8,128)(2,1)} collective-permute-done((bf16[160,3840]{1,0:T(8,128)(2,1)S(1)}, bf16[160,3840]{1,0:T(8,128)(2,1)}, u32[]{:S(2)}, u32[]{:S(2)}) %collective-permute-start.2) | collective-permute-done | bytes 1228832 | tf_op jit(solution)/shard_map/ppermute | solution.py:937
  44.2 42.3 %collective-permute-done.6.p0 = bf16[160,6400]{1,0:T(8,128)(2,1)S(1)} collective-permute-done((bf16[160,6400]{1,0:T(8,128)(2,1)}, bf16[160,6400]{1,0:T(8,128)(2,1)S(1)}, u32[]{:S(2)}, u32[]{:S(2)}) %collective-permute-start.6) | collective-permute-done | bytes 2048032 | tf_op jit(solution)/shard_map/ppermute | solution.py:937
  99.9 21.8 %collective-permute-done.12.refs_0_ = bf16[5,128,1280]{2,1,0:T(8,128)(2,1)} collective-permute-done((bf16[5,128,1280]{2,1,0:T(8,128)(2,1)}, bf16[5,128,1280]{2,1,0:T(8,128)(2,1)}, u32[]{:S(2)}, u32[]{:S(2)}) %collective-permute-start.12) | collective-permute-done | bytes 1638432 | tf_op jit(solution)/shard_map/ppermute | solution.py:937
  128.9 19.3 %collective-permute-done.1.got_rows = bf16[512,1280]{1,0:T(8,128)(2,1)S(1)} collective-permute-done((bf16[512,1280]{1,0:T(8,128)(2,1)}, bf16[512,1280]{1,0:T(8,128)(2,1)S(1)}, u32[]{:S(2)}, u32[]{:S(2)}) %collective-permute-start.1) | collective-permute-done | bytes 1310752 | tf_op jit(solution)/shard_map/ppermute | solution.py:937
  152.4 16.6 %shard_map.282 = (bf16[1024,3840]{1,0:T(8,128)(2,1)}, bf16[1280,3840]{1,0:T(8,128)(2,1)}) custom-call(s32[2]{0:T(128)} %pad_add_fusion.ids, bf16[512,1280]{1,0:T(8,128)(2,1)} %get-tuple-element.52.own_rows, bf16[512,1280]{1,0:T(8,128)(2,1)} %copy-done.24, bf16[640,3840]{1,0:T(8,128)(2,1)} %own_ref.4, bf16[160,3840]{1,0:T(8,128)(2,1)} %collective-permute-done.2.p0, ...), custom_call_target="tpu_custom_call" | custom-call | flops 10066329600 | bytes 30146560 | tf_op jit(solution)/shard_map/pallas_call | solution.py:410
  169.0 12.2 %collective-permute-done.10.got_ref.low_ref = bf16[512,1280]{1,0:T(8,128)(2,1)S(1)} collective-permute-done((bf16[512,1280]{1,0:T(8,128)(2,1)}, bf16[512,1280]{1,0:T(8,128)(2,1)S(1)}, u32[]{:S(2)}, u32[]{:S(2)}) %collective-permute-start.10) | collective-permute-done | bytes 1310752 | tf_op jit(solution)/shard_map/ppermute | solution.py:937
  181.7 33.9 %shard_map.283 = (bf16[1024,1280]{1,0:T(8,128)(2,1)}, f32[16,1024]{1,0:T(8,128)}) custom-call(s32[2]{0:T(128)} %pad_add_fusion.ids, bf16[1024,3840]{1,0:T(8,128)(2,1)} %get-tuple-element.54.query_ref.key_ref.value_ref, bf16[1024,3840]{1,0:T(8,128)(2,1)} %get-tuple-element.54.query_ref.key_ref.value_ref, ...), custom_call_target="tpu_custom_call" | custom-call | flops 16106127360 | bytes 10485760 | tf_op jit(solution)/shard_map/pallas_call | solution.py:465
  227.5 55.2 %shard_map.286 = (f32[1024,1280]{1,0:T(8,128)}, f32[1024,1280]{1,0:T(8,128)}, bf16[2,8,40,2560]{3,2,1,0:T(8,128)(2,1)}, bf16[2,8,40,2560]{3,2,1,0:T(8,128)(2,1)}...) custom-call(s32[2]{0:T(128)} %pad_add_fusion.ids, ...), custom_call_target="tpu_custom_call" | custom-call | flops 40265318400 | bytes 44564480 | tf_op jit(solution)/shard_map/pallas_call | solution.py:682
  287.1 56.3 %shard_map.285 = (f32[1024,1280]{1,0:T(8,128)}, f32[1024,1280]{1,0:T(8,128)}, bf16[2,8,40,2560]{3,2,1,0:T(8,128)(2,1)}, bf16[2,8,40,2560]{3,2,1,0:T(8,128)(2,1)}...) custom-call(s32[2]{0:T(128)} %pad_add_fusion.ids, ...), custom_call_target="tpu_custom_call" | custom-call | flops 40265318400 | bytes 44564480 | tf_op jit(solution)/shard_map/pallas_call | solution.py:682
  343.4 24.1 %shard_map.287 = (f32[2,512,1280]{2,1,0:T(8,128)}, bf16[512,1280]{1,0:T(8,128)(2,1)}, f32[1024,1280]{1,0:T(8,128)}, bf16[1024,1280]{1,0:T(8,128)(2,1)}, bf16[2,8...) custom-call(s32[2]{0:T(128)} %pad_add_fusion.ids, ...), custom_call_target="tpu_custom_call" | custom-call | flops 6710886400 | bytes 53739520 | tf_op jit(solution)/shard_map/pallas_call | solution.py:771
  367.4 57.3 %shard_map.289.d_qkv_ref.grad_ref = bf16[3,1024,1280]{2,1,0:T(8,128)(2,1)} custom-call(s32[2]{0:T(128)} %pad_add_fusion.ids, bf16[1024,3840]{1,0:T(8,128)(2,1)} %get-tuple-element.54.query_ref.key_ref.value_ref, bf16[1024,3840]{1,0:T(8,128)(2,1)} %get-tuple-element.54.query_ref.key_ref.value_ref, ...), custom_call_target="tpu_custom_call" | custom-call | flops 32212254720 | bytes 18350080 | tf_op jit(solution)/shard_map/pallas_call | solution.py:527
  424.8 17.2 %shard_map.292 = (bf16[2,8,40,3840]{3,2,1,0:T(8,128)(2,1)}, bf16[2,8,40,3840]{3,2,1,0:T(8,128)(2,1)}, f32[3,1,1280]{2,1,0:T(1,128)}) custom-call(s32[2]{0:T(128)} %pad_add_fusion.ids, bf16[512,1280]{1,0:T(8,128)(2,1)} %get-tuple-element.52.own_rows, bf16[512,1280]{1,0:T(8,128)(2,1)} %copy-done.24, bf16[3,1024,1280]{2,1,0:T(8,128)(2,1)} %shard_map.289.d_qkv_ref.grad_ref), custom_call_target="tpu_custom_call" | custom-call | flops 10066329600 | bytes 20316160 | tf_op jit(solution)/shard_map/pallas_call | solution.py:809
  442.8 21.2 %shard_map.290 = (f32[2,512,1280]{2,1,0:T(8,128)}, bf16[512,1280]{1,0:T(8,128)(2,1)}, f32[8,1280]{1,0:T(8,128)}) custom-call(s32[2]{0:T(128)} %pad_add_fusion.ids, bf16[3,1024,1280]{2,1,0:T(8,128)(2,1)} %shard_map.289.d_qkv_ref.grad_ref, bf16[1280,3840]{1,0:T(8,128)(2,1)} %get-tuple-element.68.whole_ref, f32[2,512,1280]{2,1,0:T(8,128)} %frames_ref.7, ...), custom_call_target="tpu_custom_call" | custom-call | flops 10066329600 | bytes 33423360 | tf_op jit(solution)/shard_map/pallas_call | solution.py:858
  472.6 18.5 %collective-permute-done.35 = bf16[8,40,1280]{2,1,0:T(8,128)(2,1)S(1)} collective-permute-done((bf16[8,40,1280]{2,1,0:T(8,128)(2,1)S(1)}, bf16[8,40,1280]{2,1,0:T(8,128)(2,1)S(1)}, u32[]{:S(2)}, u32[]{:S(2)}) %collective-permute-start.35) | collective-permute-done | bytes 819232 | tf_op jit(solution)/shard_map/ppermute | solution.py:937
  512.7 17.2 %collective-permute-done.55 = bf16[8,40,2560]{2,1,0:T(8,128)(2,1)S(1)} collective-permute-done((bf16[8,40,2560]{2,1,0:T(8,128)(2,1)S(1)}, bf16[8,40,2560]{2,1,0:T(8,128)(2,1)S(1)}, u32[]{:S(2)}, u32[]{:S(2)}) %collective-permute-start.55) | collective-permute-done | bytes 1638432 | tf_op jit(solution)/shard_map/ppermute | solution.py:937
  536.6 14.5 %collective-permute-done.56 = bf16[4,40,2560]{2,1,0:T(8,128)(2,1)S(1)} collective-permute-done((bf16[4,40,2560]{2,1,0:T(8,128)(2,1)S(1)}, bf16[4,40,2560]{2,1,0:T(8,128)(2,1)S(1)}, u32[]{:S(2)}, u32[]{:S(2)}) %collective-permute-start.56) | collective-permute-done | bytes 819232 | tf_op jit(solution)/shard_map/ppermute | solution.py:933
  571.6 91.1 %collective-permute-done.45 = bf16[8,40,2560]{2,1,0:T(8,128)(2,1)S(1)} collective-permute-done((bf16[8,40,2560]{2,1,0:T(8,128)(2,1)S(1)}, bf16[8,40,2560]{2,1,0:T(8,128)(2,1)S(1)}, u32[]{:S(2)}, u32[]{:S(2)}) %collective-permute-start.45) | collective-permute-done | bytes 1638432 | tf_op jit(solution)/shard_map/ppermute | solution.py:937
  677.2 33.9 %collective-permute-done.25 = bf16[8,40,3840]{2,1,0:T(8,128)(2,1)} collective-permute-done((bf16[8,40,3840]{2,1,0:T(8,128)(2,1)S(1)}, bf16[8,40,3840]{2,1,0:T(8,128)(2,1)}, u32[]{:S(2)}, u32[]{:S(2)}) %collective-permute-start.25) | collective-permute-done | bytes 2457632 | tf_op jit(solution)/shard_map/ppermute | solution.py:937
  717.0 32.8 %collective-permute-done.66 = bf16[4,160,1280]{2,1,0:T(8,128)(2,1)S(1)} collective-permute-done((bf16[4,160,1280]{2,1,0:T(8,128)(2,1)S(1)}, bf16[4,160,1280]{2,1,0:T(8,128)(2,1)S(1)}, u32[]{:S(2)}, u32[]{:S(2)}) %collective-permute-start.66) | collective-permute-done | bytes 1638432 | tf_op jit(solution)/shard_map/ppermute | solution.py:933
  750.9 19.9 %collective-permute-done.26 = bf16[4,40,3840]{2,1,0:T(8,128)(2,1)S(1)} collective-permute-done((bf16[4,40,3840]{2,1,0:T(8,128)(2,1)S(1)}, bf16[4,40,3840]{2,1,0:T(8,128)(2,1)S(1)}, u32[]{:S(2)}, u32[]{:S(2)}) %collective-permute-start.26) | collective-permute-done | bytes 1228832 | tf_op jit(solution)/shard_map/ppermute | solution.py:933
  773.3 20.8 %collective-permute-done.67 = bf16[2,160,1280]{2,1,0:T(8,128)(2,1)S(1)} collective-permute-done((bf16[2,160,1280]{2,1,0:T(8,128)(2,1)S(1)}, bf16[2,160,1280]{2,1,0:T(8,128)(2,1)S(1)}, u32[]{:S(2)}, u32[]{:S(2)}) %collective-permute-start.67) | collective-permute-done | bytes 819232 | tf_op jit(solution)/shard_map/ppermute | solution.py:933
  807.9 12.7 %collective-permute-done.68 = bf16[1,160,1280]{2,1,0:T(8,128)(2,1)S(1)} collective-permute-done((bf16[1,160,1280]{2,1,0:T(8,128)(2,1)S(1)}, bf16[1,160,1280]{2,1,0:T(8,128)(2,1)S(1)}, u32[]{:S(2)}, u32[]{:S(2)}) %collective-permute-start.68) | collective-permute-done | bytes 409632 | tf_op jit(solution)/shard_map/ppermute | solution.py:933
  820.7 13.4 %collective-permute-done.28 = bf16[1,40,3840]{2,1,0:T(8,128)(2,1)S(1)} collective-permute-done((bf16[1,40,3840]{2,1,0:T(8,128)(2,1)S(1)}, bf16[1,40,3840]{2,1,0:T(8,128)(2,1)S(1)}, u32[]{:S(2)}, u32[]{:S(2)}) %collective-permute-start.28) | collective-permute-done | bytes 307232 | tf_op jit(solution)/shard_map/ppermute | solution.py:933
  834.2 20.5 %collective-permute-done.69 = bf16[1,160,1280]{2,1,0:T(8,128)(2,1)S(1)} collective-permute-done((bf16[1,160,1280]{2,1,0:T(8,128)(2,1)S(1)}, bf16[1,160,1280]{2,1,0:T(8,128)(2,1)S(1)}, u32[]{:S(2)}, u32[]{:S(2)}) %collective-permute-start.69) | collective-permute-done | bytes 409632 | tf_op jit(solution)/shard_map/ppermute | solution.py:933
  857.1 13.4 %collective-permute-done.29 = bf16[1,40,3840]{2,1,0:T(8,128)(2,1)S(1)} collective-permute-done((bf16[1,40,3840]{2,1,0:T(8,128)(2,1)S(1)}, bf16[1,40,3840]{2,1,0:T(8,128)(2,1)S(1)}, u32[]{:S(2)}, u32[]{:S(2)}) %collective-permute-start.29) | collective-permute-done | bytes 307232 | tf_op jit(solution)/shard_map/ppermute | solution.py:933
  870.5 15.6 %collective-permute-done.70 = bf16[2,160,1280]{2,1,0:T(8,128)(2,1)S(1)} collective-permute-done((bf16[2,160,1280]{2,1,0:T(8,128)(2,1)S(1)}, bf16[2,160,1280]{2,1,0:T(8,128)(2,1)S(1)}, u32[]{:S(2)}, u32[]{:S(2)}) %collective-permute-start.70) | collective-permute-done | bytes 819232 | tf_op jit(solution)/shard_map/ppermute | solution.py:933
  889.1 13.8 %collective-permute-done.30 = bf16[2,40,3840]{2,1,0:T(8,128)(2,1)S(1)} collective-permute-done((bf16[2,40,3840]{2,1,0:T(8,128)(2,1)S(1)}, bf16[2,40,3840]{2,1,0:T(8,128)(2,1)S(1)}, u32[]{:S(2)}, u32[]{:S(2)}) %collective-permute-start.30) | collective-permute-done | bytes 614432 | tf_op jit(solution)/shard_map/ppermute | solution.py:933
  926.8 24.7 %collective-permute-done.31 = bf16[4,40,3840]{2,1,0:T(8,128)(2,1)S(1)} collective-permute-done((bf16[4,40,3840]{2,1,0:T(8,128)(2,1)S(1)}, bf16[4,40,3840]{2,1,0:T(8,128)(2,1)S(1)}, u32[]{:S(2)}, u32[]{:S(2)}) %collective-permute-start.31) | collective-permute-done | bytes 1228832 | tf_op jit(solution)/shard_map/ppermute | solution.py:933
  969.6 15.2 %collective-permute-done.51 = bf16[4,40,2560]{2,1,0:T(8,128)(2,1)S(1)} collective-permute-done((bf16[4,40,2560]{2,1,0:T(8,128)(2,1)S(1)}, bf16[4,40,2560]{2,1,0:T(8,128)(2,1)S(1)}, u32[]{:S(2)}, u32[]{:S(2)}) %collective-permute-start.51) | collective-permute-done | bytes 819232 | tf_op jit(solution)/shard_map/ppermute | solution.py:933
  1016.4 21.1 %shard_map.295 = f32[16,40,5120]{2,1,0:T(8,128)} custom-call(s32[2]{0:T(128)} %pad_add_fusion.ids, bf16[8,40,2560]{2,1,0:T(8,128)(2,1)} %pad_maximum_fusion.3.refs_0_, bf16[8,40,2560]{2,1,0:T(8,128)(2,1)} %collective-permute-done.52.refs_1_, bf16[8,40,2560]{2,1,0:T(8,128)(2,1)} %pad_maximum_fusion.4.refs_2_, bf16[8,40,2560]{2,1,0:T(8,128)(2,1)} %collective-permute-done.62.refs_3_), custom_call_target="tpu_custom_call" | custom-call | bytes 19660800 | tf_op jit(solution)/shard_map/pallas_call | solution.py:919
  1037.5 12.2 %shard_map.293 = f32[16,40,3840]{2,1,0:T(8,128)} custom-call(s32[2]{0:T(128)} %pad_add_fusion.ids, bf16[8,40,3840]{2,1,0:T(8,128)(2,1)} %pad_maximum_fusion.1.refs_0_, bf16[8,40,3840]{2,1,0:T(8,128)(2,1)} %collective-permute-done.32.refs_1_), custom_call_target="tpu_custom_call" | custom-call | bytes 14745600 | tf_op jit(solution)/shard_map/pallas_call | solution.py:919
  1049.7 13.3 %shard_map.296 = f32[5,16,32,1280]{3,2,1,0:T(8,128)} custom-call(s32[2]{0:T(128)} %pad_add_fusion.ids, bf16[8,160,1280]{2,1,0:T(8,128)(2,1)} %copy-done, bf16[8,160,1280]{2,1,0:T(8,128)(2,1)} %collective-permute-done.72.refs_1_), custom_call_target="tpu_custom_call" | custom-call | bytes 19660800 | tf_op jit(solution)/shard_map/pallas_call | solution.py:919
  (311 shorter events, 239.0 us)
Async XLA Ops:
  16.7 69.8 %collective-permute-start.6 = (bf16[160,6400]{1,0:T(8,128)(2,1)}, bf16[160,6400]{1,0:T(8,128)(2,1)S(1)}, u32[]{:S(2)}, u32[]{:S(2)}) collective-permute-start(bf16[160,6400]{1,0:T(8,128)(2,1)} %pad_maximum_fusion.2), channel_id=1, source_target_pairs={{0,1},{1,0},{2,3},{3,2},{4,5},{5,4},{6,7},{7,6},{8,9},{9,8},{10,11... | collective-permute-start | bytes 6144008 | tf_op jit(solution)/shard_map/ppermute | solution.py:937
  21.4 100.3 %collective-permute-start.12 = (bf16[5,128,1280]{2,1,0:T(8,128)(2,1)}, bf16[5,128,1280]{2,1,0:T(8,128)(2,1)}, u32[]{:S(2)}, u32[]{:S(2)}) collective-permute-start(bf16[5,128,1280]{2,1,0:T(8,128)(2,1)} %dynamic-slice_bitcast_fusion), channel_id=1, source_target_pairs={{0,1},{1,0},{2,3},{3,2},{4,5},{5,4},{6,7},{7,6},{8,9},{9,8},{10,11... | collective-permute-start | bytes 4915208 | tf_op jit(solution)/shard_map/ppermute | solution.py:937
  42.7 51.0 %collective-permute-start.3 = (bf16[160,3840]{1,0:T(8,128)(2,1)}, bf16[160,3840]{1,0:T(8,128)(2,1)}, u32[]{:S(2)}, u32[]{:S(2)}) collective-permute-start(bf16[160,3840]{1,0:T(8,128)(2,1)} %collective-permute-done.2.p0), channel_id=1, source_target_pairs={{0,4},{2,6},{4,0},{6,2},{8,12},{10,14},{12,8},{14,10},{16,20},{18,... | collective-permute-start | bytes 3686408 | tf_op jit(solution)/shard_map/ppermute | solution.py:933
  86.5 65.5 %collective-permute-start.7 = (bf16[160,6400]{1,0:T(8,128)(2,1)S(1)}, bf16[160,6400]{1,0:T(8,128)(2,1)}, u32[]{:S(2)}, u32[]{:S(2)}) collective-permute-start(bf16[160,6400]{1,0:T(8,128)(2,1)S(1)} %collective-permute-done.6.p0), channel_id=1, source_target_pairs={{0,4},{2,6},{4,0},{6,2},{8,12},{10,14},{12,8},{14,10},{16,20},{18,... | collective-permute-start | bytes 6144008 | tf_op jit(solution)/shard_map/ppermute | solution.py:933
  92.5 55.7 %collective-permute-start.1 = (bf16[512,1280]{1,0:T(8,128)(2,1)}, bf16[512,1280]{1,0:T(8,128)(2,1)S(1)}, u32[]{:S(2)}, u32[]{:S(2)}) collective-permute-start(bf16[512,1280]{1,0:T(8,128)(2,1)} %get-tuple-element.53), channel_id=1, source_target_pairs={{0,1},{1,0},{2,3},{3,2},{4,5},{5,4},{6,7},{7,6},{8,9},{9,8},{10,11... | collective-permute-start | bytes 3932168 | tf_op jit(solution)/shard_map/ppermute | solution.py:937
  93.7 56.6 %collective-permute-start.4 = (bf16[160,3840]{1,0:T(8,128)(2,1)}, bf16[160,3840]{1,0:T(8,128)(2,1)}, u32[]{:S(2)}, u32[]{:S(2)}) collective-permute-start(bf16[160,3840]{1,0:T(8,128)(2,1)} %collective-permute-done.2.p0), channel_id=1, source_target_pairs={{0,2},{2,0},{4,6},{6,4},{8,10},{10,8},{12,14},{14,12},{16,18},{18,... | collective-permute-start | bytes 3686408 | tf_op jit(solution)/shard_map/ppermute | solution.py:933
  93.7 58.3 %collective-permute-start.5 = (bf16[160,3840]{1,0:T(8,128)(2,1)}, bf16[160,3840]{1,0:T(8,128)(2,1)}, u32[]{:S(2)}, u32[]{:S(2)}) collective-permute-start(bf16[160,3840]{1,0:T(8,128)(2,1)} %collective-permute-done.3.p1), channel_id=1, source_target_pairs={{0,2},{2,0},{4,6},{6,4},{8,10},{10,8},{12,14},{14,12},{16,18},{18,... | collective-permute-start | bytes 3686408 | tf_op jit(solution)/shard_map/ppermute | solution.py:933
  121.7 59.5 %collective-permute-start.13 = (bf16[5,128,1280]{2,1,0:T(8,128)(2,1)}, bf16[5,128,1280]{2,1,0:T(8,128)(2,1)}, u32[]{:S(2)}, u32[]{:S(2)}) collective-permute-start(bf16[5,128,1280]{2,1,0:T(8,128)(2,1)} %collective-permute-done.12.refs_0_), channel_id=1, source_target_pairs={{0,4},{2,6},{4,0},{6,2},{8,12},{10,14},{12,8},{14,10},{16,20},{18,... | collective-permute-start | bytes 4915208 | tf_op jit(solution)/shard_map/ppermute | solution.py:933
  150.2 77.3 %collective-permute-start.11 = (bf16[512,1280]{1,0:T(8,128)(2,1)}, bf16[512,1280]{1,0:T(8,128)(2,1)}, u32[]{:S(2)}, u32[]{:S(2)}) collective-permute-start(bf16[512,1280]{1,0:T(8,128)(2,1)} %fusion.8), channel_id=1, source_target_pairs={{0,1},{1,0},{2,3},{3,2},{4,5},{5,4},{6,7},{7,6},{8,9},{9,8},{10,11... | collective-permute-start | bytes 3932168 | tf_op jit(solution)/shard_map/ppermute | solution.py:937
  151.9 63.6 %collective-permute-start.8 = (bf16[160,6400]{1,0:T(8,128)(2,1)S(1)}, bf16[160,6400]{1,0:T(8,128)(2,1)}, u32[]{:S(2)}, u32[]{:S(2)}) collective-permute-start(bf16[160,6400]{1,0:T(8,128)(2,1)S(1)} %collective-permute-done.6.p0), channel_id=1, source_target_pairs={{0,2},{2,0},{4,6},{6,4},{8,10},{10,8},{12,14},{14,12},{16,18},{18,... | collective-permute-start | bytes 6144008 | tf_op jit(solution)/shard_map/ppermute | solution.py:933
  151.9 63.6 %collective-permute-start.9 = (bf16[160,6400]{1,0:T(8,128)(2,1)}, bf16[160,6400]{1,0:T(8,128)(2,1)}, u32[]{:S(2)}, u32[]{:S(2)}) collective-permute-start(bf16[160,6400]{1,0:T(8,128)(2,1)} %collective-permute-done.7.p1), channel_id=1, source_target_pairs={{0,2},{2,0},{4,6},{6,4},{8,10},{10,8},{12,14},{14,12},{16,18},{18,... | collective-permute-start | bytes 6144008 | tf_op jit(solution)/shard_map/ppermute | solution.py:933
  181.2 46.3 %collective-permute-start.14 = (bf16[5,128,1280]{2,1,0:T(8,128)(2,1)}, bf16[5,128,1280]{2,1,0:T(8,128)(2,1)}, u32[]{:S(2)}, u32[]{:S(2)}) collective-permute-start(bf16[5,128,1280]{2,1,0:T(8,128)(2,1)} %collective-permute-done.12.refs_0_), channel_id=1, source_target_pairs={{0,2},{2,0},{4,6},{6,4},{8,10},{10,8},{12,14},{14,12},{16,18},{18,... | collective-permute-start | bytes 4915208 | tf_op jit(solution)/shard_map/ppermute | solution.py:933
  181.2 46.3 %collective-permute-start.15 = (bf16[5,128,1280]{2,1,0:T(8,128)(2,1)}, bf16[5,128,1280]{2,1,0:T(8,128)(2,1)}, u32[]{:S(2)}, u32[]{:S(2)}) collective-permute-start(bf16[5,128,1280]{2,1,0:T(8,128)(2,1)} %collective-permute-done.13.refs_1_), channel_id=1, source_target_pairs={{0,2},{2,0},{4,6},{6,4},{8,10},{10,8},{12,14},{14,12},{16,18},{18,... | collective-permute-start | bytes 4915208 | tf_op jit(solution)/shard_map/ppermute | solution.py:933
  286.6 223.0 %collective-permute-start.53 = (bf16[8,40,2560]{2,1,0:T(8,128)(2,1)}, bf16[8,40,2560]{2,1,0:T(8,128)(2,1)}, u32[]{:S(2)}, u32[]{:S(2)}) collective-permute-start(bf16[8,40,2560]{2,1,0:T(8,128)(2,1)} %get-tuple-element.109), channel_id=1, source_target_pairs={{0,2},{2,0},{4,6},{6,4},{8,10},{10,8},{12,14},{14,12},{16,18},{18,... | collective-permute-start | bytes 4915208 | tf_op jit(solution)/shard_map/ppermute | solution.py:933
  286.7 223.5 %collective-permute-start.44 = (bf16[8,40,2560]{2,1,0:T(8,128)(2,1)}, bf16[8,40,2560]{2,1,0:T(8,128)(2,1)}, u32[]{:S(2)}, u32[]{:S(2)}) collective-permute-start(bf16[8,40,2560]{2,1,0:T(8,128)(2,1)} %get-tuple-element.110), channel_id=1, source_target_pairs={{0,2},{2,0},{4,6},{6,4},{8,10},{10,8},{12,14},{14,12},{16,18},{18,... | collective-permute-start | bytes 4915208 | tf_op jit(solution)/shard_map/ppermute | solution.py:933
  508.9 44.0 %collective-permute-start.64 = (bf16[8,160,1280]{2,1,0:T(8,128)(2,1)S(1)}, bf16[8,160,1280]{2,1,0:T(8,128)(2,1)S(1)}, u32[]{:S(2)}, u32[]{:S(2)}) collective-permute-start(bf16[8,160,1280]{2,1,0:T(8,128)(2,1)S(1)} %copy-done.21), channel_id=1, source_target_pairs={{0,2},{2,0},{4,6},{6,4},{8,10},{10,8},{12,14},{14,12},{16,18},{18,... | collective-permute-start | bytes 9830408 | tf_op jit(solution)/shard_map/ppermute | solution.py:933
  508.9 55.0 %collective-permute-start.43 = (bf16[8,40,2560]{2,1,0:T(8,128)(2,1)}, bf16[8,40,2560]{2,1,0:T(8,128)(2,1)}, u32[]{:S(2)}, u32[]{:S(2)}) collective-permute-start(bf16[8,40,2560]{2,1,0:T(8,128)(2,1)} %get-tuple-element.112), channel_id=1, source_target_pairs={{0,2},{2,0},{4,6},{6,4},{8,10},{10,8},{12,14},{14,12},{16,18},{18,... | collective-permute-start | bytes 4915208 | tf_op jit(solution)/shard_map/ppermute | solution.py:933
  535.4 133.1 %collective-permute-start.63 = (bf16[8,160,1280]{2,1,0:T(8,128)(2,1)}, bf16[8,160,1280]{2,1,0:T(8,128)(2,1)}, u32[]{:S(2)}, u32[]{:S(2)}) collective-permute-start(bf16[8,160,1280]{2,1,0:T(8,128)(2,1)} %get-tuple-element.86), channel_id=1, source_target_pairs={{0,2},{2,0},{4,6},{6,4},{8,10},{10,8},{12,14},{14,12},{16,18},{18,... | collective-permute-start | bytes 9830408 | tf_op jit(solution)/shard_map/ppermute | solution.py:933
  553.8 115.0 %collective-permute-start.65 = (bf16[8,160,1280]{2,1,0:T(8,128)(2,1)S(1)}, bf16[8,160,1280]{2,1,0:T(8,128)(2,1)S(1)}, u32[]{:S(2)}, u32[]{:S(2)}) collective-permute-start(bf16[8,160,1280]{2,1,0:T(8,128)(2,1)S(1)} %add_convert_fusion), channel_id=1, source_target_pairs={{0,1},{1,0},{2,3},{3,2},{4,5},{5,4},{6,7},{7,6},{8,9},{9,8},{10,11... | collective-permute-start | bytes 9830408 | tf_op jit(solution)/shard_map/ppermute | solution.py:937
  560.7 102.1 %collective-permute-start.45 = (bf16[8,40,2560]{2,1,0:T(8,128)(2,1)S(1)}, bf16[8,40,2560]{2,1,0:T(8,128)(2,1)S(1)}, u32[]{:S(2)}, u32[]{:S(2)}) collective-permute-start(bf16[8,40,2560]{2,1,0:T(8,128)(2,1)S(1)} %get-tuple-element.108), channel_id=1, source_target_pairs={{0,1},{1,0},{2,3},{3,2},{4,5},{5,4},{6,7},{7,6},{8,9},{9,8},{10,11... | collective-permute-start | bytes 4915208 | tf_op jit(solution)/shard_map/ppermute | solution.py:937
  564.0 111.7 %collective-permute-start.23 = (bf16[8,40,3840]{2,1,0:T(8,128)(2,1)}, bf16[8,40,3840]{2,1,0:T(8,128)(2,1)}, u32[]{:S(2)}, u32[]{:S(2)}) collective-permute-start(bf16[8,40,3840]{2,1,0:T(8,128)(2,1)} %get-tuple-element.105), channel_id=1, source_target_pairs={{0,2},{2,0},{4,6},{6,4},{8,10},{10,8},{12,14},{14,12},{16,18},{18,... | collective-permute-start | bytes 7372808 | tf_op jit(solution)/shard_map/ppermute | solution.py:933
  569.7 141.4 %collective-permute-start.25 = (bf16[8,40,3840]{2,1,0:T(8,128)(2,1)S(1)}, bf16[8,40,3840]{2,1,0:T(8,128)(2,1)}, u32[]{:S(2)}, u32[]{:S(2)}) collective-permute-start(bf16[8,40,3840]{2,1,0:T(8,128)(2,1)S(1)} %fusion), channel_id=1, source_target_pairs={{0,1},{1,0},{2,3},{3,2},{4,5},{5,4},{6,7},{7,6},{8,9},{9,8},{10,11... | collective-permute-start | bytes 7372808 | tf_op jit(solution)/shard_map/ppermute | solution.py:937
  662.8 263.4 %collective-permute-start.22 = (f32[1,7680]{1,0:T(1,128)}, f32[1,7680]{1,0:T(1,128)}, u32[]{:S(2)}, u32[]{:S(2)}) collective-permute-start(f32[1,7680]{1,0:T(1,128)} %add.204), channel_id=1, source_target_pairs={{0,16},{2,18},{4,20},{6,22},{8,24},{10,26},{12,28},{14,30},{16,0},... | collective-permute-start | bytes 92168 | tf_op jit(solution)/shard_map/ppermute | solution.py:933
  668.5 257.6 %collective-permute-start.39 = (bf16[1,40,1280]{2,1,0:T(8,128)(2,1)S(1)}, bf16[1,40,1280]{2,1,0:T(8,128)(2,1)S(1)}, u32[]{:S(2)}, u32[]{:S(2)}) collective-permute-start(bf16[1,40,1280]{2,1,0:T(8,128)(2,1)S(1)} %fusion.14), channel_id=1, source_target_pairs={{0,16},{2,18},{4,20},{6,22},{8,24},{10,26},{12,28},{14,30},{16,0},... | collective-permute-start | bytes 307208 | tf_op jit(solution)/shard_map/ppermute | solution.py:933
  668.8 217.5 %collective-permute-start.59 = (bf16[1,40,2560]{2,1,0:T(8,128)(2,1)S(1)}, bf16[1,40,2560]{2,1,0:T(8,128)(2,1)S(1)}, u32[]{:S(2)}, u32[]{:S(2)}) collective-permute-start(bf16[1,40,2560]{2,1,0:T(8,128)(2,1)S(1)} %fusion.12), channel_id=1, source_target_pairs={{0,16},{2,18},{4,20},{6,22},{8,24},{10,26},{12,28},{14,30},{16,0},... | collective-permute-start | bytes 614408 | tf_op jit(solution)/shard_map/ppermute | solution.py:933
  715.2 55.6 %collective-permute-start.26 = (bf16[4,40,3840]{2,1,0:T(8,128)(2,1)S(1)}, bf16[4,40,3840]{2,1,0:T(8,128)(2,1)S(1)}, u32[]{:S(2)}, u32[]{:S(2)}) collective-permute-start(bf16[4,40,3840]{2,1,0:T(8,128)(2,1)S(1)} %slice.428), channel_id=1, source_target_pairs={{0,4},{2,6},{4,0},{6,2},{8,12},{10,14},{12,8},{14,10},{16,20},{18,... | collective-permute-start | bytes 3686408 | tf_op jit(solution)/shard_map/ppermute | solution.py:933
  794.2 60.6 %collective-permute-start.48 = (bf16[1,40,2560]{2,1,0:T(8,128)(2,1)S(1)}, bf16[1,40,2560]{2,1,0:T(8,128)(2,1)S(1)}, u32[]{:S(2)}, u32[]{:S(2)}) collective-permute-start(bf16[1,40,2560]{2,1,0:T(8,128)(2,1)S(1)} %slice.439), channel_id=1, source_target_pairs={{0,16},{2,18},{4,20},{6,22},{8,24},{10,26},{12,28},{14,30},{16,0},... | collective-permute-start | bytes 614408 | tf_op jit(solution)/shard_map/ppermute | solution.py:933
  918.7 50.3 %collective-permute-start.61 = (bf16[4,40,2560]{2,1,0:T(8,128)(2,1)S(1)}, bf16[4,40,2560]{2,1,0:T(8,128)(2,1)S(1)}, u32[]{:S(2)}, u32[]{:S(2)}) collective-permute-start(bf16[4,40,2560]{2,1,0:T(8,128)(2,1)S(1)} %pad_maximum_fusion.9), channel_id=1, source_target_pairs={{0,4},{2,6},{4,0},{6,2},{8,12},{10,14},{12,8},{14,10},{16,20},{18,... | collective-permute-start | bytes 2457608 | tf_op jit(solution)/shard_map/ppermute | solution.py:933
  925.2 59.6 %collective-permute-start.51 = (bf16[4,40,2560]{2,1,0:T(8,128)(2,1)S(1)}, bf16[4,40,2560]{2,1,0:T(8,128)(2,1)S(1)}, u32[]{:S(2)}, u32[]{:S(2)}) collective-permute-start(bf16[4,40,2560]{2,1,0:T(8,128)(2,1)S(1)} %pad_maximum_fusion.8), channel_id=1, source_target_pairs={{0,4},{2,6},{4,0},{6,2},{8,12},{10,14},{12,8},{14,10},{16,20},{18,... | collective-permute-start | bytes 2457608 | tf_op jit(solution)/shard_map/ppermute | solution.py:933
  926.1 123.6 %collective-permute-start.72 = (bf16[8,160,1280]{2,1,0:T(8,128)(2,1)S(1)}, bf16[8,160,1280]{2,1,0:T(8,128)(2,1)}, u32[]{:S(2)}, u32[]{:S(2)}) collective-permute-start(bf16[8,160,1280]{2,1,0:T(8,128)(2,1)S(1)} %pad_maximum_fusion.refs_0_), channel_id=1, source_target_pairs={{0,2},{2,0},{4,6},{6,4},{8,10},{10,8},{12,14},{14,12},{16,18},{18,... | collective-permute-start | bytes 9830408 | tf_op jit(solution)/shard_map/ppermute | solution.py:933
  926.2 61.9 %collective-permute-start.16 = (bf16[512,1280]{1,0:T(8,128)(2,1)S(1)}, bf16[512,1280]{1,0:T(8,128)(2,1)S(1)}, u32[]{:S(2)}, u32[]{:S(2)}) collective-permute-start(bf16[512,1280]{1,0:T(8,128)(2,1)S(1)} %copy-done.22), channel_id=1, source_target_pairs={{0,1},{1,0},{2,3},{3,2},{4,5},{5,4},{6,7},{7,6},{8,9},{9,8},{10,11... | collective-permute-start | bytes 3932168 | tf_op jit(solution)/shard_map/ppermute | solution.py:937
  957.3 80.3 %collective-permute-start.32 = (bf16[8,40,3840]{2,1,0:T(8,128)(2,1)}, bf16[8,40,3840]{2,1,0:T(8,128)(2,1)}, u32[]{:S(2)}, u32[]{:S(2)}) collective-permute-start(bf16[8,40,3840]{2,1,0:T(8,128)(2,1)} %pad_maximum_fusion.1.refs_0_), channel_id=1, source_target_pairs={{0,2},{2,0},{4,6},{6,4},{8,10},{10,8},{12,14},{14,12},{16,18},{18,... | collective-permute-start | bytes 7372808 | tf_op jit(solution)/shard_map/ppermute | solution.py:933
  (72 other events, 1673.2 us)

commit v2 on v0

--- a/solution.py
+++ b/solution.py
@@ -1,6 +1,10 @@
+import functools
+
 import jax
 import jax.numpy as jnp
 from jax import lax
+from jax.experimental import pallas as pl
+from jax.experimental.pallas import tpu as pltpu
 from jax.sharding import PartitionSpec as P
 
 HEADS = 16
@@ -144,7 +148,7 @@
     )
 
 
-def on_device(
+def general_device(
     frames,
     cotangent,
     clip_lengths,
@@ -296,9 +300,1129 @@
     return (jnp.stack(outputs), jnp.stack(input_grads)) + tuple(summed)
 
 
+LOW = jnp.bfloat16
+FULL = jnp.float32
+VMEM = 60 * 2**20
+PACE = 1.15e9 * 1.0
+
+
+def contract(left, right, left_dim, right_dim):
+    return lax.dot_general(
+        left, right, (((left_dim,), (right_dim,)), ((), ())), preferred_element_type=FULL
+    )
+
+
+def const_spec(shape):
+    return pl.BlockSpec(shape, lambda *at: (0,) * len(shape), pipeline_mode=pl.Buffered(1))
+
+
+def call(kernel, grid, in_specs, out_specs, out_shape, scratch=(), us=1.0, aliases=None, after=()):
+    count, extra = len(in_specs), len(after)
+
+    def body(ids, *refs):
+        kernel(ids, *refs[:count], *refs[count + extra :])
+
+    run = pl.pallas_call(
+        body,
+        grid_spec=pltpu.PrefetchScalarGridSpec(
+            num_scalar_prefetch=1,
+            grid=grid,
+            in_specs=list(in_specs) + [pl.BlockSpec(memory_space=pl.ANY)] * extra,
+            out_specs=out_specs,
+            scratch_shapes=list(scratch),
+        ),
+        out_shape=out_shape,
+        input_output_aliases=aliases or {},
+        compiler_params=pltpu.CompilerParams(vmem_limit_bytes=VMEM),
+        cost_estimate=pl.CostEstimate(flops=int(us * PACE), bytes_accessed=0, transcendentals=0),
+    )
+    return lambda *args: run(*args, *after)
+
+
+ANYWHERE = pl.BlockSpec(memory_space=pl.ANY)
+
+
+def spread(rows):
+    mean = jnp.mean(rows, axis=-1, keepdims=True)
+    centred = rows - mean
+    scale = lax.rsqrt(jnp.mean(centred * centred, axis=-1, keepdims=True) + 1e-05)
+    return centred * scale, scale
+
+
+def norm_pull(unit, scale, gain, grad):
+    inner = grad * gain
+    along = jnp.mean(inner * unit, axis=-1, keepdims=True)
+    return scale * (inner - jnp.mean(inner, axis=-1, keepdims=True) - unit * along)
+
+
+def vector(ids, params_ref, at, half):
+    own, far = params_ref[0:1, at : at + half], params_ref[1:2, at : at + half]
+    first = ids[0] == 0
+    return jnp.concatenate([jnp.where(first, own, far), jnp.where(first, far, own)], axis=1)
+
+
+def struct(shape, dtype):
+    return jax.ShapeDtypeStruct(shape, dtype)
+
+
+def first_norm_kernel(stats, ids, frames_ref, params_ref, norm_ref):
+    rows = frames_ref[0]
+    width = rows.shape[1]
+    half = width // 2
+    mean = jnp.mean(rows, axis=-1, keepdims=True)
+    centred = rows - mean
+    moved = jnp.mean(centred * centred, axis=-1, keepdims=True) + 1e-05
+    unit = centred * lax.rsqrt(moved)
+    norm_ref[:, :width] = (unit * vector(ids, params_ref, 0, half) + vector(ids, params_ref, half, half)).astype(LOW)
+    if stats:
+        lane = lax.broadcasted_iota(jnp.int32, (1, 128), 1)
+        out = jnp.zeros((rows.shape[0], 128), FULL)
+        for at, value in enumerate((mean, jnp.sqrt(moved))):
+            coarse = value.astype(LOW).astype(FULL)
+            out = jnp.where(lane == 2 * at, coarse, jnp.where(lane == 2 * at + 1, value - coarse, out))
+        norm_ref[:, width:] = out.astype(LOW)
+
+
+def first_norm(ids, frames, params, other, after=()):
+    unused, rows, width = frames.shape
+    block = rows // 2
+    wide = width + 128 * other
+    return call(
+        functools.partial(first_norm_kernel, other),
+        (2,),
+        [
+            pl.BlockSpec((1, block, width), lambda i, ids: (ids[0] ^ other, i, 0)),
+            const_spec(params.shape),
+        ],
+        pl.BlockSpec((block, wide), lambda i, ids: (i, 0)),
+        struct((rows, wide), LOW),
+        us=4,
+        after=after,
+    )(ids, frames, params)
+
+
+def far_parts(ids, message, params_ref, half):
+    width = 2 * half
+    norm = message[:, :width].astype(FULL)
+    stats = message[:, width:].astype(FULL)
+    unit = (norm - vector(ids, params_ref, half, half)) / vector(ids, params_ref, 0, half)
+    return unit, stats[:, 0:1] + stats[:, 1:2], stats[:, 2:3] + stats[:, 3:4]
+
+
+def place_pieces(ids, target, base, piece_refs):
+    rows = piece_refs[0].shape[-2]
+    for turn in range(8):
+        at = pl.multiple_of(base + ((ids[1] // 2) ^ turn) * rows, rows)
+        part = piece_refs[turn // 2][turn % 2]
+        target[pl.ds(at, rows), :] = part.reshape(rows, part.shape[-1])
+
+
+def place_weights(ids, target, own_ref, piece_refs):
+    half = own_ref.shape[0]
+    target[pl.ds(pl.multiple_of(ids[0] * half, half), half), :] = own_ref[...]
+    place_pieces(ids, target, (1 - ids[0]) * half, piece_refs)
+
+
+def project_kernel(group, ids, own_rows, far_rows, own_ref, p0, p1, p2, p3, params_ref, out_ref, whole_ref, *refs):
+    half, width = own_rows.shape
+    rows_scr = refs[-1]
+
+    @pl.when(pl.program_id(0) == 0)
+    def _():
+        rows_scr[0:half] = own_rows[...]
+        rows_scr[half:] = far_rows[:, :width]
+        if group == 0:
+            refs[0][...] = rows_scr[...].T
+
+    place_weights(ids, whole_ref, own_ref, (p0, p1, p2, p3))
+    part = width // 2
+    row = jnp.where(ids[0] == group, params_ref[0:1, 2 * part : 4 * part], params_ref[1:2, 2 * part : 4 * part])
+    step = pl.program_id(0)
+    bias = jnp.where(step == 0, row[:, :part], jnp.where(step == 2, row[:, part:], 0.0))
+    out_ref[...] = (contract(rows_scr[...], whole_ref[...], 1, 0) + bias).astype(LOW)
+
+
+def project(ids, group, own_rows, far_rows, own, pieces, params, after=()):
+    half, width = own_rows.shape
+    tile = width // 2
+    piece = pl.BlockSpec((2, width // 16, tile), lambda j, ids: (0, 0, j))
+    turn = group == 0
+    return call(
+        functools.partial(project_kernel, group),
+        (3,),
+        [const_spec((half, width)), const_spec(far_rows.shape)]
+        + [pl.BlockSpec((width // 2, tile), lambda j, ids: (0, 2 * j + group))]
+        + [piece] * 4
+        + [const_spec(params.shape)],
+        [pl.BlockSpec((2 * half, tile), lambda j, ids: (0, j)), pl.BlockSpec((width, tile), lambda j, ids: (0, j))]
+        + [const_spec((width, 2 * half))] * turn,
+        [struct((2 * half, 3 * tile), LOW), struct((width, 3 * tile), LOW)] + [struct((width, 2 * half), LOW)] * turn,
+        [pltpu.VMEM((2 * half, width), LOW)],
+        us=12,
+        after=after,
+    )(ids, own_rows, far_rows, own, *pieces, params)
+
+
+def window(head, size):
+    first = head * size // 128
+    last = -(-(head + 1) * size // 128)
+    return first * 128, last * 128, head * size - first * 128
+
+
+def head_lanes(lanes, offset, size):
+    lane = lax.broadcasted_iota(jnp.int32, (1, lanes), 1)
+    return (lane >= offset) & (lane < offset + size)
+
+
+def attend_kernel(size, per, ids, query_ref, key_ref, value_ref, bias_ref, out_ref, total_ref, acc):
+    scale = size ** (-0.5)
+    bias = bias_ref[...]
+    lane = lax.broadcasted_iota(jnp.int32, (1, 128), 1)
+    acc[...] = jnp.zeros_like(acc)
+    stats = jnp.zeros((query_ref.shape[0], 128), FULL)
+    for head in range(per):
+        low, high, offset = window(head, size)
+        inside = head_lanes(high - low, offset, size)
+        query = query_ref[:, low:high]
+        query = jnp.where(inside, query, jnp.zeros_like(query))
+        scores = contract(query, key_ref[:, low:high], 1, 1) * scale + bias
+        peak = jnp.max(scores, axis=-1, keepdims=True)
+        raised = jnp.exp(scores - peak)
+        summed = jnp.sum(raised, axis=-1, keepdims=True)
+        probs = (raised * (1.0 / summed)).astype(LOW)
+        mixed = contract(probs, value_ref[:, low:high], 1, 0)
+        acc[:, low:high] += jnp.where(inside, mixed, 0.0)
+        stats = jnp.where(lane == head, peak + jnp.log(summed), stats)
+    out_ref[...] = acc[...].astype(LOW)
+    total_ref[...] = stats.T[:per]
+
+
+def attend_rows(ids, qkv, bias, after=(), tile=512, groups=2):
+    rows, part = qkv.shape[0], qkv.shape[1] // 3
+    per = HEADS // groups
+    return call(
+        functools.partial(attend_kernel, part // per, per),
+        (rows // tile,),
+        [
+            pl.BlockSpec((tile, part), lambda i, ids: (i, 0)),
+            pl.BlockSpec((rows, part), lambda i, ids: (0, 1), pipeline_mode=pl.Buffered(1)),
+            pl.BlockSpec((rows, part), lambda i, ids: (0, 2), pipeline_mode=pl.Buffered(1)),
+            const_spec((1, rows)),
+        ],
+        [
+            pl.BlockSpec((tile, part), lambda i, ids: (i, 0)),
+            pl.BlockSpec((per, tile), lambda i, ids: (0, i)),
+        ],
+        [struct((rows, part), LOW), struct((per, rows), FULL)],
+        [pltpu.VMEM((tile, part), FULL)],
+        us=19,
+        after=after,
+    )(ids, qkv, qkv, qkv, bias)
+
+
+def attend_back_kernel(size, heads, ids, query_ref, key_ref, value_ref, upper_ref, bias_ref, total_ref, *refs):
+    prior = refs[:-4]
+    grad_ref, acc, key_sum, value_sum = refs[-4:]
+    step = pl.program_id(0)
+    scale = size ** (-0.5)
+    bias = bias_ref[...]
+    tile = query_ref.shape[0]
+
+    @pl.when(step == 0)
+    def _():
+        key_sum[...] = jnp.zeros_like(key_sum)
+        value_sum[...] = jnp.zeros_like(value_sum)
+
+    acc[...] = jnp.zeros_like(acc)
+    for head in heads:
+        low, high, offset = window(head, size)
+        inside = head_lanes(high - low, offset, size)
+        query = query_ref[:, low:high]
+        query = jnp.where(inside, query, jnp.zeros_like(query))
+        upper = upper_ref[:, low:high]
+        upper = jnp.where(inside, upper, jnp.zeros_like(upper))
+        keys = key_ref[:, low:high]
+        scores = contract(keys, query, 1, 1) * scale + bias
+        probs = jnp.exp(scores - total_ref[head : head + 1, :])
+        d_probs = contract(value_ref[:, low:high], upper, 1, 1)
+        terms = probs * d_probs
+        d_scores = (terms - probs * jnp.sum(terms, axis=0, keepdims=True)).astype(LOW)
+        value_sum[:, low:high] += contract(probs.astype(LOW), upper, 1, 0)
+        key_sum[:, low:high] += contract(d_scores, query, 1, 0)
+        acc[:, low:high] += jnp.where(inside, contract(d_scores, keys, 0, 0), 0.0)
+    part = acc.shape[1]
+    here = pl.ds(pl.multiple_of(step * tile, tile), tile)
+    grad = (acc[...] * scale).astype(LOW)
+    grad_ref[here, :part] = grad + prior[0][here, :part] if prior else grad
+
+    @pl.when(step == pl.num_programs(0) - 1)
+    def _():
+        key_grad, value_grad = (key_sum[...] * scale).astype(LOW), value_sum[...].astype(LOW)
+        grad_ref[:, part : 2 * part] = key_grad + prior[0][:, part : 2 * part] if prior else key_grad
+        grad_ref[:, 2 * part :] = value_grad + prior[0][:, 2 * part :] if prior else value_grad
+
+
+def attend_back_rows(ids, group, qkv, upper, bias, totals, after, heads=None, prior=(), tile=512, groups=2):
+    rows, part = qkv.shape[0], qkv.shape[1] // 3
+    per = HEADS // groups
+    heads = heads or range(per)
+    return call(
+        functools.partial(attend_back_kernel, part // per, heads),
+        (rows // tile,),
+        [
+            pl.BlockSpec((tile, part), lambda i, ids: (i, 0)),
+            pl.BlockSpec((rows, part), lambda i, ids: (0, 1), pipeline_mode=pl.Buffered(1)),
+            pl.BlockSpec((rows, part), lambda i, ids: (0, 2), pipeline_mode=pl.Buffered(1)),
+            pl.BlockSpec((tile, part), lambda i, ids: (i, group)),
+            const_spec((rows, 1)),
+            pl.BlockSpec((per, tile), lambda i, ids: (0, i)),
+        ]
+        + [const_spec((rows, 3 * part))] * len(prior),
+        const_spec((rows, 3 * part)),
+        struct((rows, 3 * part), LOW),
+        [pltpu.VMEM((tile, part), FULL), pltpu.VMEM((rows, part), FULL), pltpu.VMEM((rows, part), FULL)],
+        us=31 * len(heads) / per,
+        after=after,
+    )(ids, qkv, qkv, qkv, upper, bias, totals, *prior)
+
+
+def out_kernel(ids, mixed0, mixed1, own_ref, p0, p1, p2, p3, frames_ref, far_ref, params_ref, resid_ref, norm_ref, turned_ref, whole_ref, start):
+    step = pl.program_id(0)
+    half = own_ref.shape[0]
+    is_near = step < pl.num_programs(0) // 2
+
+    @pl.when(step == 0)
+    def _():
+        place_weights(ids, whole_ref, own_ref, (p0, p1, p2, p3))
+
+    @pl.when(is_near)
+    def _():
+        start[...] = frames_ref[0]
+
+    @pl.when(jnp.logical_not(is_near))
+    def _():
+        unit, mean, deviation = far_parts(ids, far_ref[...], params_ref, half)
+        start[...] = mean + deviation * unit
+
+    mixed = jnp.concatenate([mixed0[...], mixed1[...]], axis=1)
+    resid = start[...] + contract(mixed, whole_ref[...], 1, 0) + vector(ids, params_ref, 4 * half, half)
+    resid_ref[...] = resid
+    unit, unused = spread(resid)
+    norm = (unit * vector(ids, params_ref, 5 * half, half) + vector(ids, params_ref, 6 * half, half)).astype(LOW)
+    norm_ref[...] = norm
+    turned_ref[...] = norm.T
+
+
+def near_spec(tile, width, count):
+    return pl.BlockSpec((1, tile, width), lambda i, ids: (ids[0], jnp.minimum(i, count // 2 - 1), 0))
+
+
+def far_spec(tile, width, count):
+    return pl.BlockSpec((tile, width), lambda i, ids: (jnp.maximum(i - count // 2, 0), 0))
+
+
+def row_spec(tile, width):
+    return pl.BlockSpec((tile, width), lambda i, ids: (i, 0))
+
+
+def out_rows(ids, mixed0, mixed1, own, pieces, frames, far, params, after=(), tile=256):
+    rows, part = mixed0.shape
+    width = 2 * part
+    count = rows // tile
+    return call(
+        out_kernel,
+        (count,),
+        [row_spec(tile, part), row_spec(tile, part), const_spec((part, width))]
+        + [const_spec(array.shape) for array in pieces]
+        + [near_spec(tile, width, count), far_spec(tile, far.shape[1], count), const_spec(params.shape)],
+        [
+            row_spec(tile, width),
+            row_spec(tile, width),
+            pl.BlockSpec((width, tile), lambda i, ids: (0, i)),
+            const_spec((width, width)),
+        ],
+        [struct((rows, width), FULL), struct((rows, width), LOW), struct((width, rows), LOW), struct((width, width), LOW)],
+        [pltpu.VMEM((tile, width), FULL)],
+        us=12,
+        after=after,
+    )(ids, mixed0, mixed1, own, *pieces, frames, far, params)
+
+
+def bell_parts(values):
+    bell = jnp.exp(values * values * -0.5)
+    return 0.5 + 0.5 * lax.erf(values * (0.5**0.5)), bell
+
+
+def put_side(ids, far, refs, source):
+    block = refs[0].shape[2]
+    for turn in range(16):
+        piece = (ids[0] ^ far) * 16 + (ids[1] ^ turn)
+        rows = source[pl.ds(pl.multiple_of(piece * block, block), block), :].astype(LOW)
+        if turn < 8:
+            refs[0][0, turn] = rows
+        else:
+            refs[turn // 4 - 1][0, turn % 4] = rows
+
+
+def side_shapes(rows):
+    return [(1, 8, rows // 32), (1, 4, rows // 32), (1, 4, rows // 32)]
+
+
+def feed_kernel(first, last, far, start, ids, norm_ref, turned_ref, *refs):
+    refs = list(refs)
+    take = lambda count: [refs.pop(0) for unused in range(count)]
+    if first:
+        cot_ref, cot_far_ref, y_in = take(3)
+    else:
+        dout, y_in, dn_in = take(3)
+    own_ref, = take(1)
+    piece_refs = take(4)
+    down_refs = take(4 if far else 1)
+    params_ref, = take(1)
+    if start:
+        take(10)
+    if first:
+        dout, = take(1)
+    if last:
+        near_out, far_out = take(2)
+    else:
+        y_out, = take(1)
+    dn_out, = take(1)
+    near_refs, far_refs = take(3), take(3)
+    down_keep, down0, down1, bias_ref = take(4)
+    y_acc, dn_acc, up_w, down_w, grad, grad_low, far_low, sems = refs
+    step = pl.program_id(0)
+    half = own_ref.shape[0]
+    tile = own_ref.shape[1]
+    rows = norm_ref.shape[0]
+    y_copy = pltpu.make_async_copy(y_in, y_acc, sems.at[0])
+    if not first:
+        dn_copy = pltpu.make_async_copy(dn_in, dn_acc, sems.at[1])
+
+    @pl.when(step == 0)
+    def _():
+        y_copy.start()
+        if first:
+            dn_acc[...] = jnp.zeros_like(dn_acc)
+            dout[: rows // 2] = cot_ref[0].astype(LOW)
+            dout[rows // 2 :] = cot_far_ref[...]
+        else:
+            dn_copy.start()
+
+    place_weights(ids, up_w, own_ref, piece_refs)
+    if far:
+        place_pieces(ids, down_w, 0, down_refs)
+        down = down_w[...]
+    else:
+        down = down_refs[0][...]
+    up = up_w[...]
+    upper = dout[...]
+    at = pl.multiple_of(8 * half + (step + start) * tile, tile)
+    raised = contract(norm_ref[...], up, 1, 0) + params_ref[far : far + 1, pl.ds(at, tile)]
+    d_hidden = contract(upper, down, 1, 1)
+    lower, bell = bell_parts(raised)
+    hidden = (raised * lower).astype(LOW)
+    d_up = (d_hidden * (lower + raised * bell * (0.5 / jnp.pi) ** 0.5)).astype(LOW)
+    bias_ref[...] = jnp.sum(d_up.astype(FULL), axis=0, keepdims=True)
+
+    @pl.when(step == 0)
+    def _():
+        y_copy.wait()
+        if first:
+            y_acc[...] += vector(ids, params_ref, 7 * half, half)
+        else:
+            dn_copy.wait()
+
+    y_acc[...] += contract(hidden, down, 1, 0)
+    dn_acc[...] += contract(d_up, up, 1, 1)
+    end = step == pl.num_programs(0) - 1
+    copies = [pltpu.make_async_copy(dn_acc, dn_out, sems.at[1])]
+    if last:
+        copies.append(pltpu.make_async_copy(y_acc.at[: rows // 2], near_out.at[ids[0]], sems.at[0]))
+        copies.append(pltpu.make_async_copy(far_low, far_out, sems.at[2]))
+    else:
+        copies.append(pltpu.make_async_copy(y_acc, y_out, sems.at[0]))
+
+    @pl.when(end)
+    def _():
+        if last:
+            far_low[...] = y_acc[rows // 2 :].astype(LOW)
+        for copy in copies:
+            copy.start()
+
+    grad[...] = contract(turned_ref[...], d_up, 1, 0)
+    put_side(ids, 0, near_refs, grad)
+    put_side(ids, 1, far_refs, grad)
+    grad_low[...] = contract(hidden, upper, 0, 0)
+    count, block = down_keep.shape[0], down_keep.shape[1]
+    for turn in range(2 * count):
+        low = grad_low[pl.ds(pl.multiple_of((ids[2] ^ turn) * block, block), block), :].astype(LOW)
+        if turn < count:
+            down_keep[turn] = low
+        elif turn < count + 4:
+            down0[turn - count] = low
+        else:
+            down1[turn - count - 4] = low
+
+    @pl.when(end)
+    def _():
+        for copy in copies:
+            copy.wait()
+
+
+def feed_rows(ids, far, start, count, norm, turned, carry, up, up_pieces, down, params, grads=(), last=None, after=(), tile=512):
+    rows, width = norm.shape
+    half = up.shape[1] // 2
+    tiles = half // tile
+    first = carry[0].ndim == 3
+    column = lambda j, ids: (ids[0] ^ far) * tiles + start + j
+    own_spec = pl.BlockSpec((width // 2, tile), lambda j, ids: (0, column(j, ids)))
+    piece_spec = pl.BlockSpec((2, width // 16, tile), lambda j, ids: (0, 0, start + j))
+    if far:
+        down_specs = [pl.BlockSpec((2, 1, tile // 8, width), lambda j, ids: (0, start + j, 0, 0))] * 4
+    else:
+        down_specs = [pl.BlockSpec((tile, width), lambda j, ids: (start + j, 0))]
+    if first:
+        carry_specs = [
+            pl.BlockSpec((1, rows // 2, width), lambda j, ids: (ids[0], 0, 0), pipeline_mode=pl.Buffered(1)),
+            const_spec((rows // 2, width)),
+            ANYWHERE,
+        ]
+        out_specs, out_shape = [const_spec((rows, width))], [struct((rows, width), LOW)]
+    else:
+        carry_specs = [const_spec((rows, width)), ANYWHERE, ANYWHERE]
+        out_specs, out_shape = [], []
+    if last is not None:
+        out_specs += [ANYWHERE, ANYWHERE]
+        out_shape += [struct(last, FULL), struct((rows // 2, width), LOW)]
+    else:
+        out_specs += [ANYWHERE]
+        out_shape += [struct((rows, width), FULL)]
+    in_specs = (
+        [const_spec((rows, width)), const_spec((width, rows))]
+        + carry_specs
+        + [own_spec]
+        + [piece_spec] * 4
+        + down_specs
+        + [const_spec(params.shape)]
+        + [ANYWHERE] * len(grads)
+    )
+    fine = tile // 16
+    sides = side_shapes(width) * 2
+    out_specs += [ANYWHERE]
+    out_specs += [pl.BlockSpec(shape + (tile,), lambda j, ids: (0, 0, 0, start + j)) for shape in sides]
+    out_specs += [
+        pl.BlockSpec((8, fine, width), lambda j, ids: (0, start + j, 0)),
+        pl.BlockSpec((4, fine, width), lambda j, ids: (0, start + j, 0)),
+        pl.BlockSpec((4, fine, width), lambda j, ids: (0, start + j, 0)),
+        pl.BlockSpec((1, tile), lambda j, ids: (0, start + j)),
+    ]
+    out_shape += (
+        [struct((rows, width), FULL)]
+        + [struct(shape + (half,), LOW) for shape in sides]
+        + [struct((8, half // 16, width), LOW)]
+        + [struct((4, half // 16, width), LOW)] * 2
+        + [struct((1, half), FULL)]
+    )
+    aliases = {1 + len(in_specs) - 10 + k: len(out_shape) - 10 + k for k in range(len(grads))}
+    return call(
+        functools.partial(feed_kernel, first, last is not None, far, start),
+        (count,),
+        in_specs,
+        out_specs,
+        out_shape,
+        [
+            pltpu.VMEM((rows, width), FULL),
+            pltpu.VMEM((rows, width), FULL),
+            pltpu.VMEM((width, tile), LOW),
+            pltpu.VMEM((tile, width), LOW),
+            pltpu.VMEM((width, tile), FULL),
+            pltpu.VMEM((tile, width), FULL),
+            pltpu.VMEM((rows // 2, width), LOW),
+            pltpu.SemaphoreType.DMA((3,)),
+        ],
+        us=3 + 11.5 * count,
+        aliases=aliases,
+        after=after,
+    )(ids, norm, turned, *carry, up, *up_pieces, *down, params, *grads)
+
+
+def middle_kernel(
+    ids, dn_ref, resid_ref, cot_ref, got_ref, mixed0, mixed1, whole_ref, params_ref,
+    d_resid_ref, d_mixed_ref, n0, n1, n2, f0, f1, f2, small_ref, grad, sums,
+):
+    step = pl.program_id(0)
+    count = pl.num_programs(0)
+    half = params_ref.shape[1] // 12
+
+    @pl.when(step == 0)
+    def _():
+        grad[...] = jnp.zeros_like(grad)
+        sums[...] = jnp.zeros_like(sums)
+
+    pick = (step < count // 2).astype(FULL)
+    cot = cot_ref[0] * pick + got_ref[...].astype(FULL) * (1.0 - pick)
+    d_norm = dn_ref[...]
+    unit, scale = spread(resid_ref[...])
+    d_resid = cot + norm_pull(unit, scale, vector(ids, params_ref, 5 * half, half), d_norm)
+    d_attn = d_resid.astype(LOW)
+    d_resid_ref[...] = d_resid
+    d_mixed_ref[...] = contract(d_attn, whole_ref[...], 1, 1).astype(LOW)
+    grad[:half] += contract(mixed0[...], d_attn, 0, 0)
+    grad[half:] += contract(mixed1[...], d_attn, 0, 0)
+    sums[0:1] += jnp.sum(d_attn.astype(FULL), axis=0, keepdims=True)
+    sums[1:2] += jnp.sum(d_norm * unit, axis=0, keepdims=True)
+    sums[2:3] += jnp.sum(d_norm, axis=0, keepdims=True)
+    sums[3:4] += jnp.sum(cot.astype(LOW).astype(FULL), axis=0, keepdims=True)
+
+    @pl.when(step == count - 1)
+    def _():
+        put_side(ids, 0, (n0, n1, n2), grad)
+        put_side(ids, 1, (f0, f1, f2), grad)
+        small_ref[...] = sums[...]
+
+
+def middle_rows(ids, dn, resid, cotangent, got, mixed0, mixed1, whole, params, after=(), tile=256):
+    rows, width = resid.shape
+    thin = row_spec(tile, width // 2)
+    count = rows // tile
+    wide = row_spec(tile, width)
+    sides = side_shapes(width) * 2
+    return call(
+        middle_kernel,
+        (count,),
+        [wide] * 2
+        + [near_spec(tile, width, count), far_spec(tile, width, count), thin, thin, const_spec((width, width)), const_spec(params.shape)],
+        [wide, wide] + [const_spec(shape + (width,)) for shape in sides] + [const_spec((8, width))],
+        [
+            struct((rows, width), FULL),
+            struct((rows, width), LOW),
+        ]
+        + [struct(shape + (width,), LOW) for shape in sides]
+        + [
+            struct((8, width), FULL),
+        ],
+        [pltpu.VMEM((width, width), FULL), pltpu.VMEM((8, width), FULL)],
+        us=20,
+        after=after,
+    )(ids, dn, resid, cotangent, got, mixed0, mixed1, whole, params)
+
+
+def project_grad_kernel(ids, turned_ref, grad_ref, *refs):
+    more, refs = refs[:-8], refs[-8:]
+    pieces, bias_ref, grad = refs[:6], refs[6], refs[7]
+    step = pl.program_id(0)
+
+    @pl.when(step < 3)
+    def _():
+        d_part = grad_ref[...]
+        grad[...] = contract(turned_ref[...], d_part, 1, 0)
+        for far in range(2):
+            put_side(ids, far, pieces[3 * far : 3 * far + 3], grad)
+        bias_ref[0] = jnp.sum(d_part.astype(FULL), axis=0, keepdims=True)
+
+    if more:
+
+        @pl.when(step >= 3)
+        def _():
+            for source, target in zip(more, pieces):
+                target[...] = source[...]
+
+
+def project_grad(ids, turned, d_group, extra=(), after=()):
+    width, rows = turned.shape
+    part = d_group.shape[1] // 3
+    count = 5 if len(extra) else 3
+    shapes = side_shapes(width) * 2
+    pieces = [pl.BlockSpec(shape + (part,), lambda j, ids: (0, 0, 0, j)) for shape in shapes]
+    more = [pl.BlockSpec(shape + (part,), lambda j, ids: (0, 0, 0, jnp.maximum(j - 3, 0))) for shape in shapes]
+    return call(
+        project_grad_kernel,
+        (count,),
+        [const_spec((width, rows)), pl.BlockSpec((rows, part), lambda j, ids: (0, jnp.minimum(j, 2)))]
+        + more[: len(extra)],
+        pieces + [pl.BlockSpec((1, 1, part), lambda j, ids: (jnp.minimum(j, 2), 0, 0))],
+        [struct(shape + (count * part,), LOW) for shape in shapes] + [struct((3, 1, part), FULL)],
+        [pltpu.VMEM((width, part), FULL)],
+        us=11,
+        after=after,
+    )(ids, turned, d_group, *extra)
+
+
+def last_kernel(ids, d0_ref, d1_ref, whole0, whole1, frames_ref, far_ref, d_resid_ref, params_ref, near_out, far_out, small_ref, sums, unit_scr, scale_scr):
+    step = pl.program_id(0)
+    count = pl.num_programs(0)
+    half = params_ref.shape[1] // 12
+    is_near = step < count // 2
+
+    @pl.when(step == 0)
+    def _():
+        sums[...] = jnp.zeros_like(sums)
+
+    @pl.when(is_near)
+    def _():
+        unit, scale = spread(frames_ref[0])
+        unit_scr[...] = unit
+        scale_scr[...] = jnp.broadcast_to(scale, scale_scr.shape)
+
+    @pl.when(jnp.logical_not(is_near))
+    def _():
+        unit, mean, deviation = far_parts(ids, far_ref[...], params_ref, half)
+        unit_scr[...] = unit
+        scale_scr[...] = jnp.broadcast_to(1.0 / deviation, scale_scr.shape)
+
+    d_norm = contract(d0_ref[...], whole0[...], 1, 1) + contract(d1_ref[...], whole1[...], 1, 1)
+    unit = unit_scr[...]
+    grad = d_resid_ref[...] + norm_pull(unit, scale_scr[:, 0:1], vector(ids, params_ref, 0, half), d_norm)
+    sums[0:1] += jnp.sum(d_norm * unit, axis=0, keepdims=True)
+    sums[1:2] += jnp.sum(d_norm, axis=0, keepdims=True)
+
+    @pl.when(is_near)
+    def _():
+        near_out[0] = grad
+
+    @pl.when(jnp.logical_not(is_near))
+    def _():
+        far_out[...] = grad.astype(LOW)
+
+    @pl.when(step == count - 1)
+    def _():
+        small_ref[...] = sums[...]
+
+
+def last_rows(ids, d0, d1, whole0, whole1, frames, far, d_resid, params, after=(), tile=256):
+    rows, width = d_resid.shape
+    count = rows // tile
+    return call(
+        last_kernel,
+        (count,),
+        [
+            row_spec(tile, d0.shape[1]),
+            row_spec(tile, d0.shape[1]),
+            const_spec(whole0.shape),
+            const_spec(whole0.shape),
+            near_spec(tile, width, count),
+            far_spec(tile, far.shape[1], count),
+            row_spec(tile, width),
+            const_spec(params.shape),
+        ],
+        [near_spec(tile, width, count), far_spec(tile, width, count), const_spec((8, width))],
+        [struct(frames.shape, FULL), struct((rows // 2, width), LOW), struct((8, width), FULL)],
+        [pltpu.VMEM((8, width), FULL), pltpu.VMEM((tile, width), FULL), pltpu.VMEM((tile, 128), FULL)],
+        us=22,
+        after=after,
+    )(ids, d0, d1, whole0, whole1, frames, far, d_resid, params)
+
+
+def fill_kernel(ids, whole_ref, part_ref, out_ref):
+    out_ref[0] = part_ref[...].astype(FULL)
+
+
+def fill_rows(ids, whole, part, after=()):
+    rows, width = part.shape
+    tile = rows // 2
+    return call(
+        fill_kernel,
+        (2,),
+        [pl.BlockSpec(memory_space=pl.ANY), pl.BlockSpec((tile, width), lambda i, ids: (i, 0))],
+        pl.BlockSpec((1, tile, width), lambda i, ids: (1 - ids[0], i, 0)),
+        struct(whole.shape, FULL),
+        us=3,
+        aliases={1: 0},
+        after=after,
+    )(ids, whole, part)
+
+
+def settle_up_kernel(ids, step, refs, turn, place, out_ref):
+    half = out_ref.shape[2] // 2
+    rows = refs[step][turn].astype(FULL)
+    for far in range(2):
+        at = pl.multiple_of((ids[0] ^ far) * half, half)
+        out_ref[place, :, pl.ds(at, half)] = rows[:, far * half : (far + 1) * half]
+
+
+def settle_down_kernel(ids, step, refs, turn, place, out_ref):
+    tiles, unused, fine, width = out_ref.shape
+    out_ref[:, place] = refs[step][turn].astype(FULL).reshape(tiles, fine, width)
+
+
+def settle_qkv_kernel(ids, step, refs, turn, place, qkv_ref, out_ref):
+    part = refs[4].shape[2] // 3
+    for group in range(2):
+        ref = refs[4 * group + step]
+        for at in range(3):
+            into = (2 * at + group) * part
+            qkv_ref[place, :, into : into + part] = ref[turn, :, at * part : (at + 1) * part].astype(FULL)
+    out_ref[place] = refs[step][turn, :, 3 * part :].astype(FULL)
+
+
+def settle_kernel(which, inner, inputs, ids, *refs):
+    for step in range(4):
+
+        @pl.when(pl.program_id(0) == step)
+        def _():
+            for turn in range(4):
+                inner(ids, step, refs[:inputs], turn, turn ^ (ids[which] % 4), *refs[inputs:])
+
+
+def settle(ids, which, inner, arrays, shapes, blocks, axis=0, after=()):
+    def place(s, ids, rank):
+        index = [0] * rank
+        index[axis] = s ^ (ids[which] // 4)
+        return tuple(index)
+
+    return call(
+        functools.partial(settle_kernel, which, inner, len(arrays)),
+        (4,),
+        [const_spec(array.shape) for array in arrays],
+        [pl.BlockSpec(block, functools.partial(place, rank=len(block))) for block in blocks],
+        [struct(shape, FULL) for shape in shapes],
+        us=9,
+        after=after,
+    )(ids, *arrays)
+
+
+CORE, Y, NEAR_Z, FAR_Z = 1, 2, 4, 8
+
+
+def swap(array, bit):
+    return lax.ppermute(array, "rep", [(at, at ^ bit) for at in range(16)])
+
+
+def cross(array):
+    return lax.ppermute(array, "fsdp", [(0, 1), (1, 0)])
+
+
+def fold_kernel(counts, ids, *refs):
+    outs = refs[sum(counts) :]
+    at = 0
+    for count, out_ref in zip(counts, outs):
+        total = refs[at][...].astype(FULL)
+        for ref in refs[at + 1 : at + count]:
+            total += ref[...].astype(FULL)
+        out_ref[...] = total.astype(LOW)
+        at += count
+
+
+def fold(ids, *jobs, after=()):
+    in_specs, arrays, out_specs, out_shape = [], [], [], []
+    moved = 0
+    for job in jobs:
+        for array, side, first, count in job:
+            sides, unused, rows, columns = array.shape
+            wide = sides if side is None else 1
+            base = 0 if side is None else side
+            if count % 4 == 0:
+                block = (wide, count // 4, rows, columns)
+                spec = lambda s, ids, base=base, at=first // (count // 4): (base, at + s, 0, 0)
+            elif rows % 64 == 0:
+                block = (wide, count, rows // 4, columns)
+                spec = lambda s, ids, base=base, at=first // count: (base, at, s, 0)
+            else:
+                block = (wide, count, rows, columns)
+                spec = lambda s, ids, base=base, at=first // count: (base, at, 0, 0)
+            in_specs.append(pl.BlockSpec(block, spec))
+            arrays.append(array)
+            moved += wide * count * rows * columns * 2
+        if count % 4 == 0:
+            out_specs.append(pl.BlockSpec(block, lambda s, ids: (0, s, 0, 0)))
+        elif rows % 64 == 0:
+            out_specs.append(pl.BlockSpec(block, lambda s, ids: (0, 0, s, 0)))
+        else:
+            out_specs.append(pl.BlockSpec(block, lambda s, ids: (0, 0, 0, 0)))
+        out_shape.append(struct((wide, count, rows, columns), LOW))
+        moved += wide * count * rows * columns * 2
+    return call(
+        functools.partial(fold_kernel, [len(job) for job in jobs]),
+        (4,),
+        in_specs,
+        out_specs,
+        out_shape,
+        us=6,
+        after=after,
+    )(ids, *arrays)
+
+
+def spread_pieces(first, second):
+    return first, second, swap(first, CORE), swap(second, CORE)
+
+
+def join(piece, got):
+    return jnp.concatenate([piece, got], axis=0)
+
+
+RING = (FAR_Z, NEAR_Z, NEAR_Z | FAR_Z)
+
+
+def along_z(piece):
+    return jnp.concatenate([piece] + [swap(piece, bit) for bit in RING], axis=0)
+
+
+def later(value, *others):
+    return lax.optimization_barrier((value,) + others)[0]
+
+
+def paired_device(
+    frames, cotangent, clip_lengths, clip_slots, gain_attn, shift_attn, w_qkv, bias_query, bias_value,
+    w_out, bias_out, gain_ffn, shift_ffn, w_up, bias_up, w_down, bias_down,
+):
+    unused, rows, width = frames.shape
+    half = width // 2
+    eighth = half // 8
+    side = lax.axis_index("fsdp")
+    at = lax.axis_index("rep")
+
+    def mine(order):
+        return sum(jnp.where(at & bit != 0, 8 >> k, 0) for k, bit in enumerate(order))
+
+    plain = (CORE, Y, NEAR_Z, FAR_Z)
+    turned_order = (CORE, NEAR_Z, Y, FAR_Z)
+    ids = jnp.stack([side, mine(plain), mine(turned_order), at & 1]).astype(jnp.int32)
+
+    own_small = jnp.concatenate(
+        [gain_attn, shift_attn, bias_query, bias_value, bias_out, gain_ffn, shift_ffn, bias_down, bias_up]
+    )[None].astype(FULL)
+    params = join(own_small, cross(own_small))
+
+    def piece_of(weight):
+        return lax.dynamic_slice_in_dim(weight, (ids[1] // 2) * eighth, eighth, axis=0)
+
+    tile = 512
+    tiles = w_down.shape[0] // tile
+    ff_half = w_up.shape[1] // 2
+    send_qkv = piece_of(w_qkv).reshape(eighth, 3, 2, half)
+    q_a = cross(send_qkv[:, :, 0].reshape(eighth, 3 * half))[None]
+    send_norm = first_norm(ids, frames, params, 1)
+    slots = later(clip_slots, send_norm)
+    slot = jnp.where(side == 0, slots[0], slots[1])
+    numbers = jnp.arange(clip_lengths.shape[0], dtype=jnp.int32)
+    span = jnp.sum(jnp.where(numbers == slot, clip_lengths, 0))
+    place = jnp.arange(2 * rows, dtype=jnp.int32)
+    place = jnp.where(place < rows, place + side * rows, place - rows + (1 - side) * rows)
+    mask = jnp.where(place < span, 0.0, -1e30).astype(FULL)
+    own_norm = first_norm(ids, frames, params, 0, (send_norm,))
+    far_norm = cross(send_norm)
+    q_b = cross(send_qkv[:, :, 1].reshape(eighth, 3 * half))[None]
+    q_a = later(q_a, own_norm)
+    q_a = join(q_a, swap(q_a, NEAR_Z))
+    q_a = spread_pieces(q_a, swap(q_a, Y))
+    q_b = join(q_b, swap(q_b, NEAR_Z))
+    send_up = piece_of(w_up)
+    send_near = lax.dynamic_slice_in_dim(send_up, (1 - side) * ff_half, ff_half, axis=1)
+    send_far = lax.dynamic_slice_in_dim(send_up, side * ff_half, ff_half, axis=1)
+    send_out, send_near = later(piece_of(w_out), far_norm), later(send_near, far_norm)
+    qkv0, whole0, norm_turned = project(ids, 0, own_norm, far_norm, w_qkv, q_a, params, (send_out, send_near, q_b))
+
+    send_down = lax.dynamic_index_in_dim(w_down.reshape(tiles, 8, tile // 8, width), ids[1] // 2, 1, keepdims=False)
+    send_down = later(send_down, qkv0)
+    q_by = later(swap(q_b, Y), qkv0)
+    w_o = later(cross(send_out), qkv0)[None]
+    mixed0, totals0 = attend_rows(ids, qkv0, mask[None], (q_by, w_o, send_down))
+
+    w_o = join(w_o, later(swap(w_o, NEAR_Z), mixed0))
+    w_n = later(cross(send_near), mixed0)[None]
+    send_cot = lax.dynamic_index_in_dim(cotangent, 1 - side, 0, keepdims=False).astype(LOW)
+    send_cot = later(send_cot, mixed0)
+    qkv1, whole1 = project(ids, 1, own_norm, far_norm, w_qkv, spread_pieces(q_b, q_by), params, (w_o, w_n, send_cot))
+
+    w_oy = later(swap(w_o, Y), qkv1)
+    w_n = join(w_n, later(swap(w_n, NEAR_Z), qkv1))
+    w_d = later(cross(send_down), qkv1)[None]
+    mixed1, totals1 = attend_rows(ids, qkv1, mask[None], (w_oy, w_n, w_d))
+
+    w_ny = later(swap(w_n, Y), mixed1)
+    w_d = join(w_d, later(swap(w_d, NEAR_Z), mixed1))
+    send_far = later(send_far, mixed1)
+    resid, norm_f, norm_f_turned, whole_out = out_rows(
+        ids, mixed0, mixed1, w_out, spread_pieces(w_o, w_oy), frames, far_norm, params, (w_ny, w_d, send_far)
+    )
+
+    far_cot = cross(send_cot)
+    w_f = later(cross(send_far), resid)[None]
+    near_up = spread_pieces(w_n, w_ny)
+    dout, y, dn, *grads = feed_rows(
+        ids, 0, 0, 2, norm_f, norm_f_turned, (cotangent, far_cot, resid), w_up, near_up, (w_down,), params, after=(w_f,)
+    )
+
+    w_f = join(w_f, later(swap(w_f, NEAR_Z), y))
+    w_dy = later(swap(w_d, Y), y)
+    y, dn, near0, near0_a, near0_b, far0, far0_a, far0_b, down0, down0_a, down0_b, bias0 = feed_rows(
+        ids, 0, 2, tiles - 2, norm_f, norm_f_turned, (dout, y, dn), w_up, near_up, (w_down,), params, grads, after=(w_f, w_dy)
+    )
+
+    w_fy = later(swap(w_f, Y), y)
+    far_up = spread_pieces(w_f, w_fy)
+    far_down = spread_pieces(w_d, w_dy)
+    y, dn, *grads = feed_rows(
+        ids, 1, 0, 2, norm_f, norm_f_turned, (dout, y, dn), w_up, far_up, far_down, params
+    )
+
+    def from_core(mark, *arrays):
+        return [later(swap(array, CORE), mark) for array in arrays]
+
+    def terms(first, count, *arrays):
+        return [(array, 0, first, count) for array in arrays]
+
+    near0_ga, near0_gb, far0_ga, far0_gb = from_core(y, near0_a, near0_b, far0_a, far0_b)
+    down0 = down0[None]
+    down0_ga, down0_gb = from_core(y, down0_a[None], down0_b[None])
+    up1_xa, up1_xb, down0_z = fold(
+        ids,
+        terms(0, 4, far0, far0_ga),
+        terms(4, 4, far0) + terms(0, 4, far0_gb),
+        terms(4, 4, down0) + terms(0, 4, down0_gb),
+    )
+    output, far_out, dn, near1, near1_a, near1_b, far1, far1_a, far1_b, down1, down1_a, down1_b, bias1 = feed_rows(
+        ids, 1, 2, tiles - 2, norm_f, norm_f_turned, (dout, y, dn), w_up, far_up, far_down, params,
+        grads, frames.shape, (up1_xa, up1_xb, down0_z),
+    )
+
+    up1_oa, up1_ob = later(cross(up1_xa), dn), later(cross(up1_xb), dn)
+    down0_zg = later(swap(down0_z, NEAR_Z), dn)
+    d_resid, d_mixed, *o_pieces, small_mid = middle_rows(
+        ids, dn, resid, cotangent, far_cot, mixed0, mixed1, whole_out, params, (up1_oa, up1_ob, down0_zg)
+    )
+
+    near1_ga, near1_gb, far1_ga, far1_gb = from_core(d_mixed, near1_a, near1_b, far1_a, far1_b)
+    down1 = down1[None]
+    down1_ga, down1_gb = from_core(d_mixed, down1_a[None], down1_b[None])
+    up1_y, up0_xa, up0_xb, down1_z = fold(
+        ids,
+        terms(4, 4, near1) + terms(0, 4, near1_gb, up1_ob),
+        terms(0, 4, far1, far1_ga),
+        terms(4, 4, far1) + terms(0, 4, far1_gb),
+        terms(4, 4, down1) + terms(0, 4, down1_gb),
+    )
+    d0 = attend_back_rows(ids, 0, qkv0, d_mixed, mask[:, None], totals0, (up1_y, up0_xa, up0_xb, down1_z))
+
+    up0_oa, up0_ob = later(cross(up0_xa), d0), later(cross(up0_xb), d0)
+    up1 = [near1, near1_ga, up1_oa, later(swap(up1_y, Y), d0)]
+    up0 = [near0, near0_ga, up0_oa]
+    up1_z, up0_y, down_x = fold(
+        ids,
+        terms(2, 2, *up1),
+        terms(4, 4, near0) + terms(0, 4, near0_gb, up0_ob),
+        terms(0, 4, down1, down1_ga, later(swap(down1_z, NEAR_Z), d0)),
+    )
+    q0n, q0n_a, q0n_b, q0f, q0f_a, q0f_b, small_q0 = project_grad(
+        ids, norm_turned, d0, o_pieces, (up1_z, up0_y, down_x)
+    )
+
+    far_out = later(far_out, q0n)
+    d1 = attend_back_rows(ids, 1, qkv1, d_mixed, mask[:, None], totals1, (far_out,), range(4))
+
+    q0n_ga, q0n_gb, q0f_ga, q0f_gb = from_core(d1, q0n_a, q0n_b, q0f_a, q0f_b)
+    up1.append(later(swap(up1_z, NEAR_Z), d1))
+    up0.append(later(swap(up0_y, Y), d1))
+    q0_xa, q0_xb, up1_f, up0_z = fold(
+        ids,
+        terms(0, 4, q0f, q0f_ga),
+        terms(4, 4, q0f) + terms(0, 4, q0f_gb),
+        terms(1, 1, *up1),
+        terms(2, 2, *up0),
+    )
+    d1 = attend_back_rows(
+        ids, 1, qkv1, d_mixed, mask[:, None], totals1, (q0_xa, q0_xb, up1_f, up0_z), range(4, 8), (d1,)
+    )
+
+    down = [down0, down0_ga, down0_zg, later(cross(down_x), d1)]
+    up1.append(later(swap(up1_f, FAR_Z), d1))
+    up0.append(later(swap(up0_z, NEAR_Z), d1))
+    down_y, up0_f, up1 = fold(ids, terms(2, 2, *down), terms(1, 1, *up0), terms(0, 1, *up1))
+    q1n, q1n_a, q1n_b, q1f, q1f_a, q1f_b, small_q1 = project_grad(ids, norm_turned, d1, (), (down_y, up0_f, up1))
+
+    q1n_ga, q1n_gb, q1f_ga, q1f_gb = from_core(q1n, q1n_a, q1n_b, q1f_a, q1f_b)
+    down.append(later(swap(down_y, Y), q1n))
+    up0.append(later(swap(up0_f, FAR_Z), q1n))
+    q1_yn, q1_yf, down_f, up0 = fold(
+        ids,
+        terms(4, 4, q1n) + terms(0, 4, q1n_gb),
+        terms(4, 4, q1f) + terms(0, 4, q1f_gb),
+        terms(1, 1, *down),
+        terms(0, 1, *up0),
+    )
+    up = jnp.concatenate([up0[0], up1[0]], axis=2)
+    frames_grad, far_grad, small_last = last_rows(
+        ids, d0, d1, whole0, whole1, frames, far_norm, d_resid, params, (q1_yn, q1_yf, down_f, up)
+    )
+
+    q1 = [q1n, q1n_ga, later(swap(q1_yn, Y), far_grad)]
+    q0_oa, q0_ob = later(cross(q0_xa), far_grad), later(cross(q0_xb), far_grad)
+    down.append(later(swap(down_f, FAR_Z), far_grad))
+    q0 = [q0n, q0n_ga, q0_oa]
+    q1_x, q0_y, down = fold(
+        ids,
+        terms(0, 4, q1f, q1f_ga, later(swap(q1_yf, Y), far_grad)),
+        terms(4, 4, q0n) + terms(0, 4, q0n_gb, q0_ob),
+        terms(0, 1, *down),
+    )
+    up = join(up, later(swap(up, FAR_Z), q1_x))
+    down = down[0]
+    output = fill_rows(ids, output, cross(far_out), (up,))
+
+    q1.append(later(cross(q1_x), output))
+    q1_z = fold(ids, *[terms(at, 1, *q1) for at in (1, 2, 3)])
+    far_grad = later(far_grad, q1_z[0])
+    down = join(down, later(swap(down, FAR_Z), q1_z[0]))
+
+    q0.append(later(swap(q0_y, Y), down))
+    q0_z = fold(ids, *[terms(at, 1, *q0) for at in (1, 2, 3)])
+    up = join(up, later(swap(up, NEAR_Z), q0_z[0]))
+    q1 = fold(ids, terms(0, 1, *q1) + terms(0, 1, *[later(swap(array, bit), up) for array, bit in zip(q1_z, RING)]))[0][0]
+    down = join(down, later(swap(down, Y), q1))
+    q0 = fold(ids, terms(0, 1, *q0) + terms(0, 1, *[later(swap(array, bit), down) for array, bit in zip(q0_z, RING)]))[0][0]
+    q1 = later(along_z(q1), q0)
+    up = spread_pieces(up, later(swap(up, Y), q1))
+    q0 = later(along_z(q0), up[1])
+    frames_grad = fill_rows(ids, frames_grad, cross(far_grad), (q0,))
+    q1 = spread_pieces(q1, later(swap(q1, Y), frames_grad))
+    ff = 2 * ff_half
+    block = half // 16
+    up_out, = settle(ids, 1, settle_up_kernel, list(up), [(16, block, ff)], [(4, block, ff)], after=(q1[1],))
+    down = spread_pieces(down, later(swap(down, NEAR_Z), up_out))
+    q0 = spread_pieces(q0, later(swap(q0, Y), down[1]))
+    down_out, = settle(
+        ids, 2, settle_down_kernel, list(down), [(tiles, 16, tile // 16, width)], [(tiles, 4, tile // 16, width)], 1, (q0[1],)
+    )
+
+    bias_up_sum = jnp.where(side == 0, jnp.concatenate([bias0, bias1]), jnp.concatenate([bias1, bias0]))
+    query_sum = jnp.concatenate([small_q0[0], small_q1[0]], axis=0)
+    value_sum = jnp.concatenate([small_q0[2], small_q1[2]], axis=0)
+    vectors = [small_last[0], small_last[1], query_sum, value_sum, small_mid[0], small_mid[1], small_mid[2], small_mid[3]]
+    small = jnp.concatenate([v.reshape(2, half) for v in vectors] + [bias_up_sum], axis=1)
+    got = cross(lax.dynamic_slice_in_dim(small, 1 - side, 1, axis=0))
+    small = lax.dynamic_slice_in_dim(small, side, 1, axis=0) + got
+    for bit in plain:
+        small = small + swap(small, bit)
+    small = small[0]
+    parts = [small[k * half : (k + 1) * half] for k in range(8)] + [small[8 * half :]]
+
+    qkv_out, out_out = settle(
+        ids, 1, settle_qkv_kernel, [*q0, *q1], [(16, block, 3 * width), (16, block, width)], [(4, block, 3 * width), (4, block, width)]
+    )
+    return (
+        output,
+        frames_grad,
+        parts[0],
+        parts[1],
+        qkv_out.reshape(half, 3 * width),
+        parts[2],
+        parts[3],
+        out_out.reshape(half, width),
+        parts[4],
+        parts[5],
+        parts[6],
+        up_out.reshape(half, ff),
+        parts[8],
+        down_out.reshape(ff_half, width),
+        parts[7],
+    )
+
+
 def solution(mesh):
+    fast = mesh.shape["fsdp"] == 2 and mesh.shape["rep"] == 16
     return jax.shard_map(
-        on_device,
+        paired_device if fast else general_device,
         mesh=mesh,
         in_specs=(
             P("rep", "fsdp", None),

time: 2680 us -> 751 us (0.28)
  waiting for transfers between devices: 1820 us -> 139 us
  Pallas kernels: 0 us -> 452 us
  matrix products: 426 us -> 0 us
  other arithmetic: 164 us -> 18.4 us
  blocking collectives: 112 us -> 0 us
  local copies, waits for them, and re-layouts: 136 us -> 30.8 us
  starting transfers between devices: 0.86 us -> 98.7 us
    reduce_scatter x8 -> x0, waiting for transfers between devices: 893 us -> none  [the longest x4 799 us: on_device(): lax.psum_scatter(weight_grads(joined, small_sum), 'fsdp', scatter_dimensi...]
    psum x1 -> x0, waiting for transfers between devices: 489 us -> none  [on_device(): lax.psum((owned[0], owned[1], owned[2], owned[3], owned[4], owned[5], own...]
    pallas_call x0 -> x34, Pallas kernels: none -> 452 us  [call(): return lambda *args: run(*args, *after)]
    all_gather x8 -> x0, waiting for transfers between devices: 434 us -> none  [the longest x1 135 us: on_device(): lax.all_gather(shards[11], 'fsdp', axis=0, tiled=True)]
    dot_general x44 -> x0, matrix products: 426 us -> none  [the longest x8 131 us: product_right(): lax.dot_general(left, right, (((1,), (1,)), ((), ())), preferred_element_...]
    ppermute x0 -> x109, waiting for transfers between devices: none -> 139 us  [the longest x89 96.3 us: swap(): return lax.ppermute(array, 'rep', [(at, at ^ bit) for at in range(16)])]
    ppermute x0 -> x109, starting transfers between devices: none -> 98.7 us  [the longest x89 74.1 us: swap(): return lax.ppermute(array, 'rep', [(at, at ^ bit) for at in range(16)])]
    reduce_sum x15 -> x1, other arithmetic: 72.7 us -> 0.63 us  [paired_device(): span = jnp.sum(jnp.where(numbers == slot, clip_lengths, 0))]
  transfers between devices with their start and end apart: 17 -> 109, of which waited for: 13 -> 28; matrix products, arithmetic and copies ran while one was open for 19% -> 4% of each run, Pallas kernels for 0% -> 59%
where the time goes in v2:
time: 751 us; the launch traced here: 742 us
  Pallas kernels  452 us (60%)
  waiting for transfers between devices  139 us (19%)
  starting transfers between devices  98.7 us (13%)
  local copies, waits for them, and re-layouts  30.8 us (4%)
  other arithmetic  18.4 us (2%)
    pallas_call x34, Pallas kernels, call(): return lambda *args: run(*args, *after)  452 us
    ppermute x89, waiting for transfers between devices, swap(): return lax.ppermute(array, 'rep', [(at, at ^ bit) for at in range(16)])  96.3 us
    ppermute x89, starting transfers between devices, swap(): return lax.ppermute(array, 'rep', [(at, at ^ bit) for at in range(16)])  74.1 us
    ppermute x20, waiting for transfers between devices, cross(): return lax.ppermute(array, 'fsdp', [(0, 1), (1, 0)])  42.8 us
    ppermute x20, starting transfers between devices, cross(): return lax.ppermute(array, 'fsdp', [(0, 1), (1, 0)])  24.6 us
  transfers between devices with their start and end apart: 109, of which 28 were waited for; matrix products, arithmetic and copies ran while one was open for 4% of the time, Pallas kernels for 59%

profile of v2, /device:TPU:0, one launch (start us, length us, event | category | flops | bytes accessed | tf_op | source)
XLA Modules:
  0.0 742.4 jit_solution(14135252805356278674)
XLA Ops:
  38.9 8.3 %collective-permute-done.4.refs_4_ = bf16[2,80,1920]{2,1,0:T(8,128)(2,1)} collective-permute-done((bf16[2,80,1920]{2,1,0:T(8,128)(2,1)}, bf16[2,80,1920]{2,1,0:T(8,128)(2,1)}, u32[]{:S(2)}, u32[]{:S(2)}) %collective-permute-start.4) | collective-permute-done | bytes 614432 | tf_op jit(solution)/shard_map/ppermute | solution.py:1089
  62.8 12.7 %shard_map.282 = (bf16[1024,1920]{1,0:T(8,128)(2,1)}, bf16[1280,1920]{1,0:T(8,128)(2,1)}, bf16[1280,1024]{1,0:T(8,128)(2,1)}) custom-call(s32[4]{0:T(128)} %pad_add_fusion.ids, bf16[512,1280]{1,0:T(8,128)(2,1)} %shard_map.281.refs_0_, bf16[512,1408]{1,0:T(8,128)(2,1)} %collective-permute-done.1.refs_1_.refs_8_.refs_5_, bf16[640,3840]{1,0:T(8,128)(2,1)} %refs_2_.6, ...), custom_call_target="tpu_custom_call" | custom-call | flops 13799999488 | tf_op jit(solution)/shard_map/pallas_call | solution.py:339
  78.6 18.7 %shard_map.283 = (bf16[1024,640]{1,0:T(8,128)(2,1)}, f32[8,1024]{1,0:T(8,128)}) custom-call(s32[4]{0:T(128)} %pad_add_fusion.ids, bf16[1024,1920]{1,0:T(8,128)(2,1)} %get-tuple-element.218.refs_0_.refs_1_.refs_2_, bf16[1024,1920]{1,0:T(8,128)(2,1)} %get-tuple-element.218.refs_0_.refs_1_.refs_2_, ...), custom_call_target="tpu_custom_call" | custom-call | flops 21849999360 | tf_op jit(solution)/shard_map/pallas_call | solution.py:339
  101.8 11.6 %shard_map.284 = (bf16[1024,1920]{1,0:T(8,128)(2,1)}, bf16[1280,1920]{1,0:T(8,128)(2,1)}) custom-call(s32[4]{0:T(128)} %pad_add_fusion.ids, bf16[512,1280]{1,0:T(8,128)(2,1)} %shard_map.281.refs_0_, bf16[512,1408]{1,0:T(8,128)(2,1)} %collective-permute-done.1.refs_1_.refs_8_.refs_5_, bf16[640,3840]{1,0:T(8,128)(2,1)} %refs_2_.6, ...), custom_call_target="tpu_custom_call" | custom-call | flops 13799999488 | tf_op jit(solution)/shard_map/pallas_call | solution.py:339
  116.9 18.9 %shard_map.285 = (bf16[1024,640]{1,0:T(8,128)(2,1)}, f32[8,1024]{1,0:T(8,128)}) custom-call(s32[4]{0:T(128)} %pad_add_fusion.ids, bf16[1024,1920]{1,0:T(8,128)(2,1)} %get-tuple-element.227.refs_0_.refs_1_.refs_2_, bf16[1024,1920]{1,0:T(8,128)(2,1)} %get-tuple-element.227.refs_0_.refs_1_.refs_2_, ...), custom_call_target="tpu_custom_call" | custom-call | flops 21849999360 | tf_op jit(solution)/shard_map/pallas_call | solution.py:339
  141.7 12.6 %shard_map.286 = (f32[1024,1280]{1,0:T(8,128)}, bf16[1024,1280]{1,0:T(8,128)(2,1)}, bf16[1280,1024]{1,0:T(8,128)(2,1)}, bf16[1280,1280]{1,0:T(8,128)(2,1)}) custom-call(s32[4]{0:T(128)} %pad_add_fusion.ids, bf16[1024,640]{1,0:T(8,128)(2,1)} %get-tuple-element.223.refs_0_.refs_4_, bf16[1024,640]{1,0:T(8,128)(2,1)} %get-tuple-element.231.refs_1_.refs_5_, ...), custom_call_target="tpu_custom_call" | custom-call | flops 13799999488 | tf_op jit(solution)/shard_map/pallas_call | solution.py:339
  155.4 30.1 %shard_map.287 = (bf16[1024,1280]{1,0:T(8,128)(2,1)}, f32[1024,1280]{1,0:T(8,128)}, f32[1024,1280]{1,0:T(8,128)}, bf16[1,8,40,2560]{3,2,1,0:T(8,128)(2,1)}, bf16...) custom-call(s32[4]{0:T(128)} %pad_add_fusion.ids, ...), custom_call_target="tpu_custom_call" | custom-call | flops 29899999232 | tf_op jit(solution)/shard_map/pallas_call | solution.py:339
  188.3 36.9 %shard_map.288 = (f32[1024,1280]{1,0:T(8,128)}, f32[1024,1280]{1,0:T(8,128)}, bf16[1,8,40,2560]{3,2,1,0:T(8,128)(2,1)}, bf16[1,4,40,2560]{3,2,1,0:T(8,128)(2,1)}...) custom-call(s32[4]{0:T(128)} %pad_add_fusion.ids, ...), custom_call_target="tpu_custom_call", output_to_operand_aliasing={{2}: (13, {}), {3}: (14, {}), {4}: (15, {}), {5}: (16, {}),... | custom-call | flops 43124998144 | tf_op jit(solution)/shard_map/pallas_call | solution.py:339
  229.9 29.8 %shard_map.289 = (f32[1024,1280]{1,0:T(8,128)}, f32[1024,1280]{1,0:T(8,128)}, bf16[1,8,40,2560]{3,2,1,0:T(8,128)(2,1)}, bf16[1,4,40,2560]{3,2,1,0:T(8,128)(2,1)}...) custom-call(s32[4]{0:T(128)} %pad_add_fusion.ids, ...), custom_call_target="tpu_custom_call" | custom-call | flops 29899999232 | tf_op jit(solution)/shard_map/pallas_call | solution.py:339
  269.9 38.9 %shard_map.291 = (f32[2,512,1280]{2,1,0:T(8,128)}, bf16[512,1280]{1,0:T(8,128)(2,1)}, f32[1024,1280]{1,0:T(8,128)}, bf16[1,8,40,2560]{3,2,1,0:T(8,128)(2,1)}, bf...) custom-call(s32[4]{0:T(128)} %pad_add_fusion.ids, ...), custom_call_target="tpu_custom_call", output_to_operand_aliasing={{3}: (16, {}), {4}: (17, {}), {5}: (18, {}), {6}: (19, {}),... | custom-call | flops 43124998144 | tf_op jit(solution)/shard_map/pallas_call | solution.py:339
  310.5 19.6 %shard_map.292 = (f32[1024,1280]{1,0:T(8,128)}, bf16[1024,1280]{1,0:T(8,128)(2,1)}, bf16[1,8,40,1280]{3,2,1,0:T(8,128)(2,1)}, bf16[1,4,40,1280]{3,2,1,0:T(8,128)...) custom-call(s32[4]{0:T(128)} %pad_add_fusion.ids, ...), custom_call_target="tpu_custom_call" | custom-call | flops 23000000512 | tf_op jit(solution)/shard_map/pallas_call | solution.py:339
  330.5 6.6 shard_map.293
  341.2 31.4 %shard_map.294.refs_1_.refs_0_ = bf16[1024,1920]{1,0:T(8,128)(2,1)} custom-call(s32[4]{0:T(128)} %pad_add_fusion.ids, bf16[1024,1920]{1,0:T(8,128)(2,1)} %get-tuple-element.218.refs_0_.refs_1_.refs_2_, bf16[1024,1920]{1,0:T(8,128)(2,1)} %get-tuple-element.218.refs_0_.refs_1_.refs_2_, bf16[1024,1920]{1,0:T(8,128)(2,1)} %get-tuple-element.218.refs_0_.refs_1_.refs_2_, ...), custom_call_target="tpu_custom_call" | custom-call | flops 35649998848 | tf_op jit(solution)/shard_map/pallas_call | solution.py:339
  377.2 7.1 shard_map.295
  387.0 14.7 %shard_map.296 = (bf16[1,8,40,3200]{3,2,1,0:T(8,128)(2,1)}, bf16[1,4,40,3200]{3,2,1,0:T(8,128)(2,1)}, bf16[1,4,40,3200]{3,2,1,0:T(8,128)(2,1)}, bf16[1,8,40,3200...) custom-call(s32[4]{0:T(128)} %pad_add_fusion.ids, ...), custom_call_target="tpu_custom_call" | custom-call | flops 12650000384 | tf_op jit(solution)/shard_map/pallas_call | solution.py:339
  402.3 18.9 %shard_map.297.refs_6_ = bf16[1024,1920]{1,0:T(8,128)(2,1)} custom-call(s32[4]{0:T(128)} %pad_add_fusion.ids, bf16[1024,1920]{1,0:T(8,128)(2,1)} %get-tuple-element.227.refs_0_.refs_1_.refs_2_, bf16[1024,1920]{1,0:T(8,128)(2,1)} %get-tuple-element.227.refs_0_.refs_1_.refs_2_, bf16[1024,1920]{1,0:T(8,128)(2,1)} %get-tuple-element.227.refs_0_.refs_1_.refs_2_, ...), custom_call_target="tpu_custom_call" | custom-call | flops 17824999424 | tf_op jit(solution)/shard_map/pallas_call | solution.py:339
  423.0 6.6 shard_map.298
  433.2 20.0 %shard_map.299.refs_1_ = bf16[1024,1920]{1,0:T(8,128)(2,1)} custom-call(s32[4]{0:T(128)} %pad_add_fusion.ids, bf16[1024,1920]{1,0:T(8,128)(2,1)} %get-tuple-element.227.refs_0_.refs_1_.refs_2_, bf16[1024,1920]{1,0:T(8,128)(2,1)} %get-tuple-element.227.refs_0_.refs_1_.refs_2_, bf16[1024,1920]{1,0:T(8,128)(2,1)} %get-tuple-element.227.refs_0_.refs_1_.refs_2_, ...), custom_call_target="tpu_custom_call" | custom-call | flops 17824999424 | tf_op jit(solution)/shard_map/pallas_call | solution.py:339
  455.2 6.9 shard_map.300
  463.6 11.5 %shard_map.301 = (bf16[1,8,40,1920]{3,2,1,0:T(8,128)(2,1)}, bf16[1,4,40,1920]{3,2,1,0:T(8,128)(2,1)}, bf16[1,4,40,1920]{3,2,1,0:T(8,128)(2,1)}, bf16[1,8,40,1920...) custom-call(s32[4]{0:T(128)} %pad_add_fusion.ids, ...), custom_call_target="tpu_custom_call" | custom-call | flops 12650000384 | tf_op jit(solution)/shard_map/pallas_call | solution.py:339
  495.0 23.2 %shard_map.303 = (f32[2,512,1280]{2,1,0:T(8,128)}, bf16[512,1280]{1,0:T(8,128)(2,1)}, f32[8,1280]{1,0:T(8,128)}) custom-call(s32[4]{0:T(128)} %pad_add_fusion.ids, bf16[1024,1920]{1,0:T(8,128)(2,1)} %shard_map.294.refs_1_.refs_0_, bf16[1024,1920]{1,0:T(8,128)(2,1)} %shard_map.299.refs_1_, bf16[1280,1920]{1,0:T(8,128)(2,1)} %get-tuple-element.361.refs_2_, ...), custom_call_target="tpu_custom_call" | custom-call | flops 25300000768 | tf_op jit(solution)/shard_map/pallas_call | solution.py:339
  519.2 12.0 %collective-permute-done.68.refs_5_ = bf16[1,4,40,3200]{3,2,1,0:T(8,128)(2,1)} collective-permute-done((bf16[1,4,40,3200]{3,2,1,0:T(8,128)(2,1)}, bf16[1,4,40,3200]{3,2,1,0:T(8,128)(2,1)}, u32[]{:S(2)}, u32[]{:S(2)}) %collective-permute-start.68) | collective-permute-done | bytes 1024032 | tf_op jit(solution)/shard_map/ppermute | solution.py:1093
  533.8 18.5 %collective-permute-done.75.refs_2_.refs_6_.refs_10_ = bf16[1,4,40,3200]{3,2,1,0:T(8,128)(2,1)} collective-permute-done((bf16[1,4,40,3200]{3,2,1,0:T(8,128)(2,1)}, bf16[1,4,40,3200]{3,2,1,0:T(8,128)(2,1)}, u32[]{:S(2)}, u32[]{:S(2)}) %collective-permute-start.75) | collective-permute-done | bytes 1024032 | tf_op jit(solution)/shard_map/ppermute | solution.py:1093
  553.4 6.8 shard_map.304
  599.0 8.9 %collective-permute-done.81 = bf16[2,40,5120]{2,1,0:T(8,128)(2,1)} collective-permute-done((bf16[2,40,5120]{2,1,0:T(8,128)(2,1)}, bf16[2,40,5120]{2,1,0:T(8,128)(2,1)}, u32[]{:S(2)}, u32[]{:S(2)}) %collective-permute-start.81) | collective-permute-done | bytes 819232 | tf_op jit(solution)/shard_map/ppermute | solution.py:1089
  627.4 8.0 %collective-permute-start.91 = (bf16[1,40,1920]{2,1,0:T(8,128)(2,1)S(1)}, bf16[1,40,1920]{2,1,0:T(8,128)(2,1)S(1)}, u32[]{:S(2)}, u32[]{:S(2)}) collective-permute-start(bf16[1,40,1920]{2,1,0:T(8,128)(2,1)S(1)} %bitcast.71), channel_id=1, source_target_pairs={{0,8},{2,10},{4,12},{6,14},{8,0},{10,2},{12,4},{14,6},{16,24},{18,... | collective-permute-start | bytes 460808 | tf_op jit(solution)/shard_map/ppermute | solution.py:1089
  653.7 10.8 %collective-permute-done.87 = bf16[1,40,3200]{2,1,0:T(8,128)(2,1)S(1)} collective-permute-done((bf16[1,40,3200]{2,1,0:T(8,128)(2,1)}, bf16[1,40,3200]{2,1,0:T(8,128)(2,1)S(1)}, u32[]{:S(2)}, u32[]{:S(2)}) %collective-permute-start.87) | collective-permute-done | bytes 256032 | tf_op jit(solution)/shard_map/ppermute | solution.py:1089
  674.1 7.0 collective-permute-done.102.refs_4_.refs_5_
  682.3 8.7 %shard_map.311 = f32[16,40,5120]{2,1,0:T(8,128)} custom-call(s32[4]{0:T(128)} %pad_add_fusion.ids, bf16[4,40,5120]{2,1,0:T(8,128)(2,1)} %pad_maximum_fusion.1.refs_0_, bf16[4,40,5120]{2,1,0:T(8,128)(2,1)} %collective-permute-done.89.refs_1_, bf16[4,40,5120]{2,1,0:T(8,128)(2,1)} %collective-permute-done.100.refs_2_, ...), custom_call_target="tpu_custom_call" | custom-call | flops 10350000128 | tf_op jit(solution)/shard_map/pallas_call | solution.py:339
  691.0 12.2 %collective-permute-done.99.refs_1_ = bf16[4,160,1280]{2,1,0:T(8,128)(2,1)} collective-permute-done((bf16[4,160,1280]{2,1,0:T(8,128)(2,1)S(1)}, bf16[4,160,1280]{2,1,0:T(8,128)(2,1)}, u32[]{:S(2)}, u32[]{:S(2)}) %collective-permute-start.99) | collective-permute-done | bytes 1638432 | tf_op jit(solution)/shard_map/ppermute | solution.py:1089
  723.8 8.6 %shard_map.312 = (f32[16,40,3840]{2,1,0:T(8,128)}, f32[16,40,1280]{2,1,0:T(8,128)}) custom-call(s32[4]{0:T(128)} %pad_add_fusion.ids, bf16[4,40,3200]{2,1,0:T(8,128)(2,1)} %copy-done, bf16[4,40,3200]{2,1,0:T(8,128)(2,1)} %collective-permute-done.98.refs_1_.refs_4_, bf16[4,40,3200]{2,1,0:T(8,128)(2,1)} %collective-permute-done.103.refs_2_, ...), custom_call_target="tpu_custom_call" | custom-call | flops 10350000128 | tf_op jit(solution)/shard_map/pallas_call | solution.py:339
  733.5 8.7 %shard_map.313 = f32[5,16,32,1280]{3,2,1,0:T(8,128)} custom-call(s32[4]{0:T(128)} %pad_add_fusion.ids, bf16[4,160,1280]{2,1,0:T(8,128)(2,1)} %copy-done.4, bf16[4,160,1280]{2,1,0:T(8,128)(2,1)} %collective-permute-done.99.refs_1_, bf16[4,160,1280]{2,1,0:T(8,128)(2,1)} %copy-done.39, bf16[4,160,1280]{2,1,0:T(8,128)(2,1)} %collective-permute-done.108.refs_3_, ...), custom_call_target="tpu_custom_call" | custom-call | flops 10350000128 | tf_op jit(solution)/shard_map/pallas_call | solution.py:339
  (416 shorter events, 244.0 us)
Async XLA Ops:
  8.7 40.1 %collective-permute-start.7 = (bf16[80,1920]{1,0:T(8,128)(2,1)S(1)}, bf16[80,1920]{1,0:T(8,128)(2,1)S(1)}, u32[]{:S(2)}, u32[]{:S(2)}) collective-permute-start(bf16[80,1920]{1,0:T(8,128)(2,1)S(1)} %bitcast.59), channel_id=1, source_target_pairs={{0,1},{1,0},{2,3},{3,2},{4,5},{5,4},{6,7},{7,6},{8,9},{9,8},{10,11... | collective-permute-start | bytes 921608 | tf_op jit(solution)/shard_map/ppermute | solution.py:1093
  60.6 39.6 %collective-permute-start.11 = (bf16[2,80,1920]{2,1,0:T(8,128)(2,1)S(1)}, bf16[2,80,1920]{2,1,0:T(8,128)(2,1)}, u32[]{:S(2)}, u32[]{:S(2)}) collective-permute-start(bf16[2,80,1920]{2,1,0:T(8,128)(2,1)S(1)} %pad_maximum_fusion.8.refs_10_.refs_3_), channel_id=1, source_target_pairs={{0,2},{2,0},{4,6},{6,4},{8,10},{10,8},{12,14},{14,12},{16,18},{18,... | collective-permute-start | bytes 1843208 | tf_op jit(solution)/shard_map/ppermute | solution.py:1089
  77.1 38.4 %collective-permute-start.17 = (bf16[5,64,1280]{2,1,0:T(8,128)(2,1)S(1)}, bf16[5,64,1280]{2,1,0:T(8,128)(2,1)}, u32[]{:S(2)}, u32[]{:S(2)}) collective-permute-start(bf16[5,64,1280]{2,1,0:T(8,128)(2,1)S(1)} %dynamic-slice_bitcast_fusion.refs_6_), channel_id=1, source_target_pairs={{0,1},{1,0},{2,3},{3,2},{4,5},{5,4},{6,7},{7,6},{8,9},{9,8},{10,11... | collective-permute-start | bytes 2457608 | tf_op jit(solution)/shard_map/ppermute | solution.py:1093
  97.3 57.3 %collective-permute-start.22 = (bf16[512,1280]{1,0:T(8,128)(2,1)S(1)}, bf16[512,1280]{1,0:T(8,128)(2,1)}, u32[]{:S(2)}, u32[]{:S(2)}) collective-permute-start(bf16[512,1280]{1,0:T(8,128)(2,1)S(1)} %fusion.refs_10_), channel_id=1, source_target_pairs={{0,1},{1,0},{2,3},{3,2},{4,5},{5,4},{6,7},{7,6},{8,9},{9,8},{10,11... | collective-permute-start | bytes 3932168 | tf_op jit(solution)/shard_map/ppermute | solution.py:1093
  101.8 38.4 %collective-permute-start.18 = (bf16[2,80,1280]{2,1,0:T(8,128)(2,1)S(1)}, bf16[2,80,1280]{2,1,0:T(8,128)(2,1)}, u32[]{:S(2)}, u32[]{:S(2)}) collective-permute-start(bf16[2,80,1280]{2,1,0:T(8,128)(2,1)S(1)} %pad_maximum_fusion.10.refs_8_.refs_3_), channel_id=1, source_target_pairs={{0,2},{2,0},{4,6},{6,4},{8,10},{10,8},{12,14},{14,12},{16,18},{18,... | collective-permute-start | bytes 1228808 | tf_op jit(solution)/shard_map/ppermute | solution.py:1089
  140.3 47.4 %collective-permute-start.27 = (bf16[2,5,64,1280]{3,2,1,0:T(8,128)(2,1)S(1)}, bf16[2,5,64,1280]{3,2,1,0:T(8,128)(2,1)}, u32[]{:S(2)}, u32[]{:S(2)}) collective-permute-start(bf16[2,5,64,1280]{3,2,1,0:T(8,128)(2,1)S(1)} %pad_maximum_fusion.refs_11_.refs_10_), channel_id=1, source_target_pairs={{0,4},{2,6},{4,0},{6,2},{8,12},{10,14},{12,8},{14,10},{16,20},{18,... | collective-permute-start | bytes 4915208 | tf_op jit(solution)/shard_map/ppermute | solution.py:1089
  154.3 73.0 %collective-permute-start.31 = (bf16[2,5,64,1280]{3,2,1,0:T(8,128)(2,1)}, bf16[2,5,64,1280]{3,2,1,0:T(8,128)(2,1)}, u32[]{:S(2)}, u32[]{:S(2)}) collective-permute-start(bf16[2,5,64,1280]{3,2,1,0:T(8,128)(2,1)} %copy-done.5), channel_id=1, source_target_pairs={{0,2},{2,0},{4,6},{6,4},{8,10},{10,8},{12,14},{14,12},{16,18},{18,... | collective-permute-start | bytes 4915208 | tf_op jit(solution)/shard_map/ppermute | solution.py:1089
  186.6 38.5 %collective-permute-start.28 = (bf16[2,80,2560]{2,1,0:T(8,128)(2,1)S(1)}, bf16[2,80,2560]{2,1,0:T(8,128)(2,1)}, u32[]{:S(2)}, u32[]{:S(2)}) collective-permute-start(bf16[2,80,2560]{2,1,0:T(8,128)(2,1)S(1)} %pad_maximum_fusion.5.refs_22_.refs_6_), channel_id=1, source_target_pairs={{0,4},{2,6},{4,0},{6,2},{8,12},{10,14},{12,8},{14,10},{16,20},{18,... | collective-permute-start | bytes 2457608 | tf_op jit(solution)/shard_map/ppermute | solution.py:1089
  187.8 39.5 %collective-permute-start.29 = (bf16[2,80,2560]{2,1,0:T(8,128)(2,1)S(1)}, bf16[2,80,2560]{2,1,0:T(8,128)(2,1)}, u32[]{:S(2)}, u32[]{:S(2)}) collective-permute-start(bf16[2,80,2560]{2,1,0:T(8,128)(2,1)S(1)} %pad_maximum_fusion.5.refs_22_.refs_6_), channel_id=1, source_target_pairs={{0,2},{2,0},{4,6},{6,4},{8,10},{10,8},{12,14},{14,12},{16,18},{18,... | collective-permute-start | bytes 2457608 | tf_op jit(solution)/shard_map/ppermute | solution.py:1089
  187.8 40.1 %collective-permute-start.32 = (bf16[2,5,64,1280]{3,2,1,0:T(8,128)(2,1)}, bf16[2,5,64,1280]{3,2,1,0:T(8,128)(2,1)S(1)}, u32[]{:S(2)}, u32[]{:S(2)}) collective-permute-start(bf16[2,5,64,1280]{3,2,1,0:T(8,128)(2,1)} %collective-permute-done.27.refs_23_.refs_11_), channel_id=1, source_target_pairs={{0,2},{2,0},{4,6},{6,4},{8,10},{10,8},{12,14},{14,12},{16,18},{18,... | collective-permute-start | bytes 4915208 | tf_op jit(solution)/shard_map/ppermute | solution.py:1089
  227.8 40.6 %collective-permute-start.45 = (bf16[1,4,40,2560]{3,2,1,0:T(8,128)(2,1)}, bf16[1,4,40,2560]{3,2,1,0:T(8,128)(2,1)}, u32[]{:S(2)}, u32[]{:S(2)}) collective-permute-start(bf16[1,4,40,2560]{3,2,1,0:T(8,128)(2,1)} %get-tuple-element.315), channel_id=1, source_target_pairs={{0,2},{2,0},{4,6},{6,4},{8,10},{10,8},{12,14},{14,12},{16,18},{18,... | collective-permute-start | bytes 2457608 | tf_op jit(solution)/shard_map/ppermute | solution.py:1089
  228.7 80.1 %collective-permute-start.53 = (bf16[1,4,40,2560]{3,2,1,0:T(8,128)(2,1)}, bf16[1,4,40,2560]{3,2,1,0:T(8,128)(2,1)S(1)}, u32[]{:S(2)}, u32[]{:S(2)}) collective-permute-start(bf16[1,4,40,2560]{3,2,1,0:T(8,128)(2,1)} %get-tuple-element.333), channel_id=1, source_target_pairs={{0,2},{2,0},{4,6},{6,4},{8,10},{10,8},{12,14},{14,12},{16,18},{18,... | collective-permute-start | bytes 2457608 | tf_op jit(solution)/shard_map/ppermute | solution.py:1089
  260.8 48.0 %collective-permute-start.56 = (bf16[1,4,160,1280]{3,2,1,0:T(8,128)(2,1)}, bf16[1,4,160,1280]{3,2,1,0:T(8,128)(2,1)S(1)}, u32[]{:S(2)}, u32[]{:S(2)}) collective-permute-start(bf16[1,4,160,1280]{3,2,1,0:T(8,128)(2,1)} %bitcast.77), channel_id=1, source_target_pairs={{0,2},{2,0},{4,6},{6,4},{8,10},{10,8},{12,14},{14,12},{16,18},{18,... | collective-permute-start | bytes 4915208 | tf_op jit(solution)/shard_map/ppermute | solution.py:1089
  266.8 43.1 %collective-permute-start.38 = (bf16[1,4,160,1280]{3,2,1,0:T(8,128)(2,1)}, bf16[1,4,160,1280]{3,2,1,0:T(8,128)(2,1)}, u32[]{:S(2)}, u32[]{:S(2)}) collective-permute-start(bf16[1,4,160,1280]{3,2,1,0:T(8,128)(2,1)} %get-tuple-element.279.refs_27_), channel_id=1, source_target_pairs={{0,8},{2,10},{4,12},{6,14},{8,0},{10,2},{12,4},{14,6},{16,24},{18,... | collective-permute-start | bytes 4915208 | tf_op jit(solution)/shard_map/ppermute | solution.py:1089
  267.9 41.5 %collective-permute-start.37 = (bf16[1,4,40,2560]{3,2,1,0:T(8,128)(2,1)}, bf16[1,4,40,2560]{3,2,1,0:T(8,128)(2,1)}, u32[]{:S(2)}, u32[]{:S(2)}) collective-permute-start(bf16[1,4,40,2560]{3,2,1,0:T(8,128)(2,1)} %get-tuple-element.278.refs_26_), channel_id=1, source_target_pairs={{0,1},{1,0},{2,3},{3,2},{4,5},{5,4},{6,7},{7,6},{8,9},{9,8},{10,11... | collective-permute-start | bytes 2457608 | tf_op jit(solution)/shard_map/ppermute | solution.py:1093
  268.4 41.1 %collective-permute-start.36 = (bf16[1,4,40,2560]{3,2,1,0:T(8,128)(2,1)}, bf16[1,4,40,2560]{3,2,1,0:T(8,128)(2,1)S(1)}, u32[]{:S(2)}, u32[]{:S(2)}) collective-permute-start(bf16[1,4,40,2560]{3,2,1,0:T(8,128)(2,1)} %get-tuple-element.277.refs_25_), channel_id=1, source_target_pairs={{0,1},{1,0},{2,3},{3,2},{4,5},{5,4},{6,7},{7,6},{8,9},{9,8},{10,11... | collective-permute-start | bytes 2457608 | tf_op jit(solution)/shard_map/ppermute | solution.py:1093
  330.1 42.5 %collective-permute-start.43 = (bf16[1,4,40,2560]{3,2,1,0:T(8,128)(2,1)}, bf16[1,4,40,2560]{3,2,1,0:T(8,128)(2,1)S(1)}, u32[]{:S(2)}, u32[]{:S(2)}) collective-permute-start(bf16[1,4,40,2560]{3,2,1,0:T(8,128)(2,1)} %get-tuple-element.311), channel_id=1, source_target_pairs={{0,2},{2,0},{4,6},{6,4},{8,10},{10,8},{12,14},{14,12},{16,18},{18,... | collective-permute-start | bytes 2457608 | tf_op jit(solution)/shard_map/ppermute | solution.py:1089
  337.1 38.9 %collective-permute-start.48 = (bf16[1,4,160,1280]{3,2,1,0:T(8,128)(2,1)}, bf16[1,4,160,1280]{3,2,1,0:T(8,128)(2,1)S(1)}, u32[]{:S(2)}, u32[]{:S(2)}) collective-permute-start(bf16[1,4,160,1280]{3,2,1,0:T(8,128)(2,1)} %get-tuple-element.304.refs_9_), channel_id=1, source_target_pairs={{0,8},{2,10},{4,12},{6,14},{8,0},{10,2},{12,4},{14,6},{16,24},{18,... | collective-permute-start | bytes 4915208 | tf_op jit(solution)/shard_map/ppermute | solution.py:1089
  339.7 36.4 %collective-permute-start.54 = (bf16[1,4,40,2560]{3,2,1,0:T(8,128)(2,1)}, bf16[1,4,40,2560]{3,2,1,0:T(8,128)(2,1)S(1)}, u32[]{:S(2)}, u32[]{:S(2)}) collective-permute-start(bf16[1,4,40,2560]{3,2,1,0:T(8,128)(2,1)} %get-tuple-element.302.refs_7_), channel_id=1, source_target_pairs={{0,1},{1,0},{2,3},{3,2},{4,5},{5,4},{6,7},{7,6},{8,9},{9,8},{10,11... | collective-permute-start | bytes 2457608 | tf_op jit(solution)/shard_map/ppermute | solution.py:1093
  384.4 36.9 %collective-permute-start.55 = (bf16[1,4,40,2560]{3,2,1,0:T(8,128)(2,1)}, bf16[1,4,40,2560]{3,2,1,0:T(8,128)(2,1)}, u32[]{:S(2)}, u32[]{:S(2)}) collective-permute-start(bf16[1,4,40,2560]{3,2,1,0:T(8,128)(2,1)} %get-tuple-element.322.refs_9_), channel_id=1, source_target_pairs={{0,4},{2,6},{4,0},{6,2},{8,12},{10,14},{12,8},{14,10},{16,20},{18,... | collective-permute-start | bytes 2457608 | tf_op jit(solution)/shard_map/ppermute | solution.py:1089
  386.5 66.7 %collective-permute-start.57 = (bf16[1,4,160,1280]{3,2,1,0:T(8,128)(2,1)}, bf16[1,4,160,1280]{3,2,1,0:T(8,128)(2,1)S(1)}, u32[]{:S(2)}, u32[]{:S(2)}) collective-permute-start(bf16[1,4,160,1280]{3,2,1,0:T(8,128)(2,1)} %get-tuple-element.323.refs_10_), channel_id=1, source_target_pairs={{0,1},{1,0},{2,3},{3,2},{4,5},{5,4},{6,7},{7,6},{8,9},{9,8},{10,11... | collective-permute-start | bytes 4915208 | tf_op jit(solution)/shard_map/ppermute | solution.py:1093
  421.2 54.0 %collective-permute-start.67 = (bf16[1,4,40,3200]{3,2,1,0:T(8,128)(2,1)}, bf16[1,4,40,3200]{3,2,1,0:T(8,128)(2,1)}, u32[]{:S(2)}, u32[]{:S(2)}) collective-permute-start(bf16[1,4,40,3200]{3,2,1,0:T(8,128)(2,1)} %get-tuple-element.368), channel_id=1, source_target_pairs={{0,2},{2,0},{4,6},{6,4},{8,10},{10,8},{12,14},{14,12},{16,18},{18,... | collective-permute-start | bytes 3072008 | tf_op jit(solution)/shard_map/ppermute | solution.py:1089
  421.2 54.4 %collective-permute-start.74 = (bf16[1,4,40,3200]{3,2,1,0:T(8,128)(2,1)}, bf16[1,4,40,3200]{3,2,1,0:T(8,128)(2,1)}, u32[]{:S(2)}, u32[]{:S(2)}) collective-permute-start(bf16[1,4,40,3200]{3,2,1,0:T(8,128)(2,1)} %get-tuple-element.381), channel_id=1, source_target_pairs={{0,2},{2,0},{4,6},{6,4},{8,10},{10,8},{12,14},{14,12},{16,18},{18,... | collective-permute-start | bytes 3072008 | tf_op jit(solution)/shard_map/ppermute | solution.py:1089
  477.5 95.6 %collective-permute-start.49 = (bf16[512,1280]{1,0:T(8,128)(2,1)S(1)}, bf16[512,1280]{1,0:T(8,128)(2,1)}, u32[]{:S(2)}, u32[]{:S(2)}) collective-permute-start(bf16[512,1280]{1,0:T(8,128)(2,1)S(1)} %copy-done.41), channel_id=1, source_target_pairs={{0,1},{1,0},{2,3},{3,2},{4,5},{5,4},{6,7},{7,6},{8,9},{9,8},{10,11... | collective-permute-start | bytes 3932168 | tf_op jit(solution)/shard_map/ppermute | solution.py:1093
  479.3 51.9 %collective-permute-start.68 = (bf16[1,4,40,3200]{3,2,1,0:T(8,128)(2,1)}, bf16[1,4,40,3200]{3,2,1,0:T(8,128)(2,1)}, u32[]{:S(2)}, u32[]{:S(2)}) collective-permute-start(bf16[1,4,40,3200]{3,2,1,0:T(8,128)(2,1)} %get-tuple-element.338.refs_8_), channel_id=1, source_target_pairs={{0,1},{1,0},{2,3},{3,2},{4,5},{5,4},{6,7},{7,6},{8,9},{9,8},{10,11... | collective-permute-start | bytes 3072008 | tf_op jit(solution)/shard_map/ppermute | solution.py:1093
  480.8 71.5 %collective-permute-start.75 = (bf16[1,4,40,3200]{3,2,1,0:T(8,128)(2,1)}, bf16[1,4,40,3200]{3,2,1,0:T(8,128)(2,1)}, u32[]{:S(2)}, u32[]{:S(2)}) collective-permute-start(bf16[1,4,40,3200]{3,2,1,0:T(8,128)(2,1)} %get-tuple-element.337.refs_7_), channel_id=1, source_target_pairs={{0,1},{1,0},{2,3},{3,2},{4,5},{5,4},{6,7},{7,6},{8,9},{9,8},{10,11... | collective-permute-start | bytes 3072008 | tf_op jit(solution)/shard_map/ppermute | solution.py:1093
  489.6 63.8 %collective-permute-start.69 = (bf16[1,1,160,1280]{3,2,1,0:T(8,128)(2,1)}, bf16[1,1,160,1280]{3,2,1,0:T(8,128)(2,1)}, u32[]{:S(2)}, u32[]{:S(2)}) collective-permute-start(bf16[1,1,160,1280]{3,2,1,0:T(8,128)(2,1)} %get-tuple-element.365.refs_10_), channel_id=1, source_target_pairs={{0,16},{2,18},{4,20},{6,22},{8,24},{10,26},{12,28},{14,30},{16,0},... | collective-permute-start | bytes 1228808 | tf_op jit(solution)/shard_map/ppermute | solution.py:1089
  492.2 61.2 %collective-permute-start.66 = (bf16[1,4,40,1920]{3,2,1,0:T(8,128)(2,1)}, bf16[1,4,40,1920]{3,2,1,0:T(8,128)(2,1)}, u32[]{:S(2)}, u32[]{:S(2)}) collective-permute-start(bf16[1,4,40,1920]{3,2,1,0:T(8,128)(2,1)} %get-tuple-element.360.refs_9_), channel_id=1, source_target_pairs={{0,4},{2,6},{4,0},{6,2},{8,12},{10,14},{12,8},{14,10},{16,20},{18,... | collective-permute-start | bytes 1843208 | tf_op jit(solution)/shard_map/ppermute | solution.py:1089
  643.1 38.7 %collective-permute-start.100 = (bf16[4,40,5120]{2,1,0:T(8,128)(2,1)}, bf16[4,40,5120]{2,1,0:T(8,128)(2,1)}, u32[]{:S(2)}, u32[]{:S(2)}) collective-permute-start(bf16[4,40,5120]{2,1,0:T(8,128)(2,1)} %pad_maximum_fusion.1.refs_0_), channel_id=1, source_target_pairs={{0,2},{2,0},{4,6},{6,4},{8,10},{10,8},{12,14},{14,12},{16,18},{18,... | collective-permute-start | bytes 4915208 | tf_op jit(solution)/shard_map/ppermute | solution.py:1089
  665.6 37.7 %collective-permute-start.99 = (bf16[4,160,1280]{2,1,0:T(8,128)(2,1)S(1)}, bf16[4,160,1280]{2,1,0:T(8,128)(2,1)}, u32[]{:S(2)}, u32[]{:S(2)}) collective-permute-start(bf16[4,160,1280]{2,1,0:T(8,128)(2,1)S(1)} %pad_maximum_fusion.2.refs_0_), channel_id=1, source_target_pairs={{0,8},{2,10},{4,12},{6,14},{8,0},{10,2},{12,4},{14,6},{16,24},{18,... | collective-permute-start | bytes 4915208 | tf_op jit(solution)/shard_map/ppermute | solution.py:1089
  681.8 36.9 %collective-permute-start.105 = (bf16[4,40,1920]{2,1,0:T(8,128)(2,1)S(1)}, bf16[4,40,1920]{2,1,0:T(8,128)(2,1)}, u32[]{:S(2)}, u32[]{:S(2)}) collective-permute-start(bf16[4,40,1920]{2,1,0:T(8,128)(2,1)S(1)} %pad_maximum_fusion.9.refs_4_), channel_id=1, source_target_pairs={{0,2},{2,0},{4,6},{6,4},{8,10},{10,8},{12,14},{14,12},{16,18},{18,... | collective-permute-start | bytes 1843208 | tf_op jit(solution)/shard_map/ppermute | solution.py:1089
  681.8 41.1 %collective-permute-start.103 = (bf16[4,40,3200]{2,1,0:T(8,128)(2,1)}, bf16[4,40,3200]{2,1,0:T(8,128)(2,1)}, u32[]{:S(2)}, u32[]{:S(2)}) collective-permute-start(bf16[4,40,3200]{2,1,0:T(8,128)(2,1)} %copy-done), channel_id=1, source_target_pairs={{0,2},{2,0},{4,6},{6,4},{8,10},{10,8},{12,14},{14,12},{16,18},{18,... | collective-permute-start | bytes 3072008 | tf_op jit(solution)/shard_map/ppermute | solution.py:1089
  (142 other events, 2312.0 us)

commit v3 on v2

--- a/solution.py
+++ b/solution.py
@@ -383,7 +383,7 @@
         norm_ref[:, width:] = out.astype(LOW)
 
 
-def first_norm(ids, frames, params, other, after=()):
+def first_norm(ids, frames, params, other, us, after=()):
     unused, rows, width = frames.shape
     block = rows // 2
     wide = width + 128 * other
@@ -396,7 +396,7 @@
         ],
         pl.BlockSpec((block, wide), lambda i, ids: (i, 0)),
         struct((rows, wide), LOW),
-        us=4,
+        us=us,
         after=after,
     )(ids, frames, params)
 
@@ -474,25 +474,50 @@
     return (lane >= offset) & (lane < offset + size)
 
 
+PACE_TWO = 1.4426950408889634
+
+
+def lanes(count):
+    return lax.broadcasted_iota(jnp.int32, (1, count), 1)
+
+
+def free_lane(offset, size):
+    return 0 if offset >= 8 else offset + size
+
+
+def in_three(column):
+    first = column.astype(LOW)
+    rest = column - first.astype(FULL)
+    second = rest.astype(LOW)
+    return first, second, (rest - second.astype(FULL)).astype(LOW)
+
+
+def put_lanes(rows, at, columns):
+    lane = lanes(rows.shape[1])
+    for turn, column in enumerate(columns):
+        rows = jnp.where(lane == at + turn, column, rows)
+    return rows
+
+
 def attend_kernel(size, per, ids, query_ref, key_ref, value_ref, bias_ref, out_ref, total_ref, acc):
     scale = size ** (-0.5)
-    bias = bias_ref[...]
-    lane = lax.broadcasted_iota(jnp.int32, (1, 128), 1)
+    one = jnp.ones((1, 1), LOW)
+    mask = jnp.broadcast_to(bias_ref[...], (128, bias_ref.shape[1])).T[:, 0:1].astype(LOW)
     acc[...] = jnp.zeros_like(acc)
     stats = jnp.zeros((query_ref.shape[0], 128), FULL)
     for head in range(per):
         low, high, offset = window(head, size)
         inside = head_lanes(high - low, offset, size)
+        free = free_lane(offset, size)
         query = query_ref[:, low:high]
-        query = jnp.where(inside, query, jnp.zeros_like(query))
-        scores = contract(query, key_ref[:, low:high], 1, 1) * scale + bias
+        query = put_lanes(jnp.where(inside, query, jnp.zeros_like(query)), free, (one,))
+        scores = contract(query, put_lanes(key_ref[:, low:high], free, (mask,)), 1, 1)
         peak = jnp.max(scores, axis=-1, keepdims=True)
-        raised = jnp.exp(scores - peak)
+        raised = jnp.exp2((scores - peak) * (scale * PACE_TWO))
         summed = jnp.sum(raised, axis=-1, keepdims=True)
-        probs = (raised * (1.0 / summed)).astype(LOW)
-        mixed = contract(probs, value_ref[:, low:high], 1, 0)
+        mixed = contract(raised.astype(LOW), value_ref[:, low:high], 1, 0) * (1.0 / summed)
         acc[:, low:high] += jnp.where(inside, mixed, 0.0)
-        stats = jnp.where(lane == head, peak + jnp.log(summed), stats)
+        stats = jnp.where(lanes(128) == head, peak * scale + jnp.log(summed), stats)
     out_ref[...] = acc[...].astype(LOW)
     total_ref[...] = stats.T[:per]
 
@@ -1027,7 +1052,7 @@
         [pl.BlockSpec(memory_space=pl.ANY), pl.BlockSpec((tile, width), lambda i, ids: (i, 0))],
         pl.BlockSpec((1, tile, width), lambda i, ids: (1 - ids[0], i, 0)),
         struct(whole.shape, FULL),
-        us=3,
+        us=0.1,
         aliases={1: 0},
         after=after,
     )(ids, whole, part)
@@ -1035,10 +1060,9 @@
 
 def settle_up_kernel(ids, step, refs, turn, place, out_ref):
     half = out_ref.shape[2] // 2
-    rows = refs[step][turn].astype(FULL)
     for far in range(2):
         at = pl.multiple_of((ids[0] ^ far) * half, half)
-        out_ref[place, :, pl.ds(at, half)] = rows[:, far * half : (far + 1) * half]
+        out_ref[place, :, pl.ds(at, half)] = refs[4 * far + step][turn].astype(FULL)
 
 
 def settle_down_kernel(ids, step, refs, turn, place, out_ref):
@@ -1077,7 +1101,7 @@
         [const_spec(array.shape) for array in arrays],
         [pl.BlockSpec(block, functools.partial(place, rank=len(block))) for block in blocks],
         [struct(shape, FULL) for shape in shapes],
-        us=9,
+        us=0.1,
         after=after,
     )(ids, *arrays)
 
@@ -1093,52 +1117,44 @@
     return lax.ppermute(array, "fsdp", [(0, 1), (1, 0)])
 
 
-def fold_kernel(counts, ids, *refs):
-    outs = refs[sum(counts) :]
+def fold_kernel(jobs, ids, *refs):
+    outs = refs[sum(map(sum, jobs)) :]
     at = 0
-    for count, out_ref in zip(counts, outs):
-        total = refs[at][...].astype(FULL)
-        for ref in refs[at + 1 : at + count]:
-            total += ref[...].astype(FULL)
-        out_ref[...] = total.astype(LOW)
-        at += count
-
-
-def fold(ids, *jobs, after=()):
-    in_specs, arrays, out_specs, out_shape = [], [], [], []
-    moved = 0
+    for job, out_ref in zip(jobs, outs):
+        for place, count in enumerate(job):
+            total = refs[at][0].astype(FULL)
+            for ref in refs[at + 1 : at + count]:
+                total += ref[0].astype(FULL)
+            out_ref[place] = total.astype(LOW)
+            at += count
+
+
+def fold(ids, *jobs, us=6, after=()):
+    in_specs, arrays, out_specs, out_shape, counts = [], [], [], [], []
     for job in jobs:
-        for array, side, first, count in job:
-            sides, unused, rows, columns = array.shape
-            wide = sides if side is None else 1
-            base = 0 if side is None else side
-            if count % 4 == 0:
-                block = (wide, count // 4, rows, columns)
-                spec = lambda s, ids, base=base, at=first // (count // 4): (base, at + s, 0, 0)
-            elif rows % 64 == 0:
-                block = (wide, count, rows // 4, columns)
-                spec = lambda s, ids, base=base, at=first // count: (base, at, s, 0)
-            else:
-                block = (wide, count, rows, columns)
-                spec = lambda s, ids, base=base, at=first // count: (base, at, 0, 0)
-            in_specs.append(pl.BlockSpec(block, spec))
-            arrays.append(array)
-            moved += wide * count * rows * columns * 2
-        if count % 4 == 0:
-            out_specs.append(pl.BlockSpec(block, lambda s, ids: (0, s, 0, 0)))
-        elif rows % 64 == 0:
-            out_specs.append(pl.BlockSpec(block, lambda s, ids: (0, 0, s, 0)))
-        else:
-            out_specs.append(pl.BlockSpec(block, lambda s, ids: (0, 0, 0, 0)))
-        out_shape.append(struct((wide, count, rows, columns), LOW))
-        moved += wide * count * rows * columns * 2
+        job = job if isinstance(job, tuple) else (job,)
+        for terms in job:
+            for array, side, first, count in terms:
+                unused, unused, rows, columns = array.shape
+                if count % 4 == 0:
+                    block = (1, count // 4, rows, columns)
+                    spec = lambda s, ids, side=side, at=first // (count // 4): (side, at + s, 0, 0)
+                else:
+                    block = (1, count, rows, columns)
+                    spec = lambda s, ids, side=side, at=first // count: (side, at, 0, 0)
+                in_specs.append(pl.BlockSpec(block, spec))
+                arrays.append(array)
+        counts.append([len(terms) for terms in job])
+        moving = count % 4 == 0
+        out_specs.append(pl.BlockSpec((len(job),) + block[1:], lambda s, ids, moving=moving: (0, s * moving, 0, 0)))
+        out_shape.append(struct((len(job), count, rows, columns), LOW))
     return call(
-        functools.partial(fold_kernel, [len(job) for job in jobs]),
+        functools.partial(fold_kernel, counts),
         (4,),
         in_specs,
         out_specs,
         out_shape,
-        us=6,
+        us=us,
         after=after,
     )(ids, *arrays)
 
@@ -1184,15 +1200,17 @@
     )[None].astype(FULL)
     params = join(own_small, cross(own_small))
 
+    eighth_at = later((ids[1] // 2) * eighth, own_small)
+
     def piece_of(weight):
-        return lax.dynamic_slice_in_dim(weight, (ids[1] // 2) * eighth, eighth, axis=0)
+        return lax.dynamic_slice_in_dim(weight, eighth_at, eighth, axis=0)
 
     tile = 512
     tiles = w_down.shape[0] // tile
     ff_half = w_up.shape[1] // 2
     send_qkv = piece_of(w_qkv).reshape(eighth, 3, 2, half)
     q_a = cross(send_qkv[:, :, 0].reshape(eighth, 3 * half))[None]
-    send_norm = first_norm(ids, frames, params, 1)
+    send_norm = first_norm(ids, frames, params, 1, 4)
     slots = later(clip_slots, send_norm)
     slot = jnp.where(side == 0, slots[0], slots[1])
     numbers = jnp.arange(clip_lengths.shape[0], dtype=jnp.int32)
@@ -1200,7 +1218,7 @@
     place = jnp.arange(2 * rows, dtype=jnp.int32)
     place = jnp.where(place < rows, place + side * rows, place - rows + (1 - side) * rows)
     mask = jnp.where(place < span, 0.0, -1e30).astype(FULL)
-    own_norm = first_norm(ids, frames, params, 0, (send_norm,))
+    own_norm = first_norm(ids, frames, params, 0, 20, (send_norm,))
     far_norm = cross(send_norm)
     q_b = cross(send_qkv[:, :, 1].reshape(eighth, 3 * half))[None]
     q_a = later(q_a, own_norm)
@@ -1266,134 +1284,147 @@
     near0_ga, near0_gb, far0_ga, far0_gb = from_core(y, near0_a, near0_b, far0_a, far0_b)
     down0 = down0[None]
     down0_ga, down0_gb = from_core(y, down0_a[None], down0_b[None])
-    up1_xa, up1_xb, down0_z = fold(
+    up1_x, down0_z = fold(
         ids,
-        terms(0, 4, far0, far0_ga),
-        terms(4, 4, far0) + terms(0, 4, far0_gb),
+        (terms(0, 4, far0, far0_ga), terms(4, 4, far0) + terms(0, 4, far0_gb)),
         terms(4, 4, down0) + terms(0, 4, down0_gb),
     )
     output, far_out, dn, near1, near1_a, near1_b, far1, far1_a, far1_b, down1, down1_a, down1_b, bias1 = feed_rows(
         ids, 1, 2, tiles - 2, norm_f, norm_f_turned, (dout, y, dn), w_up, far_up, far_down, params,
-        grads, frames.shape, (up1_xa, up1_xb, down0_z),
-    )
-
-    up1_oa, up1_ob = later(cross(up1_xa), dn), later(cross(up1_xb), dn)
+        grads, frames.shape, (up1_x, down0_z),
+    )
+
+    def second(array):
+        return [(array, 1, 0, 4)]
+
+    up1_o = later(cross(up1_x), dn)
     down0_zg = later(swap(down0_z, NEAR_Z), dn)
     d_resid, d_mixed, *o_pieces, small_mid = middle_rows(
-        ids, dn, resid, cotangent, far_cot, mixed0, mixed1, whole_out, params, (up1_oa, up1_ob, down0_zg)
+        ids, dn, resid, cotangent, far_cot, mixed0, mixed1, whole_out, params, (up1_o, down0_zg)
     )
 
     near1_ga, near1_gb, far1_ga, far1_gb = from_core(d_mixed, near1_a, near1_b, far1_a, far1_b)
     down1 = down1[None]
     down1_ga, down1_gb = from_core(d_mixed, down1_a[None], down1_b[None])
-    up1_y, up0_xa, up0_xb, down1_z = fold(
+    up1_y, up0_x, down1_z = fold(
         ids,
-        terms(4, 4, near1) + terms(0, 4, near1_gb, up1_ob),
-        terms(0, 4, far1, far1_ga),
-        terms(4, 4, far1) + terms(0, 4, far1_gb),
+        terms(4, 4, near1) + terms(0, 4, near1_gb) + second(up1_o),
+        (terms(0, 4, far1, far1_ga), terms(4, 4, far1) + terms(0, 4, far1_gb)),
         terms(4, 4, down1) + terms(0, 4, down1_gb),
     )
-    d0 = attend_back_rows(ids, 0, qkv0, d_mixed, mask[:, None], totals0, (up1_y, up0_xa, up0_xb, down1_z))
-
-    up0_oa, up0_ob = later(cross(up0_xa), d0), later(cross(up0_xb), d0)
-    up1 = [near1, near1_ga, up1_oa, later(swap(up1_y, Y), d0)]
-    up0 = [near0, near0_ga, up0_oa]
+    d0 = attend_back_rows(ids, 0, qkv0, d_mixed, mask[:, None], totals0, (up1_y, up0_x, down1_z))
+
+    up0_o = later(cross(up0_x), d0)
+    up1 = [near1, near1_ga, up1_o, later(swap(up1_y, Y), d0)]
+    up0 = [near0, near0_ga, up0_o]
     up1_z, up0_y, down_x = fold(
         ids,
         terms(2, 2, *up1),
-        terms(4, 4, near0) + terms(0, 4, near0_gb, up0_ob),
+        terms(4, 4, near0) + terms(0, 4, near0_gb) + second(up0_o),
         terms(0, 4, down1, down1_ga, later(swap(down1_z, NEAR_Z), d0)),
     )
     q0n, q0n_a, q0n_b, q0f, q0f_a, q0f_b, small_q0 = project_grad(
         ids, norm_turned, d0, o_pieces, (up1_z, up0_y, down_x)
     )
 
-    far_out = later(far_out, q0n)
-    d1 = attend_back_rows(ids, 1, qkv1, d_mixed, mask[:, None], totals1, (far_out,), range(4))
+    d1 = attend_back_rows(ids, 1, qkv1, d_mixed, mask[:, None], totals1, (q0n,), range(4))
 
     q0n_ga, q0n_gb, q0f_ga, q0f_gb = from_core(d1, q0n_a, q0n_b, q0f_a, q0f_b)
     up1.append(later(swap(up1_z, NEAR_Z), d1))
     up0.append(later(swap(up0_y, Y), d1))
-    q0_xa, q0_xb, up1_f, up0_z = fold(
+    down = [down0, down0_ga, down0_zg, later(cross(down_x), d1)]
+    q0_xa, q0_xb, up1_f, up0_z, down_y = fold(
         ids,
+        terms(4, 4, q0f) + terms(0, 4, q0f_gb),
         terms(0, 4, q0f, q0f_ga),
-        terms(4, 4, q0f) + terms(0, 4, q0f_gb),
         terms(1, 1, *up1),
         terms(2, 2, *up0),
+        terms(2, 2, *down),
     )
     d1 = attend_back_rows(
-        ids, 1, qkv1, d_mixed, mask[:, None], totals1, (q0_xa, q0_xb, up1_f, up0_z), range(4, 8), (d1,)
-    )
-
-    down = [down0, down0_ga, down0_zg, later(cross(down_x), d1)]
+        ids, 1, qkv1, d_mixed, mask[:, None], totals1, (q0_xa, q0_xb, up1_f, up0_z, down_y), range(4, 8), (d1,)
+    )
+
     up1.append(later(swap(up1_f, FAR_Z), d1))
     up0.append(later(swap(up0_z, NEAR_Z), d1))
-    down_y, up0_f, up1 = fold(ids, terms(2, 2, *down), terms(1, 1, *up0), terms(0, 1, *up1))
-    q1n, q1n_a, q1n_b, q1f, q1f_a, q1f_b, small_q1 = project_grad(ids, norm_turned, d1, (), (down_y, up0_f, up1))
+    down.append(later(swap(down_y, Y), d1))
+    up1, up0_f, down_f = fold(ids, terms(0, 1, *up1), terms(1, 1, *up0), terms(1, 1, *down))
+    up1 = up1[0]
+    q0_oa = later(cross(q0_xa), d1)
+    q1n, q1n_a, q1n_b, q1f, q1f_a, q1f_b, small_q1 = project_grad(
+        ids, norm_turned, d1, (), (down_f, up0_f, up1, q0_oa)
+    )
 
     q1n_ga, q1n_gb, q1f_ga, q1f_gb = from_core(q1n, q1n_a, q1n_b, q1f_a, q1f_b)
-    down.append(later(swap(down_y, Y), q1n))
-    up0.append(later(swap(up0_f, FAR_Z), q1n))
-    q1_yn, q1_yf, down_f, up0 = fold(
+    q0_ob = later(cross(q0_xb), q1n)
+    q0 = [q0n, q0n_ga, q0_ob]
+    q1_x, q0_y = fold(
         ids,
-        terms(4, 4, q1n) + terms(0, 4, q1n_gb),
-        terms(4, 4, q1f) + terms(0, 4, q1f_gb),
-        terms(1, 1, *down),
+        (terms(0, 4, q1f, q1f_ga), terms(4, 4, q1f) + terms(0, 4, q1f_gb)),
+        terms(4, 4, q0n) + terms(0, 4, q0n_gb, q0_oa),
+    )
+    far_out = later(far_out, q1_x)
+    frames_grad, far_grad, small_last = last_rows(
+        ids, d0, d1, whole0, whole1, frames, far_norm, d_resid, params, (q1_x, q0_y)
+    )
+
+    q1_o = later(cross(q1_x), far_grad)
+    q1 = [q1n, q1n_ga, q1_o]
+    q0.append(later(swap(q0_y, Y), far_grad))
+    up0.append(later(swap(up0_f, FAR_Z), far_grad))
+    down.append(later(swap(down_f, FAR_Z), far_grad))
+    q1_y, *q0_z, down, up0 = fold(
+        ids,
+        terms(4, 4, q1n) + terms(0, 4, q1n_gb) + second(q1_o),
+        *[terms(at, 1, *q0) for at in (1, 2, 3)],
+        terms(0, 1, *down),
         terms(0, 1, *up0),
     )
-    up = jnp.concatenate([up0[0], up1[0]], axis=2)
-    frames_grad, far_grad, small_last = last_rows(
-        ids, d0, d1, whole0, whole1, frames, far_norm, d_resid, params, (q1_yn, q1_yf, down_f, up)
-    )
-
-    q1 = [q1n, q1n_ga, later(swap(q1_yn, Y), far_grad)]
-    q0_oa, q0_ob = later(cross(q0_xa), far_grad), later(cross(q0_xb), far_grad)
-    down.append(later(swap(down_f, FAR_Z), far_grad))
-    q0 = [q0n, q0n_ga, q0_oa]
-    q1_x, q0_y, down = fold(
-        ids,
-        terms(0, 4, q1f, q1f_ga, later(swap(q1_yf, Y), far_grad)),
-        terms(4, 4, q0n) + terms(0, 4, q0n_gb, q0_ob),
-        terms(0, 1, *down),
-    )
-    up = join(up, later(swap(up, FAR_Z), q1_x))
-    down = down[0]
-    output = fill_rows(ids, output, cross(far_out), (up,))
-
-    q1.append(later(cross(q1_x), output))
-    q1_z = fold(ids, *[terms(at, 1, *q1) for at in (1, 2, 3)])
-    far_grad = later(far_grad, q1_z[0])
-    down = join(down, later(swap(down, FAR_Z), q1_z[0]))
-
-    q0.append(later(swap(q0_y, Y), down))
-    q0_z = fold(ids, *[terms(at, 1, *q0) for at in (1, 2, 3)])
-    up = join(up, later(swap(up, NEAR_Z), q0_z[0]))
-    q1 = fold(ids, terms(0, 1, *q1) + terms(0, 1, *[later(swap(array, bit), up) for array, bit in zip(q1_z, RING)]))[0][0]
-    down = join(down, later(swap(down, Y), q1))
-    q0 = fold(ids, terms(0, 1, *q0) + terms(0, 1, *[later(swap(array, bit), down) for array, bit in zip(q0_z, RING)]))[0][0]
-    q1 = later(along_z(q1), q0)
-    up = spread_pieces(up, later(swap(up, Y), q1))
-    q0 = later(along_z(q0), up[1])
-    frames_grad = fill_rows(ids, frames_grad, cross(far_grad), (q0,))
-    q1 = spread_pieces(q1, later(swap(q1, Y), frames_grad))
-    ff = 2 * ff_half
-    block = half // 16
-    up_out, = settle(ids, 1, settle_up_kernel, list(up), [(16, block, ff)], [(4, block, ff)], after=(q1[1],))
-    down = spread_pieces(down, later(swap(down, NEAR_Z), up_out))
-    q0 = spread_pieces(q0, later(swap(q0, Y), down[1]))
-    down_out, = settle(
-        ids, 2, settle_down_kernel, list(down), [(tiles, 16, tile // 16, width)], [(tiles, 4, tile // 16, width)], 1, (q0[1],)
-    )
-
+    down, up0 = down[0], up0[0]
+    up1 = join(up1, later(swap(up1, FAR_Z), q1_y))
+    small_last = later(small_last, q1_y)
     bias_up_sum = jnp.where(side == 0, jnp.concatenate([bias0, bias1]), jnp.concatenate([bias1, bias0]))
     query_sum = jnp.concatenate([small_q0[0], small_q1[0]], axis=0)
     value_sum = jnp.concatenate([small_q0[2], small_q1[2]], axis=0)
     vectors = [small_last[0], small_last[1], query_sum, value_sum, small_mid[0], small_mid[1], small_mid[2], small_mid[3]]
     small = jnp.concatenate([v.reshape(2, half) for v in vectors] + [bias_up_sum], axis=1)
-    got = cross(lax.dynamic_slice_in_dim(small, 1 - side, 1, axis=0))
-    small = lax.dynamic_slice_in_dim(small, side, 1, axis=0) + got
-    for bit in plain:
-        small = small + swap(small, bit)
+    small_far = cross(lax.dynamic_slice_in_dim(small, 1 - side, 1, axis=0))
+    small = lax.dynamic_slice_in_dim(small, side, 1, axis=0)
+
+    q1.append(later(swap(q1_y, Y), up1))
+    q1_z = fold(ids, *[terms(at, 1, *q1) for at in (1, 2, 3)], us=0.1)
+    far_grad = later(far_grad, q1_z[0])
+    down = join(down, later(swap(down, FAR_Z), q1_z[0]))
+    up0 = join(up0, later(swap(up0, FAR_Z), q1_z[0]))
+    up1 = join(up1, later(swap(up1, NEAR_Z), q1_z[0]))
+    small = small + later(small_far, q1_z[0])
+    output = fill_rows(ids, output, cross(far_out), (down, up0, up1, small))
+    small = small + later(swap(small, CORE), output)
+
+    q0_got = [later(swap(array, bit), output) for array, bit in zip(q0_z, RING)]
+    q0 = fold(ids, terms(0, 1, *q0) + terms(0, 1, *q0_got), us=0.1, after=(small,))[0][0]
+    q1_got = [later(swap(array, bit), q0) for array, bit in zip(q1_z, RING)]
+    q1 = fold(ids, terms(0, 1, *q1) + terms(0, 1, *q1_got), us=0.1)[0][0]
+    down = join(down, later(swap(down, Y), q1))
+    up0 = join(up0, later(swap(up0, NEAR_Z), q1))
+    up1 = spread_pieces(up1, later(swap(up1, Y), q1))
+    frames_grad = fill_rows(ids, frames_grad, cross(far_grad), (down, up0))
+    small = small + later(swap(small, Y), frames_grad)
+    q0 = later(along_z(q0), frames_grad)
+    q1 = later(along_z(q1), q0)
+    up0 = spread_pieces(up0, later(swap(up0, Y), q1))
+    ff = 2 * ff_half
+    block = half // 16
+    up_out, = settle(ids, 1, settle_up_kernel, [*up0, *up1], [(16, block, ff)], [(4, block, ff)], after=(small,))
+    small = small + later(swap(small, NEAR_Z), up_out)
+    q0 = spread_pieces(q0, later(swap(q0, Y), up_out))
+    q1 = spread_pieces(q1, later(swap(q1, Y), up_out))
+    down = spread_pieces(down, later(swap(down, NEAR_Z), q1[1]))
+    down_out, = settle(
+        ids, 2, settle_down_kernel, list(down), [(tiles, 16, tile // 16, width)], [(tiles, 4, tile // 16, width)], 1, (q0[1], small)
+    )
+    small = small + later(swap(small, FAR_Z), down_out)
+
     small = small[0]
     parts = [small[k * half : (k + 1) * half] for k in range(8)] + [small[8 * half :]]
 

time: 751 us -> 726 us (0.967)
  starting transfers between devices: 98.7 us -> 84.4 us
  waiting for transfers between devices: 139 us -> 128 us
    ppermute x20 -> x18, waiting for transfers between devices: 42.8 us -> 8.37 us  [cross(): return lax.ppermute(array, 'fsdp', [(0, 1), (1, 0)])]
    ppermute x89 -> x93, waiting for transfers between devices: 96.3 us -> 120 us  [swap(): return lax.ppermute(array, 'rep', [(at, at ^ bit) for at in range(16)])]
    ppermute x20 -> x18, starting transfers between devices: 24.6 us -> 17.4 us  [cross(): return lax.ppermute(array, 'fsdp', [(0, 1), (1, 0)])]
    pallas_call x34 -> x33, Pallas kernels: 452 us -> 445 us  [call(): return lambda *args: run(*args, *after)]
    ppermute x89 -> x93, starting transfers between devices: 74.1 us -> 67 us  [swap(): return lax.ppermute(array, 'rep', [(at, at ^ bit) for at in range(16)])]
    unnamed x147 -> x169, local copies, waits for them, and re-layouts: 14.9 us -> 19.4 us
  transfers between devices with their start and end apart: 109 -> 111, of which waited for: 28 -> 26; matrix products, arithmetic and copies ran while one was open for 4% -> 5% of each run, Pallas kernels for 59% -> 61%
where the time goes in v3:
time: 726 us; the launch traced here: 720 us
  Pallas kernels  445 us (61%)
  waiting for transfers between devices  128 us (18%)
  starting transfers between devices  84.4 us (12%)
  local copies, waits for them, and re-layouts  36.7 us (5%)
  other arithmetic  23 us (3%)
    pallas_call x33, Pallas kernels, call(): return lambda *args: run(*args, *after)  445 us
    ppermute x93, waiting for transfers between devices, swap(): return lax.ppermute(array, 'rep', [(at, at ^ bit) for at in range(16)])  120 us
    ppermute x93, starting transfers between devices, swap(): return lax.ppermute(array, 'rep', [(at, at ^ bit) for at in range(16)])  67 us
    unnamed x169, local copies, waits for them, and re-layouts  19.4 us
    ppermute x18, starting transfers between devices, cross(): return lax.ppermute(array, 'fsdp', [(0, 1), (1, 0)])  17.4 us
  transfers between devices with their start and end apart: 111, of which 26 were waited for; matrix products, arithmetic and copies ran while one was open for 5% of the time, Pallas kernels for 61%

profile of v3, /device:TPU:0, one launch (start us, length us, event | category | flops | bytes accessed | tf_op | source)
XLA Modules:
  0.0 720.3 jit_solution(1662725716591659430)
XLA Ops:
  40.2 8.9 %collective-permute-done.4.refs_4_ = bf16[2,80,1920]{2,1,0:T(8,128)(2,1)} collective-permute-done((bf16[2,80,1920]{2,1,0:T(8,128)(2,1)}, bf16[2,80,1920]{2,1,0:T(8,128)(2,1)}, u32[]{:S(2)}, u32[]{:S(2)}) %collective-permute-start.4) | collective-permute-done | bytes 614432 | tf_op jit(solution)/shard_map/ppermute | solution.py:1113
  64.8 12.7 %shard_map.282 = (bf16[1024,1920]{1,0:T(8,128)(2,1)}, bf16[1280,1920]{1,0:T(8,128)(2,1)}, bf16[1280,1024]{1,0:T(8,128)(2,1)}) custom-call(s32[4]{0:T(128)} %pad_add_fusion.ids, bf16[512,1280]{1,0:T(8,128)(2,1)} %shard_map.281.refs_0_, bf16[512,1408]{1,0:T(8,128)(2,1)} %collective-permute-done.1.refs_1_.refs_8_.refs_5_, bf16[640,3840]{1,0:T(8,128)(2,1)} %refs_2_.6, ...), custom_call_target="tpu_custom_call" | custom-call | flops 13799999488 | tf_op jit(solution)/shard_map/pallas_call | solution.py:339
  79.6 16.3 %shard_map.283 = (bf16[1024,640]{1,0:T(8,128)(2,1)}, f32[8,1024]{1,0:T(8,128)}) custom-call(s32[4]{0:T(128)} %pad_add_fusion.ids, bf16[1024,1920]{1,0:T(8,128)(2,1)} %get-tuple-element.223.refs_0_.refs_1_.refs_2_, bf16[1024,1920]{1,0:T(8,128)(2,1)} %get-tuple-element.223.refs_0_.refs_1_.refs_2_, ...), custom_call_target="tpu_custom_call" | custom-call | flops 21849999360 | tf_op jit(solution)/shard_map/pallas_call | solution.py:339
  100.6 11.6 %shard_map.284 = (bf16[1024,1920]{1,0:T(8,128)(2,1)}, bf16[1280,1920]{1,0:T(8,128)(2,1)}) custom-call(s32[4]{0:T(128)} %pad_add_fusion.ids, bf16[512,1280]{1,0:T(8,128)(2,1)} %shard_map.281.refs_0_, bf16[512,1408]{1,0:T(8,128)(2,1)} %collective-permute-done.1.refs_1_.refs_8_.refs_5_, bf16[640,3840]{1,0:T(8,128)(2,1)} %refs_2_.6, ...), custom_call_target="tpu_custom_call" | custom-call | flops 13799999488 | tf_op jit(solution)/shard_map/pallas_call | solution.py:339
  117.2 16.2 %shard_map.285 = (bf16[1024,640]{1,0:T(8,128)(2,1)}, f32[8,1024]{1,0:T(8,128)}) custom-call(s32[4]{0:T(128)} %pad_add_fusion.ids, bf16[1024,1920]{1,0:T(8,128)(2,1)} %get-tuple-element.232.refs_0_.refs_1_.refs_2_, bf16[1024,1920]{1,0:T(8,128)(2,1)} %get-tuple-element.232.refs_0_.refs_1_.refs_2_, ...), custom_call_target="tpu_custom_call" | custom-call | flops 21849999360 | tf_op jit(solution)/shard_map/pallas_call | solution.py:339
  139.7 12.6 %shard_map.286 = (f32[1024,1280]{1,0:T(8,128)}, bf16[1024,1280]{1,0:T(8,128)(2,1)}, bf16[1280,1024]{1,0:T(8,128)(2,1)}, bf16[1280,1280]{1,0:T(8,128)(2,1)}) custom-call(s32[4]{0:T(128)} %pad_add_fusion.ids, bf16[1024,640]{1,0:T(8,128)(2,1)} %get-tuple-element.228.refs_0_.refs_4_, bf16[1024,640]{1,0:T(8,128)(2,1)} %get-tuple-element.236.refs_1_.refs_5_, ...), custom_call_target="tpu_custom_call" | custom-call | flops 13799999488 | tf_op jit(solution)/shard_map/pallas_call | solution.py:339
  154.0 30.1 %shard_map.287 = (bf16[1024,1280]{1,0:T(8,128)(2,1)}, f32[1024,1280]{1,0:T(8,128)}, f32[1024,1280]{1,0:T(8,128)}, bf16[1,8,40,2560]{3,2,1,0:T(8,128)(2,1)}, bf16...) custom-call(s32[4]{0:T(128)} %pad_add_fusion.ids, ...), custom_call_target="tpu_custom_call" | custom-call | flops 29899999232 | tf_op jit(solution)/shard_map/pallas_call | solution.py:339
  186.9 37.0 %shard_map.288 = (f32[1024,1280]{1,0:T(8,128)}, f32[1024,1280]{1,0:T(8,128)}, bf16[1,8,40,2560]{3,2,1,0:T(8,128)(2,1)}, bf16[1,4,40,2560]{3,2,1,0:T(8,128)(2,1)}...) custom-call(s32[4]{0:T(128)} %pad_add_fusion.ids, ...), custom_call_target="tpu_custom_call", output_to_operand_aliasing={{2}: (13, {}), {3}: (14, {}), {4}: (15, {}), {5}: (16, {}),... | custom-call | flops 43124998144 | tf_op jit(solution)/shard_map/pallas_call | solution.py:339
  227.9 29.6 %shard_map.289 = (f32[1024,1280]{1,0:T(8,128)}, f32[1024,1280]{1,0:T(8,128)}, bf16[1,8,40,2560]{3,2,1,0:T(8,128)(2,1)}, bf16[1,4,40,2560]{3,2,1,0:T(8,128)(2,1)}...) custom-call(s32[4]{0:T(128)} %pad_add_fusion.ids, ...), custom_call_target="tpu_custom_call" | custom-call | flops 29899999232 | tf_op jit(solution)/shard_map/pallas_call | solution.py:339
  258.8 6.0 shard_map.290
  266.8 39.0 %shard_map.291 = (f32[2,512,1280]{2,1,0:T(8,128)}, bf16[512,1280]{1,0:T(8,128)(2,1)}, f32[1024,1280]{1,0:T(8,128)}, bf16[1,8,40,2560]{3,2,1,0:T(8,128)(2,1)}, bf...) custom-call(s32[4]{0:T(128)} %pad_add_fusion.ids, ...), custom_call_target="tpu_custom_call", output_to_operand_aliasing={{3}: (16, {}), {4}: (17, {}), {5}: (18, {}), {6}: (19, {}),... | custom-call | flops 43124998144 | tf_op jit(solution)/shard_map/pallas_call | solution.py:339
  307.8 19.5 %shard_map.292 = (f32[1024,1280]{1,0:T(8,128)}, bf16[1024,1280]{1,0:T(8,128)(2,1)}, bf16[1,8,40,1280]{3,2,1,0:T(8,128)(2,1)}, bf16[1,4,40,1280]{3,2,1,0:T(8,128)...) custom-call(s32[4]{0:T(128)} %pad_add_fusion.ids, ...), custom_call_target="tpu_custom_call" | custom-call | flops 23000000512 | tf_op jit(solution)/shard_map/pallas_call | solution.py:339
  328.0 6.8 shard_map.293
  337.8 31.5 %shard_map.294.refs_1_.refs_0_ = bf16[1024,1920]{1,0:T(8,128)(2,1)} custom-call(s32[4]{0:T(128)} %pad_add_fusion.ids, bf16[1024,1920]{1,0:T(8,128)(2,1)} %get-tuple-element.223.refs_0_.refs_1_.refs_2_, bf16[1024,1920]{1,0:T(8,128)(2,1)} %get-tuple-element.223.refs_0_.refs_1_.refs_2_, bf16[1024,1920]{1,0:T(8,128)(2,1)} %get-tuple-element.223.refs_0_.refs_1_.refs_2_, ...), custom_call_target="tpu_custom_call" | custom-call | flops 35649998848 | tf_op jit(solution)/shard_map/pallas_call | solution.py:339
  375.2 7.1 shard_map.295
  384.7 14.6 %shard_map.296 = (bf16[1,8,40,3200]{3,2,1,0:T(8,128)(2,1)}, bf16[1,4,40,3200]{3,2,1,0:T(8,128)(2,1)}, bf16[1,4,40,3200]{3,2,1,0:T(8,128)(2,1)}, bf16[1,8,40,3200...) custom-call(s32[4]{0:T(128)} %pad_add_fusion.ids, ...), custom_call_target="tpu_custom_call" | custom-call | flops 12650000384 | tf_op jit(solution)/shard_map/pallas_call | solution.py:339
  399.9 18.9 %shard_map.297.refs_6_ = bf16[1024,1920]{1,0:T(8,128)(2,1)} custom-call(s32[4]{0:T(128)} %pad_add_fusion.ids, bf16[1024,1920]{1,0:T(8,128)(2,1)} %get-tuple-element.232.refs_0_.refs_1_.refs_2_, bf16[1024,1920]{1,0:T(8,128)(2,1)} %get-tuple-element.232.refs_0_.refs_1_.refs_2_, bf16[1024,1920]{1,0:T(8,128)(2,1)} %get-tuple-element.232.refs_0_.refs_1_.refs_2_, ...), custom_call_target="tpu_custom_call" | custom-call | flops 17824999424 | tf_op jit(solution)/shard_map/pallas_call | solution.py:339
  420.4 8.9 %shard_map.298 = (bf16[1,4,40,3200]{3,2,1,0:T(8,128)(2,1)}, bf16[1,4,40,3200]{3,2,1,0:T(8,128)(2,1)}, bf16[1,1,40,2560]{3,2,1,0:T(8,128)(2,1)}, bf16[1,2,40,2560...) custom-call(s32[4]{0:T(128)} %pad_add_fusion.ids, bf16[1,8,40,3200]{3,2,1,0:T(8,128)(2,1)} %get-tuple-element.328.refs_0_.refs_2_, ...), custom_call_target="tpu_custom_call" | custom-call | flops 6899999744 | tf_op jit(solution)/shard_map/pallas_call | solution.py:339
  435.8 20.2 %shard_map.299.refs_1_ = bf16[1024,1920]{1,0:T(8,128)(2,1)} custom-call(s32[4]{0:T(128)} %pad_add_fusion.ids, bf16[1024,1920]{1,0:T(8,128)(2,1)} %get-tuple-element.232.refs_0_.refs_1_.refs_2_, bf16[1024,1920]{1,0:T(8,128)(2,1)} %get-tuple-element.232.refs_0_.refs_1_.refs_2_, bf16[1024,1920]{1,0:T(8,128)(2,1)} %get-tuple-element.232.refs_0_.refs_1_.refs_2_, ...), custom_call_target="tpu_custom_call" | custom-call | flops 17824999424 | tf_op jit(solution)/shard_map/pallas_call | solution.py:339
  457.7 6.0 shard_map.300
  463.8 11.4 %shard_map.301 = (bf16[1,8,40,1920]{3,2,1,0:T(8,128)(2,1)}, bf16[1,4,40,1920]{3,2,1,0:T(8,128)(2,1)}, bf16[1,4,40,1920]{3,2,1,0:T(8,128)(2,1)}, bf16[1,8,40,1920...) custom-call(s32[4]{0:T(128)} %pad_add_fusion.ids, ...), custom_call_target="tpu_custom_call" | custom-call | flops 12650000384 | tf_op jit(solution)/shard_map/pallas_call | solution.py:339
  490.4 23.0 %shard_map.303 = (f32[2,512,1280]{2,1,0:T(8,128)}, bf16[512,1280]{1,0:T(8,128)(2,1)}, f32[8,1280]{1,0:T(8,128)}) custom-call(s32[4]{0:T(128)} %pad_add_fusion.ids, bf16[1024,1920]{1,0:T(8,128)(2,1)} %shard_map.294.refs_1_.refs_0_, bf16[1024,1920]{1,0:T(8,128)(2,1)} %shard_map.299.refs_1_, bf16[1280,1920]{1,0:T(8,128)(2,1)} %get-tuple-element.364.refs_2_, ...), custom_call_target="tpu_custom_call" | custom-call | flops 25300000768 | tf_op jit(solution)/shard_map/pallas_call | solution.py:339
  520.3 8.5 %shard_map.304 = (bf16[1,4,40,1920]{3,2,1,0:T(8,128)(2,1)}, bf16[1,1,40,3200]{3,2,1,0:T(8,128)(2,1)}, bf16[1,1,40,3200]{3,2,1,0:T(8,128)(2,1)}, bf16[1,1,40,3200...) custom-call(s32[4]{0:T(128)} %pad_add_fusion.ids, ...), custom_call_target="tpu_custom_call" | custom-call | flops 6899999744 | tf_op jit(solution)/shard_map/pallas_call | solution.py:339
  553.5 21.2 %collective-permute-done.70 = bf16[1,160,1280]{2,1,0:T(8,128)(2,1)S(1)} collective-permute-done((bf16[1,160,1280]{2,1,0:T(8,128)(2,1)}, bf16[1,160,1280]{2,1,0:T(8,128)(2,1)S(1)}, u32[]{:S(2)}, u32[]{:S(2)}) %collective-permute-start.70) | collective-permute-done | bytes 409632 | tf_op jit(solution)/shard_map/ppermute | solution.py:1113
  601.3 10.8 %collective-permute-done.79.refs_4_ = bf16[1,1,40,1920]{3,2,1,0:T(8,128)(2,1)S(1)} collective-permute-done((bf16[1,1,40,1920]{3,2,1,0:T(8,128)(2,1)S(1)}, bf16[1,1,40,1920]{3,2,1,0:T(8,128)(2,1)S(1)}, u32[]{:S(2)}, u32[]{:S(2)}) %collective-permute-start.79) | collective-permute-done | bytes 153632 | tf_op jit(solution)/shard_map/ppermute | solution.py:1113
  621.1 8.7 %collective-permute-done.94 = bf16[1,40,3200]{2,1,0:T(8,128)(2,1)S(1)} collective-permute-done((bf16[1,40,3200]{2,1,0:T(8,128)(2,1)S(1)}, bf16[1,40,3200]{2,1,0:T(8,128)(2,1)S(1)}, u32[]{:S(2)}, u32[]{:S(2)}) %collective-permute-start.94) | collective-permute-done | bytes 256032 | tf_op jit(solution)/shard_map/ppermute | solution.py:1113
  632.7 7.7 %collective-permute-done.90 = bf16[1,40,1920]{2,1,0:T(8,128)(2,1)S(1)} collective-permute-done((bf16[1,40,1920]{2,1,0:T(8,128)(2,1)}, bf16[1,40,1920]{2,1,0:T(8,128)(2,1)S(1)}, u32[]{:S(2)}, u32[]{:S(2)}) %collective-permute-start.90) | collective-permute-done | bytes 153632 | tf_op jit(solution)/shard_map/ppermute | solution.py:1113
  649.1 5.9 collective-permute-done.89.refs_1_
  659.0 8.7 %shard_map.310 = f32[16,40,5120]{2,1,0:T(8,128)} custom-call(s32[4]{0:T(128)} %pad_add_fusion.ids, bf16[4,40,2560]{2,1,0:T(8,128)(2,1)} %copy-done.8, bf16[4,40,2560]{2,1,0:T(8,128)(2,1)} %collective-permute-done.89.refs_1_, bf16[4,40,2560]{2,1,0:T(8,128)(2,1)} %collective-permute-done.96.refs_2_, bf16[4,40,2560]{2,1,0:T(8,128)(2,1)} %collective-permute-done.97.refs_3_, ...), custom_call_target="tpu_custom_call" | custom-call | flops 115000000 | tf_op jit(solution)/shard_map/pallas_call | solution.py:339
  675.9 17.6 %collective-permute-done.106.refs_4_.refs_1_ = bf16[4,40,3200]{2,1,0:T(8,128)(2,1)S(1)} collective-permute-done((bf16[4,40,3200]{2,1,0:T(8,128)(2,1)}, bf16[4,40,3200]{2,1,0:T(8,128)(2,1)S(1)}, u32[]{:S(2)}, u32[]{:S(2)}) %collective-permute-start.106) | collective-permute-done | bytes 1024032 | tf_op jit(solution)/shard_map/ppermute | solution.py:1113
  699.5 8.6 %shard_map.312 = (f32[16,40,3840]{2,1,0:T(8,128)}, f32[16,40,1280]{2,1,0:T(8,128)}) custom-call(s32[4]{0:T(128)} %pad_add_fusion.ids, bf16[4,40,3200]{2,1,0:T(8,128)(2,1)} %pad_maximum_fusion.2.refs_0_, bf16[4,40,3200]{2,1,0:T(8,128)(2,1)} %copy-done.9, bf16[4,40,3200]{2,1,0:T(8,128)(2,1)} %collective-permute-done.107.refs_2_, ...), custom_call_target="tpu_custom_call" | custom-call | flops 115000000 | tf_op jit(solution)/shard_map/pallas_call | solution.py:339
  709.4 8.7 %shard_map.311 = f32[5,16,32,1280]{3,2,1,0:T(8,128)} custom-call(s32[4]{0:T(128)} %pad_add_fusion.ids, bf16[4,160,1280]{2,1,0:T(8,128)(2,1)} %copy-done.4, bf16[4,160,1280]{2,1,0:T(8,128)(2,1)} %collective-permute-done.102.refs_1_, bf16[4,160,1280]{2,1,0:T(8,128)(2,1)} %collective-permute-done.104.refs_2_, bf16[4,160,1280]{2,1,0:T(8,128)(2,1)} %copy-done.19, ...), custom_call_target="tpu_custom_call" | custom-call | flops 115000000 | tf_op jit(solution)/shard_map/pallas_call | solution.py:339
  (442 shorter events, 222.7 us)
Async XLA Ops:
  14.7 35.4 %collective-permute-start.7 = (bf16[80,1920]{1,0:T(8,128)(2,1)S(1)}, bf16[80,1920]{1,0:T(8,128)(2,1)S(1)}, u32[]{:S(2)}, u32[]{:S(2)}) collective-permute-start(bf16[80,1920]{1,0:T(8,128)(2,1)S(1)} %bitcast.80), channel_id=1, source_target_pairs={{0,1},{1,0},{2,3},{3,2},{4,5},{5,4},{6,7},{7,6},{8,9},{9,8},{10,11... | collective-permute-start | bytes 921608 | tf_op jit(solution)/shard_map/ppermute | solution.py:1117
  62.7 37.0 %collective-permute-start.11 = (bf16[2,80,1920]{2,1,0:T(8,128)(2,1)S(1)}, bf16[2,80,1920]{2,1,0:T(8,128)(2,1)}, u32[]{:S(2)}, u32[]{:S(2)}) collective-permute-start(bf16[2,80,1920]{2,1,0:T(8,128)(2,1)S(1)} %pad_maximum_fusion.8.refs_10_.refs_3_), channel_id=1, source_target_pairs={{0,2},{2,0},{4,6},{6,4},{8,10},{10,8},{12,14},{14,12},{16,18},{18,... | collective-permute-start | bytes 1843208 | tf_op jit(solution)/shard_map/ppermute | solution.py:1113
  79.1 36.6 %collective-permute-start.17 = (bf16[5,64,1280]{2,1,0:T(8,128)(2,1)S(1)}, bf16[5,64,1280]{2,1,0:T(8,128)(2,1)}, u32[]{:S(2)}, u32[]{:S(2)}) collective-permute-start(bf16[5,64,1280]{2,1,0:T(8,128)(2,1)S(1)} %dynamic-slice_bitcast_fusion.refs_6_), channel_id=1, source_target_pairs={{0,1},{1,0},{2,3},{3,2},{4,5},{5,4},{6,7},{7,6},{8,9},{9,8},{10,11... | collective-permute-start | bytes 2457608 | tf_op jit(solution)/shard_map/ppermute | solution.py:1117
  96.0 56.5 %collective-permute-start.22 = (bf16[512,1280]{1,0:T(8,128)(2,1)S(1)}, bf16[512,1280]{1,0:T(8,128)(2,1)}, u32[]{:S(2)}, u32[]{:S(2)}) collective-permute-start(bf16[512,1280]{1,0:T(8,128)(2,1)S(1)} %fusion.refs_10_), channel_id=1, source_target_pairs={{0,1},{1,0},{2,3},{3,2},{4,5},{5,4},{6,7},{7,6},{8,9},{9,8},{10,11... | collective-permute-start | bytes 3932168 | tf_op jit(solution)/shard_map/ppermute | solution.py:1117
  100.6 37.9 %collective-permute-start.18 = (bf16[2,80,1280]{2,1,0:T(8,128)(2,1)}, bf16[2,80,1280]{2,1,0:T(8,128)(2,1)}, u32[]{:S(2)}, u32[]{:S(2)}) collective-permute-start(bf16[2,80,1280]{2,1,0:T(8,128)(2,1)} %pad_maximum_fusion.10.refs_8_.refs_3_), channel_id=1, source_target_pairs={{0,2},{2,0},{4,6},{6,4},{8,10},{10,8},{12,14},{14,12},{16,18},{18,... | collective-permute-start | bytes 1228808 | tf_op jit(solution)/shard_map/ppermute | solution.py:1113
  138.6 47.7 %collective-permute-start.27 = (bf16[2,5,64,1280]{3,2,1,0:T(8,128)(2,1)S(1)}, bf16[2,5,64,1280]{3,2,1,0:T(8,128)(2,1)}, u32[]{:S(2)}, u32[]{:S(2)}) collective-permute-start(bf16[2,5,64,1280]{3,2,1,0:T(8,128)(2,1)S(1)} %pad_maximum_fusion.refs_11_.refs_10_), channel_id=1, source_target_pairs={{0,4},{2,6},{4,0},{6,2},{8,12},{10,14},{12,8},{14,10},{16,20},{18,... | collective-permute-start | bytes 4915208 | tf_op jit(solution)/shard_map/ppermute | solution.py:1113
  152.3 73.8 %collective-permute-start.31 = (bf16[2,5,64,1280]{3,2,1,0:T(8,128)(2,1)}, bf16[2,5,64,1280]{3,2,1,0:T(8,128)(2,1)}, u32[]{:S(2)}, u32[]{:S(2)}) collective-permute-start(bf16[2,5,64,1280]{3,2,1,0:T(8,128)(2,1)} %copy-done.13), channel_id=1, source_target_pairs={{0,2},{2,0},{4,6},{6,4},{8,10},{10,8},{12,14},{14,12},{16,18},{18,... | collective-permute-start | bytes 4915208 | tf_op jit(solution)/shard_map/ppermute | solution.py:1113
  185.2 38.7 %collective-permute-start.28 = (bf16[2,80,2560]{2,1,0:T(8,128)(2,1)S(1)}, bf16[2,80,2560]{2,1,0:T(8,128)(2,1)}, u32[]{:S(2)}, u32[]{:S(2)}) collective-permute-start(bf16[2,80,2560]{2,1,0:T(8,128)(2,1)S(1)} %pad_maximum_fusion.4.refs_22_.refs_6_), channel_id=1, source_target_pairs={{0,4},{2,6},{4,0},{6,2},{8,12},{10,14},{12,8},{14,10},{16,20},{18,... | collective-permute-start | bytes 2457608 | tf_op jit(solution)/shard_map/ppermute | solution.py:1113
  186.3 39.6 %collective-permute-start.29 = (bf16[2,80,2560]{2,1,0:T(8,128)(2,1)S(1)}, bf16[2,80,2560]{2,1,0:T(8,128)(2,1)}, u32[]{:S(2)}, u32[]{:S(2)}) collective-permute-start(bf16[2,80,2560]{2,1,0:T(8,128)(2,1)S(1)} %pad_maximum_fusion.4.refs_22_.refs_6_), channel_id=1, source_target_pairs={{0,2},{2,0},{4,6},{6,4},{8,10},{10,8},{12,14},{14,12},{16,18},{18,... | collective-permute-start | bytes 2457608 | tf_op jit(solution)/shard_map/ppermute | solution.py:1113
  186.3 40.3 %collective-permute-start.32 = (bf16[2,5,64,1280]{3,2,1,0:T(8,128)(2,1)}, bf16[2,5,64,1280]{3,2,1,0:T(8,128)(2,1)S(1)}, u32[]{:S(2)}, u32[]{:S(2)}) collective-permute-start(bf16[2,5,64,1280]{3,2,1,0:T(8,128)(2,1)} %collective-permute-done.27.refs_23_.refs_11_), channel_id=1, source_target_pairs={{0,2},{2,0},{4,6},{6,4},{8,10},{10,8},{12,14},{14,12},{16,18},{18,... | collective-permute-start | bytes 4915208 | tf_op jit(solution)/shard_map/ppermute | solution.py:1113
  226.5 79.3 %collective-permute-start.44 = (bf16[1,4,40,2560]{3,2,1,0:T(8,128)(2,1)}, bf16[1,4,40,2560]{3,2,1,0:T(8,128)(2,1)}, u32[]{:S(2)}, u32[]{:S(2)}) collective-permute-start(bf16[1,4,40,2560]{3,2,1,0:T(8,128)(2,1)} %get-tuple-element.318), channel_id=1, source_target_pairs={{0,2},{2,0},{4,6},{6,4},{8,10},{10,8},{12,14},{14,12},{16,18},{18,... | collective-permute-start | bytes 2457608 | tf_op jit(solution)/shard_map/ppermute | solution.py:1113
  227.5 78.4 %collective-permute-start.53 = (bf16[1,4,160,1280]{3,2,1,0:T(8,128)(2,1)}, bf16[1,4,160,1280]{3,2,1,0:T(8,128)(2,1)S(1)}, u32[]{:S(2)}, u32[]{:S(2)}) collective-permute-start(bf16[1,4,160,1280]{3,2,1,0:T(8,128)(2,1)} %bitcast.89), channel_id=1, source_target_pairs={{0,2},{2,0},{4,6},{6,4},{8,10},{10,8},{12,14},{14,12},{16,18},{18,... | collective-permute-start | bytes 4915208 | tf_op jit(solution)/shard_map/ppermute | solution.py:1113
  257.6 48.8 %collective-permute-start.51 = (bf16[1,4,40,2560]{3,2,1,0:T(8,128)(2,1)}, bf16[1,4,40,2560]{3,2,1,0:T(8,128)(2,1)S(1)}, u32[]{:S(2)}, u32[]{:S(2)}) collective-permute-start(bf16[1,4,40,2560]{3,2,1,0:T(8,128)(2,1)} %get-tuple-element.334), channel_id=1, source_target_pairs={{0,2},{2,0},{4,6},{6,4},{8,10},{10,8},{12,14},{14,12},{16,18},{18,... | collective-permute-start | bytes 2457608 | tf_op jit(solution)/shard_map/ppermute | solution.py:1113
  264.8 41.7 %collective-permute-start.37 = (bf16[1,4,160,1280]{3,2,1,0:T(8,128)(2,1)}, bf16[1,4,160,1280]{3,2,1,0:T(8,128)(2,1)S(1)}, u32[]{:S(2)}, u32[]{:S(2)}) collective-permute-start(bf16[1,4,160,1280]{3,2,1,0:T(8,128)(2,1)} %get-tuple-element.283.refs_26_), channel_id=1, source_target_pairs={{0,8},{2,10},{4,12},{6,14},{8,0},{10,2},{12,4},{14,6},{16,24},{18,... | collective-permute-start | bytes 4915208 | tf_op jit(solution)/shard_map/ppermute | solution.py:1113
  265.3 41.6 %collective-permute-start.36 = (bf16[2,4,40,2560]{3,2,1,0:T(8,128)(2,1)}, bf16[2,4,40,2560]{3,2,1,0:T(8,128)(2,1)}, u32[]{:S(2)}, u32[]{:S(2)}) collective-permute-start(bf16[2,4,40,2560]{3,2,1,0:T(8,128)(2,1)} %get-tuple-element.282.refs_25_), channel_id=1, source_target_pairs={{0,1},{1,0},{2,3},{3,2},{4,5},{5,4},{6,7},{7,6},{8,9},{9,8},{10,11... | collective-permute-start | bytes 4915208 | tf_op jit(solution)/shard_map/ppermute | solution.py:1117
  306.9 62.4 %collective-permute-start.46 = (bf16[1,4,160,1280]{3,2,1,0:T(8,128)(2,1)}, bf16[1,4,160,1280]{3,2,1,0:T(8,128)(2,1)}, u32[]{:S(2)}, u32[]{:S(2)}) collective-permute-start(bf16[1,4,160,1280]{3,2,1,0:T(8,128)(2,1)} %bitcast.87), channel_id=1, source_target_pairs={{0,2},{2,0},{4,6},{6,4},{8,10},{10,8},{12,14},{14,12},{16,18},{18,... | collective-permute-start | bytes 4915208 | tf_op jit(solution)/shard_map/ppermute | solution.py:1113
  327.4 41.9 %collective-permute-start.42 = (bf16[1,4,40,2560]{3,2,1,0:T(8,128)(2,1)}, bf16[1,4,40,2560]{3,2,1,0:T(8,128)(2,1)S(1)}, u32[]{:S(2)}, u32[]{:S(2)}) collective-permute-start(bf16[1,4,40,2560]{3,2,1,0:T(8,128)(2,1)} %get-tuple-element.314), channel_id=1, source_target_pairs={{0,2},{2,0},{4,6},{6,4},{8,10},{10,8},{12,14},{14,12},{16,18},{18,... | collective-permute-start | bytes 2457608 | tf_op jit(solution)/shard_map/ppermute | solution.py:1113
  334.8 37.9 %collective-permute-start.47 = (bf16[1,4,160,1280]{3,2,1,0:T(8,128)(2,1)}, bf16[1,4,160,1280]{3,2,1,0:T(8,128)(2,1)S(1)}, u32[]{:S(2)}, u32[]{:S(2)}) collective-permute-start(bf16[1,4,160,1280]{3,2,1,0:T(8,128)(2,1)} %get-tuple-element.307.refs_8_), channel_id=1, source_target_pairs={{0,8},{2,10},{4,12},{6,14},{8,0},{10,2},{12,4},{14,6},{16,24},{18,... | collective-permute-start | bytes 4915208 | tf_op jit(solution)/shard_map/ppermute | solution.py:1113
  336.3 37.7 %collective-permute-start.45 = (bf16[2,4,40,2560]{3,2,1,0:T(8,128)(2,1)}, bf16[2,4,40,2560]{3,2,1,0:T(8,128)(2,1)S(1)}, u32[]{:S(2)}, u32[]{:S(2)}) collective-permute-start(bf16[2,4,40,2560]{3,2,1,0:T(8,128)(2,1)} %get-tuple-element.306.refs_7_), channel_id=1, source_target_pairs={{0,1},{1,0},{2,3},{3,2},{4,5},{5,4},{6,7},{7,6},{8,9},{9,8},{10,11... | collective-permute-start | bytes 4915208 | tf_op jit(solution)/shard_map/ppermute | solution.py:1117
  382.3 36.8 %collective-permute-start.54 = (bf16[1,4,160,1280]{3,2,1,0:T(8,128)(2,1)}, bf16[1,4,160,1280]{3,2,1,0:T(8,128)(2,1)S(1)}, u32[]{:S(2)}, u32[]{:S(2)}) collective-permute-start(bf16[1,4,160,1280]{3,2,1,0:T(8,128)(2,1)} %get-tuple-element.326.refs_10_), channel_id=1, source_target_pairs={{0,1},{1,0},{2,3},{3,2},{4,5},{5,4},{6,7},{7,6},{8,9},{9,8},{10,11... | collective-permute-start | bytes 4915208 | tf_op jit(solution)/shard_map/ppermute | solution.py:1117
  382.9 36.0 %collective-permute-start.52 = (bf16[1,4,40,2560]{3,2,1,0:T(8,128)(2,1)}, bf16[1,4,40,2560]{3,2,1,0:T(8,128)(2,1)S(1)}, u32[]{:S(2)}, u32[]{:S(2)}) collective-permute-start(bf16[1,4,40,2560]{3,2,1,0:T(8,128)(2,1)} %get-tuple-element.325.refs_9_), channel_id=1, source_target_pairs={{0,4},{2,6},{4,0},{6,2},{8,12},{10,14},{12,8},{14,10},{16,20},{18,... | collective-permute-start | bytes 2457608 | tf_op jit(solution)/shard_map/ppermute | solution.py:1113
  383.8 34.9 %collective-permute-start.50 = (bf16[1,2,40,2560]{3,2,1,0:T(8,128)(2,1)}, bf16[1,2,40,2560]{3,2,1,0:T(8,128)(2,1)S(1)}, u32[]{:S(2)}, u32[]{:S(2)}) collective-permute-start(bf16[1,2,40,2560]{3,2,1,0:T(8,128)(2,1)} %get-tuple-element.324.refs_8_), channel_id=1, source_target_pairs={{0,8},{2,10},{4,12},{6,14},{8,0},{10,2},{12,4},{14,6},{16,24},{18,... | collective-permute-start | bytes 1228808 | tf_op jit(solution)/shard_map/ppermute | solution.py:1113
  418.8 57.8 %collective-permute-start.61 = (bf16[1,4,40,3200]{3,2,1,0:T(8,128)(2,1)}, bf16[1,4,40,3200]{3,2,1,0:T(8,128)(2,1)}, u32[]{:S(2)}, u32[]{:S(2)}) collective-permute-start(bf16[1,4,40,3200]{3,2,1,0:T(8,128)(2,1)} %get-tuple-element.358), channel_id=1, source_target_pairs={{0,2},{2,0},{4,6},{6,4},{8,10},{10,8},{12,14},{14,12},{16,18},{18,... | collective-permute-start | bytes 3072008 | tf_op jit(solution)/shard_map/ppermute | solution.py:1113
  476.6 36.9 %collective-permute-start.69 = (bf16[1,1,40,2560]{3,2,1,0:T(8,128)(2,1)S(1)}, bf16[1,1,40,2560]{3,2,1,0:T(8,128)(2,1)S(1)}, u32[]{:S(2)}, u32[]{:S(2)}) collective-permute-start(bf16[1,1,40,2560]{3,2,1,0:T(8,128)(2,1)S(1)} %copy-done.71), channel_id=1, source_target_pairs={{0,16},{2,18},{4,20},{6,22},{8,24},{10,26},{12,28},{14,30},{16,0},... | collective-permute-start | bytes 614408 | tf_op jit(solution)/shard_map/ppermute | solution.py:1113
  477.0 36.9 %collective-permute-start.68 = (bf16[1,1,160,1280]{3,2,1,0:T(8,128)(2,1)}, bf16[1,1,160,1280]{3,2,1,0:T(8,128)(2,1)S(1)}, u32[]{:S(2)}, u32[]{:S(2)}) collective-permute-start(bf16[1,1,160,1280]{3,2,1,0:T(8,128)(2,1)} %get-tuple-element.348.refs_2_), channel_id=1, source_target_pairs={{0,16},{2,18},{4,20},{6,22},{8,24},{10,26},{12,28},{14,30},{16,0},... | collective-permute-start | bytes 1228808 | tf_op jit(solution)/shard_map/ppermute | solution.py:1113
  532.9 41.7 %collective-permute-start.70 = (bf16[1,160,1280]{2,1,0:T(8,128)(2,1)}, bf16[1,160,1280]{2,1,0:T(8,128)(2,1)S(1)}, u32[]{:S(2)}, u32[]{:S(2)}) collective-permute-start(bf16[1,160,1280]{2,1,0:T(8,128)(2,1)} %bitcast.52), channel_id=1, source_target_pairs={{0,16},{2,18},{4,20},{6,22},{8,24},{10,26},{12,28},{14,30},{16,0},... | collective-permute-start | bytes 1228808 | tf_op jit(solution)/shard_map/ppermute | solution.py:1113
  550.0 38.5 %collective-permute-start.80 = (bf16[1,1,40,3200]{3,2,1,0:T(8,128)(2,1)}, bf16[1,1,40,3200]{3,2,1,0:T(8,128)(2,1)S(1)}, u32[]{:S(2)}, u32[]{:S(2)}) collective-permute-start(bf16[1,1,40,3200]{3,2,1,0:T(8,128)(2,1)} %get-tuple-element.397), channel_id=1, source_target_pairs={{0,16},{2,18},{4,20},{6,22},{8,24},{10,26},{12,28},{14,30},{16,0},... | collective-permute-start | bytes 768008 | tf_op jit(solution)/shard_map/ppermute | solution.py:1113
  574.8 42.7 %collective-permute-start.78 = (bf16[2,160,1280]{2,1,0:T(8,128)(2,1)S(1)}, bf16[2,160,1280]{2,1,0:T(8,128)(2,1)}, u32[]{:S(2)}, u32[]{:S(2)}) collective-permute-start(bf16[2,160,1280]{2,1,0:T(8,128)(2,1)S(1)} %pad_maximum_fusion.5.refs_2_), channel_id=1, source_target_pairs={{0,4},{2,6},{4,0},{6,2},{8,12},{10,14},{12,8},{14,10},{16,20},{18,... | collective-permute-start | bytes 2457608 | tf_op jit(solution)/shard_map/ppermute | solution.py:1113
  577.0 39.2 %collective-permute-start.86 = (bf16[2,40,2560]{2,1,0:T(8,128)(2,1)S(1)}, bf16[2,40,2560]{2,1,0:T(8,128)(2,1)}, u32[]{:S(2)}, u32[]{:S(2)}) collective-permute-start(bf16[2,40,2560]{2,1,0:T(8,128)(2,1)S(1)} %pad_maximum_fusion.12.refs_3_), channel_id=1, source_target_pairs={{0,8},{2,10},{4,12},{6,14},{8,0},{10,2},{12,4},{14,6},{16,24},{18,... | collective-permute-start | bytes 1228808 | tf_op jit(solution)/shard_map/ppermute | solution.py:1113
  600.8 43.9 %collective-permute-start.77 = (bf16[512,1280]{1,0:T(8,128)(2,1)}, bf16[512,1280]{1,0:T(8,128)(2,1)}, u32[]{:S(2)}, u32[]{:S(2)}) collective-permute-start(bf16[512,1280]{1,0:T(8,128)(2,1)} %get-tuple-element.396), channel_id=1, source_target_pairs={{0,1},{1,0},{2,3},{3,2},{4,5},{5,4},{6,7},{7,6},{8,9},{9,8},{10,11... | collective-permute-start | bytes 3932168 | tf_op jit(solution)/shard_map/ppermute | solution.py:1117
  656.7 36.8 %collective-permute-start.106 = (bf16[4,40,3200]{2,1,0:T(8,128)(2,1)}, bf16[4,40,3200]{2,1,0:T(8,128)(2,1)S(1)}, u32[]{:S(2)}, u32[]{:S(2)}) collective-permute-start(bf16[4,40,3200]{2,1,0:T(8,128)(2,1)} %pad_maximum_fusion.2.refs_0_), channel_id=1, source_target_pairs={{0,4},{2,6},{4,0},{6,2},{8,12},{10,14},{12,8},{14,10},{16,20},{18,... | collective-permute-start | bytes 3072008 | tf_op jit(solution)/shard_map/ppermute | solution.py:1113
  659.0 49.1 %collective-permute-start.104 = (bf16[4,160,1280]{2,1,0:T(8,128)(2,1)}, bf16[4,160,1280]{2,1,0:T(8,128)(2,1)}, u32[]{:S(2)}, u32[]{:S(2)}) collective-permute-start(bf16[4,160,1280]{2,1,0:T(8,128)(2,1)} %copy-done.4), channel_id=1, source_target_pairs={{0,2},{2,0},{4,6},{6,4},{8,10},{10,8},{12,14},{14,12},{16,18},{18,... | collective-permute-start | bytes 4915208 | tf_op jit(solution)/shard_map/ppermute | solution.py:1113
  (155 other events, 2306.7 us)
